TPU v7x, 32 devices: a whole 2x2x4 slice. The times are simulated.
32 devices in a mesh: section: 2 (over core), fsdp: 4 (over z), rep: 4 (over y, x).
Axes of the slice: x: 2, y: 2, z: 4, core: 2. Of those that a mesh axis runs over, the one named last changes fastest.
Arguments:
- tokens: bfloat16 [4, 2, 1024, 2048], P('rep', None, 'fsdp'), may hold values from -6 to 6
- segment_ids: int32 [4, 2, 1024], P('rep', None, 'fsdp'), may hold values from 0 to 1, as said below
- cotangent: bfloat16 [4, 2, 1024, 2048], P('rep', None, 'fsdp'), may hold values from -6 to 6
- norm_attn: bfloat16 [2, 2048], P('section', 'fsdp'), may hold values from 0.099609375 to 1.8984375
- w_query: bfloat16 [2, 2048, 2048], P('section', 'fsdp'), may hold values from -0.125 to 0.125
- w_key: bfloat16 [2, 2048, 512], P('section', 'fsdp'), may hold values from -0.125 to 0.125
- w_value: bfloat16 [2, 2048, 512], P('section', 'fsdp'), may hold values from -0.125 to 0.125
- w_output: bfloat16 [2, 2048, 2048], P('section', 'fsdp'), may hold values from -1 to 1
- norm_ffn: bfloat16 [2, 2048], P('section', 'fsdp'), may hold values from 0.099609375 to 1.8984375
- w_gate: bfloat16 [2, 2048, 8192], P('section', 'fsdp'), may hold values from -0.125 to 0.125
- w_up: bfloat16 [2, 2048, 8192], P('section', 'fsdp'), may hold values from -0.125 to 0.125
- w_down: bfloat16 [2, 8192, 2048], P('section', 'fsdp'), may hold values from -0.0625 to 0.0625
Outputs:
- section_outputs: bfloat16 [2, 4, 2, 1024, 2048], P('section', 'rep', None, 'fsdp')
- input_grads: bfloat16 [2, 4, 2, 1024, 2048], P('section', 'rep', None, 'fsdp')
- grad_norm_attn: float32 [2, 2048], P('section', 'fsdp')
- grad_w_query: float32 [2, 2048, 2048], P('section', 'fsdp')
- grad_w_key: float32 [2, 2048, 512], P('section', 'fsdp')
- grad_w_value: float32 [2, 2048, 512], P('section', 'fsdp')
- grad_w_output: float32 [2, 2048, 2048], P('section', 'fsdp')
- grad_norm_ffn: float32 [2, 2048], P('section', 'fsdp')
- grad_w_gate: float32 [2, 2048, 8192], P('section', 'fsdp')
- grad_w_up: float32 [2, 2048, 8192], P('section', 'fsdp')
- grad_w_down: float32 [2, 8192, 2048], P('section', 'fsdp')
Inputs may be any that keep to these rules, and one draw needn't show every extreme that they name: `segment_ids`: along the 1024 positions of each micro-batch the ids never fall; positions with equal ids form one sequence; in some micro-batch one sequence fills all 1024 positions.
All inputs are finite; a program needn't handle non-finite values.
Results may differ from a plain program's by a relative error of at most 0.025.
Values may be sent and summed in bfloat16 or wider, within the bound.
A program may use at most 832 MiB of HBM per device.

v0:
```python
import jax
import jax.numpy as jnp
from jax import lax
from jax.sharding import PartitionSpec as P

HQ = 32
KVH = 8
HD = 64
FF = 8192


epsilon = 1e-05
rope_base = 500000.0
masked_score = -1e30


def passed_along(value, axis, steps):
    count = lax.axis_size(axis)
    initial, last = (max(0, -steps), min(count, count - steps))
    return lax.ppermute(value, axis, [(source, source + steps) for source in range(initial, last)])


def rms_scale(values, gain_vec):
    return (
        values * lax.rsqrt(jnp.mean(values * values, axis=-1, keepdims=True) + epsilon) * gain_vec
    )


def rope_tables(positions):
    half_size = HD // 2
    frequency = rope_base ** (-(jnp.arange(half_size).astype(jnp.float32) * 2.0) / HD)
    angles = positions[:, None] * frequency[None, :]
    angles = jnp.concatenate([angles, angles], axis=-1)
    return (jnp.cos(angles)[:, None, :], jnp.sin(angles)[:, None, :])


def rotary(values, cosine_table, sine_table):
    half_size = values.shape[-1] // 2
    turned = jnp.concatenate([-values[..., half_size:], values[..., :half_size]], axis=-1)
    return values * cosine_table + turned * sine_table


def rotary_back(grad_rot, cosine_table, sine_table):
    half_size = grad_rot.shape[-1] // 2
    scaled = grad_rot * sine_table
    return grad_rot * cosine_table + jnp.concatenate(
        [scaled[..., half_size:], -scaled[..., :half_size]], axis=-1
    )


def times_back(left, weight):
    return lax.dot_general(
        left, weight, (((1,), (1,)), ((), ())), preferred_element_type=jnp.float32
    )


def swiglu(gate_in, up_in):
    return jax.nn.silu(gate_in) * up_in


def when_valid(flag, step_fn, *operands):
    return lax.cond(
        flag, step_fn, lambda *inner: jax.tree.map(jnp.zeros_like, step_fn(*inner)), *operands
    )


def store_at(buffer, value, index, flag):
    previous = lax.dynamic_index_in_dim(buffer, index, 0, keepdims=False)
    return lax.dynamic_update_index_in_dim(buffer, jnp.where(flag, value, previous), index, 0)


def layer_tables(seg_row, row_start, rows_here):
    glob_rows = row_start + jnp.arange(rows_here)
    seg_query = lax.dynamic_slice_in_dim(seg_row, row_start, rows_here)
    seg_start = jnp.sum((seg_row[None, :] < seg_query[:, None]).astype(jnp.int32), axis=-1)
    cosine_table, sine_table = rope_tables((glob_rows - seg_start).astype(jnp.float32))
    key_rows = jnp.arange(seg_row.shape[0])
    allowed = (seg_row[None, :] == seg_query[:, None]) & (key_rows[None, :] <= glob_rows[:, None])
    return (cosine_table, sine_table, allowed)


def project_inputs(layer_in, weights, cosine_table, sine_table):
    norm_attn, w_query, w_key, w_value = weights[:4]
    rows_here = layer_in.shape[0]
    f32 = jnp.float32
    normed = rms_scale(layer_in, norm_attn.astype(f32)).astype(jnp.bfloat16)
    query = jnp.dot(normed, w_query, preferred_element_type=f32).reshape(rows_here, HQ, HD)
    key_pre = jnp.dot(normed, w_key, preferred_element_type=f32).reshape(rows_here, KVH, HD)
    value_rows = jnp.dot(normed, w_value, preferred_element_type=f32).astype(jnp.bfloat16)
    query_rot = (
        rotary(query, cosine_table, sine_table)
        .astype(jnp.bfloat16)
        .reshape(rows_here, KVH, HQ // KVH, HD)
    )
    key_rot = (
        rotary(key_pre, cosine_table, sine_table).astype(jnp.bfloat16).reshape(rows_here, KVH * HD)
    )
    return (normed, query_rot, key_rot, value_rows)


def attend_rest(layer_in, query_rot, keys_all, values_all, weights, allowed):
    w_output, norm_ffn, w_gate, w_up, w_down = weights[4:]
    rows_here = layer_in.shape[0]
    scale = HD ** (-0.5)
    f32 = jnp.float32
    key_heads = keys_all.reshape(-1, KVH, HD)
    value_heads = values_all.reshape(-1, KVH, HD)
    scores = jnp.einsum("tkgd,skd->kgts", query_rot, key_heads, preferred_element_type=f32) * scale
    scores = jnp.where(allowed[None, None], scores, masked_score)
    row_max = jnp.max(scores, axis=-1)
    exp_scores = jnp.exp(scores - row_max[..., None])
    row_total = jnp.sum(exp_scores, axis=-1)
    attn_probs = (exp_scores / row_total[..., None]).astype(jnp.bfloat16)
    log_total = row_max + jnp.log(row_total)
    mixed_heads = jnp.einsum("kgts,skd->tkgd", attn_probs, value_heads, preferred_element_type=f32)
    mixed_low = mixed_heads.reshape(rows_here, HQ * HD).astype(jnp.bfloat16)
    residual = layer_in + jnp.dot(mixed_low, w_output, preferred_element_type=f32)
    normed_ffn = rms_scale(residual, norm_ffn.astype(f32)).astype(jnp.bfloat16)
    gate_pre = jnp.dot(normed_ffn, w_gate, preferred_element_type=f32)
    up_pre = jnp.dot(normed_ffn, w_up, preferred_element_type=f32)
    hidden = swiglu(gate_pre, up_pre).astype(jnp.bfloat16)
    layer_out = residual + jnp.dot(hidden, w_down, preferred_element_type=f32)
    return (layer_out, (log_total, mixed_low, residual, normed_ffn, gate_pre, up_pre, hidden))


def attend_back(grad_out, pieces, weights, allowed):
    w_output, norm_ffn, w_gate, w_up, w_down = weights[4:]
    (
        query_rot,
        keys_all,
        values_all,
        log_total,
        mixed_low,
        residual,
        normed_ffn,
        gate_pre,
        up_pre,
        hidden,
    ) = pieces
    f32 = jnp.float32
    bf16 = jnp.bfloat16
    rows_here = residual.shape[0]
    scale = HD ** (-0.5)
    key_heads = keys_all.reshape(-1, KVH, HD)
    value_heads = values_all.reshape(-1, KVH, HD)
    branch = grad_out.astype(bf16)
    grad_hidden = times_back(branch, w_down)
    _, swiglu_back = jax.vjp(swiglu, gate_pre, up_pre)
    grad_gate_pre, grad_up_pre = swiglu_back(grad_hidden)
    grad_gate_pre = grad_gate_pre.astype(bf16)
    grad_up_pre = grad_up_pre.astype(bf16)
    grad_normed_ffn = times_back(grad_gate_pre, w_gate) + times_back(grad_up_pre, w_up)
    _, norm_ffn_back = jax.vjp(rms_scale, residual, norm_ffn.astype(f32))
    grad_residual, grad_gain_ffn = norm_ffn_back(grad_normed_ffn)
    grad_residual = grad_residual + grad_out
    branch_attn = grad_residual.astype(bf16)
    grad_mixed = times_back(branch_attn, w_output).astype(bf16)
    grad_mixed = grad_mixed.reshape(rows_here, KVH, HQ // KVH, HD)
    scores = jnp.einsum("tkgd,skd->kgts", query_rot, key_heads, preferred_element_type=f32) * scale
    scores = jnp.where(allowed[None, None], scores, masked_score)
    attn_probs = jnp.exp(scores - log_total[..., None])
    grad_probs = jnp.einsum("tkgd,skd->kgts", grad_mixed, value_heads, preferred_element_type=f32)
    grad_scores = (
        attn_probs * (grad_probs - jnp.sum(attn_probs * grad_probs, axis=-1, keepdims=True))
    ).astype(bf16)
    grad_query_rot = (
        jnp.einsum("kgts,skd->tkgd", grad_scores, key_heads, preferred_element_type=f32) * scale
    )
    grad_key_part = (
        jnp.einsum("kgts,tkgd->skd", grad_scores, query_rot, preferred_element_type=f32) * scale
    )
    grad_value_part = jnp.einsum(
        "kgts,tkgd->skd", attn_probs.astype(bf16), grad_mixed, preferred_element_type=f32
    )
    key_width = KVH * HD
    return (
        grad_key_part.reshape(-1, key_width),
        grad_value_part.reshape(-1, key_width),
        grad_query_rot,
        grad_residual,
        branch,
        grad_gate_pre,
        grad_up_pre,
        branch_attn,
        grad_gain_ffn,
    )


def inputs_back(
    grad_query_rot,
    grad_key_rot,
    grad_value_rows,
    grad_residual,
    layer_in,
    weights,
    cosine_table,
    sine_table,
):
    norm_attn, w_query, w_key, w_value = weights[:4]
    f32 = jnp.float32
    bf16 = jnp.bfloat16
    rows_here = layer_in.shape[0]
    key_width = KVH * HD
    grad_query = rotary_back(grad_query_rot.reshape(rows_here, HQ, HD), cosine_table, sine_table)
    grad_query = grad_query.reshape(rows_here, HQ * HD).astype(bf16)
    grad_key_rows = rotary_back(grad_key_rot.reshape(rows_here, KVH, HD), cosine_table, sine_table)
    grad_key_rows = grad_key_rows.reshape(rows_here, key_width).astype(bf16)
    grad_value_low = grad_value_rows.astype(bf16)
    grad_normed = (
        times_back(grad_query, w_query)
        + times_back(grad_key_rows, w_key)
        + times_back(grad_value_low, w_value)
    )
    _, norm_attn_back = jax.vjp(rms_scale, layer_in, norm_attn.astype(f32))
    grad_in, grad_gain_attn = norm_attn_back(grad_normed)
    return (grad_in + grad_residual, grad_query, grad_key_rows, grad_value_low, grad_gain_attn)


def merge_micro(buffer):
    return buffer.reshape((-1,) + buffer.shape[2:])


def shards(
    tokens,
    segment_ids,
    cotangent,
    norm_attn,
    w_query,
    w_key,
    w_value,
    w_output,
    norm_ffn,
    w_gate,
    w_up,
    w_down,
):
    bf16 = jnp.bfloat16
    f32 = jnp.float32
    section_idx = lax.axis_index("section")
    shard_idx = lax.axis_index("fsdp")
    seg_all = lax.all_gather(segment_ids, "fsdp", axis=2, tiled=True)[0]
    local_weights = (norm_attn, w_query, w_key, w_value, w_output, norm_ffn, w_gate, w_up, w_down)
    gathered = (
        lax.all_gather(local_weights[0], "fsdp", axis=1, tiled=True),
        lax.all_gather(local_weights[1], "fsdp", axis=1, tiled=True),
        lax.all_gather(local_weights[2], "fsdp", axis=1, tiled=True),
        lax.all_gather(local_weights[3], "fsdp", axis=1, tiled=True),
        lax.all_gather(local_weights[4], "fsdp", axis=1, tiled=True),
        lax.all_gather(local_weights[5], "fsdp", axis=1, tiled=True),
        lax.all_gather(local_weights[6], "fsdp", axis=1, tiled=True),
        lax.all_gather(local_weights[7], "fsdp", axis=1, tiled=True),
        lax.all_gather(local_weights[8], "fsdp", axis=1, tiled=True),
    )
    weights = tuple((piece[0] for piece in gathered))
    micro_count = tokens.shape[1]
    rows_here = tokens.shape[2]
    width = tokens.shape[3]
    row_start = shard_idx * rows_here
    received = jnp.zeros((rows_here, width), bf16)
    outputs = jnp.zeros(tokens.shape[1:], bf16)
    forward_buffers = None
    for turn_at in range(micro_count + 1):
        offset = turn_at - section_idx
        micro_index = jnp.clip(offset, 0, micro_count - 1)
        is_valid = (offset >= 0) & (offset < micro_count)
        own_rows = lax.dynamic_index_in_dim(tokens[0], micro_index, 0, keepdims=False)
        input_low = jnp.where(section_idx == 0, own_rows, received)
        layer_in = input_low.astype(f32)
        seg_row = lax.dynamic_index_in_dim(seg_all, micro_index, 0, keepdims=False)
        cosine_table, sine_table, allowed = layer_tables(seg_row, row_start, rows_here)
        normed, query_rot, key_rot, value_rows = when_valid(
            is_valid,
            lambda values, cosines, sines: project_inputs(values, weights, cosines, sines),
            layer_in,
            cosine_table,
            sine_table,
        )
        keys_all, values_all = (
            lax.all_gather(key_rot, "fsdp", axis=0, tiled=True),
            lax.all_gather(value_rows, "fsdp", axis=0, tiled=True),
        )
        layer_out, rest = when_valid(
            is_valid,
            lambda values, queries, keys, vals, masks: attend_rest(
                values, queries, keys, vals, weights, masks
            ),
            layer_in,
            query_rot,
            keys_all,
            values_all,
            allowed,
        )
        to_send = layer_out.astype(bf16)
        outputs = store_at(outputs, to_send, micro_index, is_valid)
        kept = (input_low, normed, query_rot, keys_all, values_all) + tuple(rest)
        if forward_buffers is None:
            forward_buffers = tuple(
                (jnp.zeros((micro_count,) + value.shape, value.dtype) for value in kept)
            )
        forward_buffers = tuple(
            (
                store_at(buffer, value, micro_index, is_valid)
                for buffer, value in zip(forward_buffers, kept)
            )
        )
        if turn_at < micro_count:
            received = passed_along(to_send, "section", 1)
    input_grads = jnp.zeros(tokens.shape[1:], bf16)
    passed = jnp.zeros((rows_here, width), bf16)
    gain_attn_sum = jnp.zeros((width,), f32)
    gain_ffn_sum = jnp.zeros((width,), f32)
    back_buffers = None
    for turn_at in range(micro_count + 1):
        offset = micro_count - turn_at - section_idx
        micro_index = jnp.clip(offset, 0, micro_count - 1)
        is_valid = (offset >= 0) & (offset < micro_count)
        state = tuple(
            (
                lax.dynamic_index_in_dim(buffer, micro_index, 0, keepdims=False)
                for buffer in forward_buffers
            )
        )
        layer_in = state[0].astype(f32)
        seg_row = lax.dynamic_index_in_dim(seg_all, micro_index, 0, keepdims=False)
        cosine_table, sine_table, allowed = layer_tables(seg_row, row_start, rows_here)
        own_rows = lax.dynamic_index_in_dim(cotangent[0], micro_index, 0, keepdims=False)
        grad_out = jnp.where(section_idx == 1, own_rows, passed).astype(f32)
        (
            grad_key_flat,
            grad_value_flat,
            grad_query_rot,
            grad_residual,
            branch,
            grad_gate_pre,
            grad_up_pre,
            branch_attn,
            grad_gain_ffn,
        ) = when_valid(
            is_valid,
            lambda grads, pieces, masks: attend_back(grads, pieces, weights, masks),
            grad_out,
            state[2:],
            allowed,
        )
        grad_key_rot, grad_value_rows = (
            lax.psum_scatter(
                grad_key_flat.astype(jnp.bfloat16), "fsdp", scatter_dimension=0, tiled=True
            ).astype(jnp.float32),
            lax.psum_scatter(
                grad_value_flat.astype(jnp.bfloat16), "fsdp", scatter_dimension=0, tiled=True
            ).astype(jnp.float32),
        )
        grad_in, grad_query, grad_key_rows, grad_value_low, grad_gain_attn = when_valid(
            is_valid,
            lambda gq, gk, gv, gres, values, cosines, sines: inputs_back(
                gq, gk, gv, gres, values, weights, cosines, sines
            ),
            grad_query_rot,
            grad_key_rot,
            grad_value_rows,
            grad_residual,
            layer_in,
            cosine_table,
            sine_table,
        )
        to_send = grad_in.astype(bf16)
        input_grads = store_at(input_grads, to_send, micro_index, is_valid)
        gain_attn_sum = gain_attn_sum + grad_gain_attn
        gain_ffn_sum = gain_ffn_sum + grad_gain_ffn
        kept_grads = (
            branch,
            grad_gate_pre,
            grad_up_pre,
            branch_attn,
            grad_query,
            grad_key_rows,
            grad_value_low,
        )
        if back_buffers is None:
            back_buffers = tuple(
                (jnp.zeros((micro_count,) + value.shape, value.dtype) for value in kept_grads)
            )
        back_buffers = tuple(
            (
                store_at(buffer, value, micro_index, is_valid)
                for buffer, value in zip(back_buffers, kept_grads)
            )
        )
        if turn_at < micro_count:
            passed = passed_along(to_send, "section", -1)
    normed_all = merge_micro(forward_buffers[1])
    mixed_all = merge_micro(forward_buffers[6])
    ffn_in_all = merge_micro(forward_buffers[8])
    hidden_all = merge_micro(forward_buffers[11])
    down_grads_all = merge_micro(back_buffers[0])
    ffn_grads_all = jnp.concatenate(
        [merge_micro(back_buffers[1]), merge_micro(back_buffers[2])], axis=1
    )
    output_grads_all = merge_micro(back_buffers[3])
    attn_grads_all = jnp.concatenate(
        [merge_micro(back_buffers[4]), merge_micro(back_buffers[5]), merge_micro(back_buffers[6])],
        axis=1,
    )
    ratio = FF // (HQ * HD)
    groups = lax.axis_size("fsdp") * lax.axis_size("rep")
    attn_part = jnp.einsum("rc,rk->ck", normed_all, attn_grads_all, preferred_element_type=f32)
    ffn_part = jnp.einsum("rc,rk->ck", ffn_in_all, ffn_grads_all, preferred_element_type=f32)
    gains = jnp.stack([gain_attn_sum, gain_ffn_sum], axis=1)
    rows_part = lax.psum_scatter(
        jnp.concatenate([attn_part, ffn_part, gains], axis=1),
        ("fsdp", "rep"),
        scatter_dimension=0,
        tiled=True,
    )
    out_part = jnp.einsum("rc,rk->ck", mixed_all, output_grads_all, preferred_element_type=f32)
    down_part = jnp.einsum("rc,rk->ck", hidden_all, down_grads_all, preferred_element_type=f32)
    proj_part = lax.psum_scatter(
        jnp.concatenate(
            [
                out_part,
                down_part.reshape(
                    lax.axis_size(("fsdp", "rep")) * (HQ * HD // groups), ratio * width
                ),
            ],
            axis=1,
        ),
        ("fsdp", "rep"),
        scatter_dimension=0,
        tiled=True,
    )
    rows_part, proj_part = (
        lax.all_gather(rows_part.astype(jnp.bfloat16), "rep", axis=0, tiled=True).astype(
            rows_part.dtype
        ),
        lax.all_gather(proj_part.astype(jnp.bfloat16), "rep", axis=0, tiled=True).astype(
            proj_part.dtype
        ),
    )
    query_width = HQ * HD
    key_width = KVH * HD
    edge_key = query_width + key_width
    edge_value = edge_key + key_width
    edge_gate = edge_value + FF
    edge_up = edge_gate + FF
    grad_wquery = rows_part[:, :query_width]
    grad_wkey = rows_part[:, query_width:edge_key]
    grad_wvalue = rows_part[:, edge_key:edge_value]
    grad_gate = rows_part[:, edge_value:edge_gate]
    grad_up = rows_part[:, edge_gate:edge_up]
    grad_gain_attn = rows_part[:, edge_up]
    grad_gain_ffn = rows_part[:, edge_up + 1]
    grad_output = proj_part[:, :width]
    grad_down = proj_part[:, width:].reshape(-1, width)
    return (
        outputs[None, None],
        input_grads[None, None],
        grad_gain_attn[None],
        grad_wquery[None],
        grad_wkey[None],
        grad_wvalue[None],
        grad_output[None],
        grad_gain_ffn[None],
        grad_gate[None],
        grad_up[None],
        grad_down[None],
    )


def solution(mesh):
    in_specs = (
        P("rep", None, "fsdp", None),
        P("rep", None, "fsdp"),
        P("rep", None, "fsdp", None),
        P("section", "fsdp"),
        P("section", "fsdp", None),
        P("section", "fsdp", None),
        P("section", "fsdp", None),
        P("section", "fsdp", None),
        P("section", "fsdp"),
        P("section", "fsdp", None),
        P("section", "fsdp", None),
        P("section", "fsdp", None),
    )
    out_specs = (
        P("section", "rep", None, "fsdp", None),
        P("section", "rep", None, "fsdp", None),
        P("section", "fsdp"),
        P("section", "fsdp", None),
        P("section", "fsdp", None),
        P("section", "fsdp", None),
        P("section", "fsdp", None),
        P("section", "fsdp"),
        P("section", "fsdp", None),
        P("section", "fsdp", None),
        P("section", "fsdp", None),
    )
    return jax.shard_map(shards, mesh=mesh, in_specs=in_specs, out_specs=out_specs, check_vma=False)
```

profile of v0, /device:TPU:1, one launch (start us, length us, event | category | flops | bytes accessed | tf_op | source)
XLA Modules:
  0.0 7938.4 jit_solution(11929378696490156065)
XLA Ops:
  33.7 24.1 all-gather.18.cloned.1.call-done
  57.8 46.2 all-gather.20.cloned.1.call-done
  104.0 150.2 %all-gather.16.cloned.1.call-done = bf16[1,2048,2048]{2,1,0:T(8,128)(2,1)} async-done(((bf16[1,512,2048]{2,1,0:T(8,128)(2,1)}), bf16[1,2048,2048]{2,1,0:T(8,128)(2,1)}) %all-gather.16.cloned.1.call-update) | async-done | bytes 8388624 | tf_op jit(solution)/shard_map/all_gather | solution.py:245
  285.7 25.5 all-gather.24.cloned.1.call-done
  344.6 145.9 %all-gather.26.cloned.1.call-done = bf16[1,2048,2048]{2,1,0:T(8,128)(2,1)} async-done(((bf16[1,512,2048]{2,1,0:T(8,128)(2,1)}), bf16[1,2048,2048]{2,1,0:T(8,128)(2,1)}) %all-gather.26.cloned.1.call-update) | async-done | bytes 8388624 | tf_op jit(solution)/shard_map/all_gather | solution.py:248
  490.5 561.2 %all-gather.28.cloned.1.call-done = bf16[1,2048,8192]{2,1,0:T(8,128)(2,1)} async-done(((bf16[1,512,8192]{2,1,0:T(8,128)(2,1)}), bf16[1,2048,8192]{2,1,0:T(8,128)(2,1)}) %all-gather.28.cloned.1.call-update) | async-done | bytes 33554448 | tf_op jit(solution)/shard_map/all_gather | solution.py:250
  1051.7 561.2 %all-gather.30.cloned.1.call-done = bf16[1,2048,8192]{2,1,0:T(8,128)(2,1)} async-done(((bf16[1,512,8192]{2,1,0:T(8,128)(2,1)}), bf16[1,2048,8192]{2,1,0:T(8,128)(2,1)}) %all-gather.30.cloned.1.call-update) | async-done | bytes 33554448 | tf_op jit(solution)/shard_map/all_gather | solution.py:251
  1612.9 561.2 %all-gather.32.cloned.1.call-done = bf16[1,8192,2048]{2,1,0:T(8,128)(2,1)} async-done(((bf16[1,2048,2048]{2,1,0:T(8,128)(2,1)}), bf16[1,8192,2048]{2,1,0:T(8,128)(2,1)}) %all-gather.32.cloned.1.call-update) | async-done | bytes 33554448 | tf_op jit(solution)/shard_map/all_gather | solution.py:252
  2174.1 25.2 conditional.13
  2240.2 64.2 collective-permute-done
  2305.4 25.0 conditional.14
  2356.5 46.6 all-gather.34.cloned.1.call-done
  2403.0 30.7 all-gather.36.cloned.1.call-done
  2433.7 111.0 %conditional.15 = (f32[8,4,256]{2,1,0:T(4,128)S(1)}, f32[256,2048]{1,0:T(8,128)}, bf16[256,2048]{1,0:T(8,128)(2,1)}, f32[256,8192]{1,0:T(8,128)}, f32[256,8192]{...) conditional(s32[]{:T(128)} %convert_element_type.493, ...), branch_computations={%region_13.14_spmd, %region_14.18_spmd} | conditional | flops 30182729728 | bytes 297820288 | solution.py:62
  2577.1 25.1 conditional.16
  2633.6 29.1 all-gather.40.cloned.1.call-done
  2662.6 112.0 %conditional.17 = (f32[8,4,256]{2,1,0:T(4,128)S(1)}, f32[256,2048]{1,0:T(8,128)}, bf16[256,2048]{1,0:T(8,128)(2,1)}, f32[256,8192]{1,0:T(8,128)}, f32[256,8192]{...) conditional(s32[]{:T(128)} %convert_element_type.497, ...), branch_computations={%region_22.23_spmd, %region_23.27_spmd} | conditional | flops 30182729728 | bytes 297820288 | solution.py:62
  2803.6 176.7 %conditional.18 = (bf16[1024,512]{0,1:T(8,128)(2,1)}, bf16[1024,512]{0,1:T(8,128)(2,1)}, f32[256,8,4,64]{0,3,2,1:T(8,128)}, f32[256,2048]{1,0:T(8,128)}, bf16[25...) conditional(s32[]{:T(128)} %convert_element_type.497, ...), branch_computations={%region_27.28_spmd, %region_28.33_spmd.clone.clone} | conditional | flops 33452713984 | bytes 518012096 | solution.py:62
  2936.5 27.9 fusion.120
  3007.9 27.2 reduce-scatter.11.cloned.1.call-done
  3067.0 175.9 %conditional.20 = (bf16[1024,512]{0,1:T(8,128)(2,1)}, bf16[1024,512]{0,1:T(8,128)(2,1)}, f32[256,8,4,64]{0,3,2,1:T(8,128)}, f32[256,2048]{1,0:T(8,128)}, bf16[25...) conditional(s32[]{:T(128)} %convert_element_type.493, ...), branch_computations={%region_40.41_spmd, %region_41.46_spmd} | conditional | flops 33452189696 | bytes 519060672 | solution.py:62
  3199.2 27.9 fusion.38
  3269.3 27.1 reduce-scatter.15.cloned.1.call-done
  3356.8 31.1 convolution_bitcast_fusion
  3387.8 79.5 %reshape.935 = f32[2048,8192]{1,0:T(8,128)} reshape(f32[8192,2048]{1,0:T(8,128)} %convolution_bitcast_fusion) | data formatting | bytes 134217728 | tf_op jit(solution)/shard_map/reshape | solution.py:421
  3477.6 54.2 pad_maximum_fusion.6
  3594.2 55.7 fusion.151
  3674.3 185.6 %concatenate.149 = f32[2048,19458]{1,0:T(8,128)} concatenate(f32[2048,3072]{1,0:T(8,128)} %fusion.155, f32[2048,16384]{1,0:T(8,128)} %fusion.151, f32[2048,1]{1,0:T(8,128)} %copy.151, f32[2048,1]{1,0:T(8,128)S(1)} %copy-done.63), dimensions={1} | concatenate | bytes 318799872 | tf_op jit(solution)/shard_map/concatenate | solution.py:410
  3860.0 1520.3 %reduce-scatter.23.cloned.1.call-done = f32[128,10240]{1,0:T(8,128)} async-done(((f32[2048,10240]{1,0:T(8,128)}), f32[128,10240]{1,0:T(8,128)}) %reduce-scatter.23.cloned.1.call-update) | async-done | bytes 5242896 | tf_op jit(solution)/shard_map/reduce_scatter | solution.py:417
  5384.8 2198.8 %reduce-scatter.21.cloned.1.call-done = f32[128,19458]{1,0:T(8,128)} async-done(((f32[2048,19458]{1,0:T(8,128)}), f32[128,19458]{1,0:T(8,128)}) %reduce-scatter.21.cloned.1.call-update) | async-done | bytes 9962512 | tf_op jit(solution)/shard_map/reduce_scatter | solution.py:409
  7600.0 92.1 %all-gather.44.cloned.1.call-done = bf16[512,10240]{1,0:T(8,128)(2,1)} async-done(((bf16[128,10240]{1,0:T(8,128)(2,1)}), bf16[512,10240]{1,0:T(8,128)(2,1)}) %all-gather.44.cloned.1.call-update) | async-done | bytes 10485776 | tf_op jit(solution)/shard_map/all_gather | solution.py:435
  7743.3 136.9 %all-gather.42.cloned.1.call-done = bf16[512,19458]{1,0:T(8,128)(2,1)} async-done(((bf16[128,19458]{1,0:T(8,128)(2,1)}), bf16[512,19458]{1,0:T(8,128)(2,1)}) %all-gather.42.cloned.1.call-update) | async-done | bytes 19925008 | tf_op jit(solution)/shard_map/all_gather | solution.py:432
  (632 shorter events, 1264.2 us)
Async XLA Ops:
  7.2 50.6 all-gather.18.cloned.1.call-start
  7.9 96.1 %all-gather.20.cloned.1.call-start = ((), (), s32[]{:S(2)}) async-start(), calls=%async_computation.10 | async-start | bytes 2621440 | tf_op jit(solution)/shard_map/all_gather | solution.py:247
  8.7 245.5 %all-gather.16.cloned.1.call-start = ((), (), s32[]{:S(2)}) async-start(), calls=%async_computation.8 | async-start | bytes 10485760 | tf_op jit(solution)/shard_map/all_gather | solution.py:245
  9.4 301.8 %all-gather.24.cloned.1.call-start = ((), (), s32[]{:S(2)}) async-start(), calls=%async_computation.12 | async-start | bytes 1310720 | tf_op jit(solution)/shard_map/all_gather | solution.py:280
  257.0 82.5 %all-gather.22.cloned.1.call-start = ((), (), s32[]{:S(2)}) async-start(), calls=%async_computation.11 | async-start | bytes 1310720 | tf_op jit(solution)/shard_map/all_gather | solution.py:279
  258.9 231.6 %all-gather.26.cloned.1.call-start = ((), (), s32[]{:S(2)}) async-start(), calls=%async_computation.13 | async-start | bytes 10485760 | tf_op jit(solution)/shard_map/all_gather | solution.py:248
  259.4 792.3 %all-gather.28.cloned.1.call-start = ((), (), s32[]{:S(2)}) async-start(), calls=%async_computation.14 | async-start | bytes 41943040 | tf_op jit(solution)/shard_map/all_gather | solution.py:250
  260.2 1352.7 %all-gather.30.cloned.1.call-start = ((), (), s32[]{:S(2)}) async-start(), calls=%async_computation.15 | async-start | bytes 41943040 | tf_op jit(solution)/shard_map/all_gather | solution.py:251
  260.9 1913.1 %all-gather.32.cloned.1.call-start = ((), (), s32[]{:S(2)}) async-start(), calls=%async_computation.16 | async-start | bytes 41943040 | tf_op jit(solution)/shard_map/all_gather | solution.py:252
  261.7 2141.4 %all-gather.34.cloned.1.call-start = ((), (), s32[]{:S(2)}) async-start(), calls=%async_computation.17 | async-start | bytes 1310720 | tf_op jit(solution)/shard_map/all_gather | solution.py:279
  271.1 1903.0 %copy-start.98 = (bf16[2048]{0:T(1024)(128)(2,1)}, bf16[2048]{0:T(1024)(128)(2,1)S(1)}, u32[]{:S(2)}) copy-start(bf16[2048]{0:T(1024)(128)(2,1)S(1)} %reduce.1) | copy-start | bytes 12292
  280.5 1893.6 %copy-start.14 = (pred[256,1024]{0,1:T(8,128)(4,1)}, pred[256,1024]{0,1:T(8,128)(4,1)S(1)}, u32[]{:S(2)}) copy-start(pred[256,1024]{0,1:T(8,128)(4,1)S(1)} %get-tuple-element.1278) | copy-start | bytes 786436
  2204.4 99.9 %collective-permute-start = (bf16[256,2048]{1,0:T(8,128)(2,1)}, bf16[256,2048]{1,0:T(8,128)(2,1)S(1)}, u32[]{:S(2)}, u32[]{:S(2)}) collective-permute-start(bf16[256,2048]{1,0:T(8,128)(2,1)} %get-tuple-element.881), channel_id=1, source_target_pairs={{0,16},{1,17},{2,18},{3,19},{4,20},{5,21},{6,22},{7,23},{8,24},{9,... | collective-permute-start | bytes 3145736 | tf_op jit(solution)/shard_map/ppermute | solution.py:20
  2332.2 101.5 %all-gather.36.cloned.1.call-start = ((), (), s32[]{:S(2)}) async-start(), calls=%async_computation.18 | async-start | bytes 1310720 | tf_op jit(solution)/shard_map/all_gather | solution.py:280
  2343.6 290.0 %all-gather.38.cloned.1.call-start = ((), (), s32[]{:S(2)}) async-start(), calls=%async_computation.19 | async-start | bytes 1310720 | tf_op jit(solution)/shard_map/all_gather | solution.py:279
  2352.8 81.0 %copy-start.16 = (pred[256,1024]{0,1:T(8,128)(4,1)S(1)}, pred[256,1024]{0,1:T(8,128)(4,1)}, u32[]{:S(2)}) copy-start(pred[256,1024]{0,1:T(8,128)(4,1)} %get-tuple-element.1277) | copy-start | bytes 786436
  2352.8 81.0 %copy-start.99 = (bf16[2048]{0:T(1024)(128)(2,1)S(1)}, bf16[2048]{0:T(1024)(128)(2,1)}, u32[]{:S(2)}) copy-start(bf16[2048]{0:T(1024)(128)(2,1)} %copy-done.98) | copy-start | bytes 12292
  2544.7 28.1 collective-permute-start.1
  2604.0 58.6 all-gather.40.cloned.1.call-start
  2619.3 387.6 %reduce-scatter.9.cloned.1.call-start = ((), (), s32[]{:S(2)}) async-start(), calls=%async_computation.21 | async-start | bytes 1310720 | tf_op jit(solution)/shard_map/reduce_scatter | solution.py:346
  2980.4 54.7 reduce-scatter.11.cloned.1.call-start
  2996.5 271.8 %reduce-scatter.13.cloned.1.call-start = ((), (), s32[]{:S(2)}) async-start(), calls=%async_computation.23 | async-start | bytes 1310720 | tf_op jit(solution)/shard_map/reduce_scatter | solution.py:346
  3057.0 9.0 collective-permute-start.2
  3242.9 53.5 reduce-scatter.15.cloned.1.call-start
  3255.5 394.4 %reduce-scatter.17.cloned.1.call-start = ((), (), s32[]{:S(2)}) async-start(), calls=%async_computation.25 | async-start | bytes 1310720 | tf_op jit(solution)/shard_map/reduce_scatter | solution.py:346
  3318.3 11.4 collective-permute-start.3
  3350.7 300.3 %reduce-scatter.19.cloned.1.call-start = ((), (), s32[]{:S(2)}) async-start(), calls=%async_computation.26 | async-start | bytes 1310720 | tf_op jit(solution)/shard_map/reduce_scatter | solution.py:349
  3387.8 79.6 %copy-start.44 = (bf16[2,256,2048]{2,1,0:T(8,128)(2,1)S(1)}, bf16[2,256,2048]{2,1,0:T(8,128)(2,1)}, u32[]{:S(2)}) copy-start(bf16[2,256,2048]{2,1,0:T(8,128)(2,1)} %get-tuple-element.1285) | copy-start | bytes 6291460
  3467.4 1912.9 %reduce-scatter.23.cloned.1.call-start = ((), (), s32[]{:S(2)}) async-start(), calls=%async_computation.29 | async-start | bytes 89128960 | tf_op jit(solution)/shard_map/reduce_scatter | solution.py:417
  3531.8 4051.7 %reduce-scatter.21.cloned.1.call-start = ((), (), s32[]{:S(2)}) async-start(), calls=%async_computation.27 | async-start | bytes 170459136 | tf_op jit(solution)/shard_map/reduce_scatter | solution.py:409
  3859.9 3832.2 %all-gather.44.cloned.1.call-start = ((), (), s32[]{:S(2)}) async-start(), calls=%async_computation.30 | async-start | bytes 13107200 | tf_op jit(solution)/shard_map/all_gather | solution.py:435
  5384.5 2495.7 %all-gather.42.cloned.1.call-start = ((), (), s32[]{:S(2)}) async-start(), calls=%async_computation.28 | async-start | bytes 25067520 | tf_op jit(solution)/shard_map/all_gather | solution.py:432
  (111 other events, 1440.0 us)
Sparse Core Ops, SparseCore 0:
  9.6 48.1 all-gather.17
  59.3 44.6 all-gather.19
  105.6 148.5 all-gather.15
  257.1 54.0 all-gather.23
  313.2 26.2 all-gather.21
  340.9 149.4 all-gather.25
  492.0 559.6 all-gather.27
  1053.3 559.5 all-gather.29
  1614.5 559.5 all-gather.31
  2332.4 70.6 all-gather.33
  2405.2 28.4 all-gather.35
  2604.1 27.7 all-gather.37
  2634.1 28.4 all-gather.39
  2980.5 25.9 reduce-scatter.8
  3009.2 25.7 reduce-scatter.10
  3243.0 25.2 reduce-scatter.12
  3270.5 25.8 reduce-scatter.14
  3350.8 180.2 reduce-scatter.16
  3533.4 115.1 reduce-scatter.18
  3650.9 1729.3 reduce-scatter.22
  5387.4 2196.1 reduce-scatter.20
  7586.0 106.0 all-gather.43
  7694.6 185.6 all-gather.41
where the time goes:
time: 7960 us; the launch traced here: 7940 us
  waiting for transfers between devices  6280 us (79%)
  matrix products  595 us (7%)
  local copies, waits for them, and re-layouts  574 us (7%)
  other arithmetic  414 us (5%)
    reduce_scatter x1, waiting for transfers between devices, shards(): lax.psum_scatter(jnp.concatenate([attn_part, ffn_part, gains], axis=1), (...  2200 us
    reduce_scatter x1, waiting for transfers between devices, shards(): lax.psum_scatter(jnp.concatenate([out_part, down_part.reshape(lax.axis_si...  1520 us
    all_gather x1, waiting for transfers between devices, shards(): lax.all_gather(local_weights[6], 'fsdp', axis=1, tiled=True)  561 us
    all_gather x1, waiting for transfers between devices, shards(): lax.all_gather(local_weights[8], 'fsdp', axis=1, tiled=True)  561 us
    all_gather x1, waiting for transfers between devices, shards(): lax.all_gather(local_weights[7], 'fsdp', axis=1, tiled=True)  561 us
    concatenate x1, local copies, waits for them, and re-layouts, shards(): jnp.concatenate([attn_part, ffn_part, gains], axis=1)  186 us
    dynamic_update_slice x59, other arithmetic, store_at(): lax.dynamic_update_index_in_dim(buffer, jnp.where(flag, value, previous),...  166 us
  transfers between devices with their start and end apart: 27, of which 20 were waited for; matrix products, arithmetic and copies ran while one was open for 10% of the time, Pallas kernels for 0%

commit v1 on v0

v1 whole, which is shorter than its diff:
```python
import jax
import jax.numpy as jnp
from jax import lax
from jax.sharding import PartitionSpec as P

HQ = 32
KVH = 8
HD = 64
FF = 8192

epsilon = 1e-05
rope_base = 500000.0
masked_score = -1e30
bf16 = jnp.bfloat16
f32 = jnp.float32
SWAP = [(0, 1), (1, 0)]


def partner(value, bit):
    count = lax.axis_size("rep")
    return lax.ppermute(value, "rep", [(i, i ^ bit) for i in range(count)])


def bit_list(count):
    found = []
    bit = 1
    while bit < count:
        found.append(bit)
        bit *= 2
    return found


def plane_gather(own):
    bits = bit_list(lax.axis_size("rep"))
    half = own.shape[0] // 2
    first, second = own[None, :half], own[None, half:]
    for bit in bits:
        first = jnp.concatenate([first, partner(first, bit)], axis=0)
    for bit in bits[::-1]:
        other = partner(second, bit)
        second = jnp.stack([second, other], axis=1).reshape((-1,) + own[:half].shape)
    return jnp.stack([first, second])


def plane_reduce(parts):
    bits = bit_list(lax.axis_size("rep"))
    first, second = parts[0], parts[1]
    for bit in bits[::-1]:
        keep, away = first[:bit], first[bit:]
        first = keep.astype(f32) + partner(away.astype(bf16), bit).astype(f32)
    for bit in bits:
        pair = second.reshape((-1, 2) + second.shape[1:])
        keep, away = pair[:, 0], pair[:, 1]
        second = keep.astype(f32) + partner(away.astype(bf16), bit).astype(f32)
    return jnp.concatenate([first[0], second[0]], axis=0)


def core_split(value, core):
    half = value.shape[0] // 2
    kept = lax.dynamic_slice_in_dim(value, core * half, half)
    sent = lax.dynamic_slice_in_dim(value, (1 - core) * half, half)
    got = lax.ppermute(sent, "section", SWAP)
    return (jnp.where(core == 0, kept, got), jnp.where(core == 0, got, kept))


def rope_tables(positions):
    half_size = HD // 2
    frequency = rope_base ** (-(jnp.arange(half_size).astype(f32) * 2.0) / HD)
    angles = positions[..., None] * frequency
    angles = jnp.concatenate([angles, angles], axis=-1)
    return (jnp.cos(angles), jnp.sin(angles))


def rotary(values, cosine_table, sine_table):
    half_size = values.shape[-1] // 2
    turned = jnp.concatenate([-values[..., half_size:], values[..., :half_size]], axis=-1)
    return values * cosine_table + turned * sine_table


def rotary_back(grad_rot, cosine_table, sine_table):
    half_size = grad_rot.shape[-1] // 2
    scaled = grad_rot * sine_table
    return grad_rot * cosine_table + jnp.concatenate(
        [scaled[..., half_size:], -scaled[..., :half_size]], axis=-1
    )


def times(left, weight):
    return jnp.dot(left, weight, preferred_element_type=f32)


def times_back(left, weight):
    return lax.dot_general(
        left, weight, (((1,), (1,)), ((), ())), preferred_element_type=f32
    )


def rows_product(left, right):
    return lax.dot_general(
        left, right, (((0,), (0,)), ((), ())), preferred_element_type=f32
    ).astype(bf16)


def scale_of(values):
    return lax.rsqrt(jnp.mean(values * values, axis=-1, keepdims=True) + epsilon)


def norm_back(grad, gain, unit, scale):
    scaled = gain * grad
    out = scale * (scaled - unit * jnp.mean(scaled * unit, axis=-1, keepdims=True))
    return (out, jnp.sum(grad * unit, axis=0))


def attend(query, keyvals, bias):
    two, reps, half, width = query.shape
    kv_heads = keyvals[0].shape[-1] // (2 * HD)
    group = width // HD // kv_heads
    q = query.reshape(two, reps, half, kv_heads, group, HD)
    kv = jnp.stack(keyvals).reshape(len(keyvals), two, reps, half, 2, kv_heads, HD)
    kv = kv.transpose(4, 2, 0, 1, 3, 5, 6).reshape(2, reps, -1, kv_heads, HD)
    q = q.transpose(1, 0, 2, 3, 4, 5).reshape(reps, two * half, kv_heads, group, HD)
    scores = jnp.einsum("jtkgd,jskd->jkgst", q, kv[0], preferred_element_type=f32) * HD ** (-0.5)
    scores = scores + bias[:, None, None].astype(f32)
    row_max = jnp.max(scores, axis=-2)
    exp_scores = jnp.exp(scores - row_max[..., None, :])
    total = jnp.sum(exp_scores, axis=-2)
    probs = (exp_scores / total[..., None, :]).astype(bf16)
    mixed = jnp.einsum("jkgst,jskd->jtkgd", probs, kv[1], preferred_element_type=f32).astype(bf16)
    mixed = mixed.reshape(reps, two, half, width).transpose(1, 0, 2, 3)
    log_total = (row_max + jnp.log(total)).reshape(reps, kv_heads * group, two * half)
    return (mixed, log_total)


def attend_back(query, keyvals, grad_mixed, log_total, bias):
    two, reps, half, width = query.shape
    kv_heads = keyvals[0].shape[-1] // (2 * HD)
    group = width // HD // kv_heads
    depth = len(keyvals)

    def heads(v):
        v = v.reshape(two, reps, half, kv_heads, group, HD)
        return v.transpose(1, 0, 2, 3, 4, 5).reshape(reps, two * half, kv_heads, group, HD)

    q, go = heads(query), heads(grad_mixed)
    kv = jnp.stack(keyvals).reshape(depth, two, reps, half, 2, kv_heads, HD)
    kv = kv.transpose(4, 2, 0, 1, 3, 5, 6).reshape(2, reps, -1, kv_heads, HD)
    scale = HD ** (-0.5)
    scores = jnp.einsum("jtkgd,jskd->jkgst", q, kv[0], preferred_element_type=f32) * scale
    scores = scores + bias[:, None, None].astype(f32)
    lse = log_total.reshape(reps, kv_heads, group, 1, two * half)
    probs = jnp.exp(scores - lse)
    grad_probs = jnp.einsum("jtkgd,jskd->jkgst", go, kv[1], preferred_element_type=f32)
    inner = jnp.sum(probs * grad_probs, axis=-2, keepdims=True)
    grad_scores = (probs * (grad_probs - inner)).astype(bf16)
    grad_q = jnp.einsum("jkgst,jskd->jtkgd", grad_scores, kv[0], preferred_element_type=f32) * scale
    grad_k = jnp.einsum("jkgst,jtkgd->jskd", grad_scores, q, preferred_element_type=f32) * scale
    grad_v = jnp.einsum("jkgst,jtkgd->jskd", probs.astype(bf16), go, preferred_element_type=f32)
    grad_q = grad_q.reshape(reps, two, half, width).transpose(1, 0, 2, 3)
    grad_kv = jnp.stack([grad_k, grad_v]).astype(bf16)
    grad_kv = grad_kv.reshape(2, reps, depth, two, half, kv_heads, HD)
    grad_kv = grad_kv.transpose(2, 3, 1, 4, 0, 5, 6).reshape(depth, two, reps, half, -1)
    return (grad_q, [grad_kv[i] for i in range(depth)])


def shards(
    tokens,
    segment_ids,
    cotangent,
    norm_attn,
    w_query,
    w_key,
    w_value,
    w_output,
    norm_ffn,
    w_gate,
    w_up,
    w_down,
):
    core = lax.axis_index("section")
    layer_z = lax.axis_index("fsdp")
    rep = lax.axis_index("rep")
    depth = lax.axis_size("fsdp")
    reps = lax.axis_size("rep")
    rows, width = tokens.shape[2:]
    half = rows // 2
    count = reps * rows
    q_width = HQ * HD // reps
    k_width = KVH * HD // reps
    ff_width = FF // reps
    ff_piece = FF // (reps * depth)

    gains = lax.all_gather(
        jnp.concatenate([norm_attn, norm_ffn], axis=0), ("section", "fsdp"), axis=0, tiled=False
    )
    gains = gains.reshape(2, depth, 2, -1).transpose(0, 2, 1, 3).reshape(2, 2, width).astype(f32)
    own_ids = lax.dynamic_index_in_dim(segment_ids[0], core, 0, keepdims=False)
    ids = lax.all_gather(own_ids, ("rep", "fsdp"), axis=0, tiled=True).reshape(reps, depth * rows)
    ids = jnp.stack([lax.dynamic_index_in_dim(ids, rep ^ j, 0, keepdims=False) for j in range(reps)])

    def columns(weight, size):
        return lax.dynamic_slice_in_dim(weight[0], rep * size, size, axis=1)

    def hidden_columns(weight):
        cut = weight[0].reshape(weight.shape[1], depth, reps, ff_piece)
        return lax.dynamic_index_in_dim(cut, rep, 2, keepdims=False).reshape(weight.shape[1], -1)

    qkv_cut = jnp.concatenate(
        [columns(w_query, q_width), columns(w_key, k_width), columns(w_value, k_width)], axis=1
    )
    out_rows = w_output.shape[1] // reps
    out_cut = lax.dynamic_slice_in_dim(w_output[0], rep * out_rows, out_rows)
    ffn_cut = jnp.concatenate([hidden_columns(w_gate), hidden_columns(w_up)], axis=1)
    down_cut = lax.dynamic_slice_in_dim(w_down[0], rep * ff_piece, ff_piece)

    def spread(pieces):
        return [lax.all_gather(v, ("fsdp", "section"), axis=0, tiled=True) for v in pieces]

    qkv_all = spread(core_split(qkv_cut, core))
    ffn_all = spread(core_split(ffn_cut, core))
    down_all = spread(core_split(down_cut, core))
    out_all = [
        lax.all_to_all(v, "rep", 0, 0, tiled=True) for v in spread(core_split(out_cut, core))
    ]

    row_at = layer_z * rows + jnp.arange(rows)
    query_ids = lax.dynamic_slice_in_dim(ids, layer_z * rows, rows, axis=1)
    starts = jnp.sum((ids[:, None, :] < query_ids[:, :, None]).astype(jnp.int32), axis=-1)
    cosine, sine = rope_tables((row_at[None, :] - starts).astype(f32))

    def by_half(table):
        return table.reshape(reps, 2, half, 1, HD).transpose(1, 0, 2, 3, 4)

    cosine, sine = by_half(cosine), by_half(sine)
    biases = []
    for step in range(depth):
        block = jnp.maximum(layer_z - step, 0)
        key_ids = lax.dynamic_slice_in_dim(ids, block * rows, rows, axis=1)
        key_at = (layer_z - step) * rows + jnp.arange(rows)
        allowed = (key_ids[:, :, None] == query_ids[:, None, :]) & (
            (key_at[:, None] <= row_at[None, :]) & (key_at[:, None] >= 0)
        )
        biases.append(jnp.where(allowed, 0.0, masked_score).astype(bf16))
    bias = jnp.concatenate(biases, axis=1)

    def flat(value):
        return value.reshape(count, -1)

    def blocks(value):
        return value.reshape(2, reps, half, -1)

    def forward(layer, layer_in):
        gain_attn, gain_ffn = gains[layer, 0], gains[layer, 1]
        scale_in = scale_of(layer_in)
        a_all = plane_gather((layer_in * scale_in * gain_attn).astype(bf16))
        qkv = times(flat(a_all), qkv_all[layer])
        query = qkv[:, :q_width].reshape(2, reps, half, -1, HD)
        key = qkv[:, q_width : q_width + k_width].reshape(2, reps, half, -1, HD)
        query = blocks(rotary(query, cosine, sine).astype(bf16))
        key = blocks(rotary(key, cosine, sine).astype(bf16))
        value = blocks(qkv[:, q_width + k_width :].astype(bf16))
        keyval = jnp.concatenate([key, value], axis=-1)
        keyvals = [keyval] + [
            lax.ppermute(keyval, "fsdp", [(i, i + s) for i in range(depth - s)])
            for s in range(1, depth)
        ]
        mixed, log_total = attend(query, keyvals, bias)
        residual = layer_in + plane_reduce(blocks(times(flat(mixed), out_all[layer]).astype(bf16)))
        scale_mid = scale_of(residual)
        b_all = plane_gather((residual * scale_mid * gain_ffn).astype(bf16))
        pre = times(flat(b_all), ffn_all[layer])
        gate, up = pre[:, :ff_width], pre[:, ff_width:]
        hidden = (jax.nn.silu(gate) * up).astype(bf16)
        out = residual + plane_reduce(blocks(times(hidden, down_all[layer]).astype(bf16)))
        kept = (layer_in, scale_in, a_all, query, keyvals, mixed, log_total)
        return out.astype(bf16), kept + (residual, scale_mid, b_all, gate, up, hidden)

    def collect(part):
        return lax.psum_scatter(part, ("fsdp", "section"), scatter_dimension=0, tiled=True)

    def backward(layer, grad_out, kept):
        (layer_in, scale_in, a_all, query, keyvals, mixed, log_total) = kept[:7]
        (residual, scale_mid, b_all, gate, up, hidden) = kept[7:]
        gain_attn, gain_ffn = gains[layer, 0], gains[layer, 1]
        gm_all = plane_gather(grad_out)
        grad_hidden = times_back(flat(gm_all), down_all[layer])
        sig = jax.nn.sigmoid(gate)
        grad_gate = (grad_hidden * up * (sig * (1.0 + gate * (1.0 - sig)))).astype(bf16)
        grad_up = (grad_hidden * (gate * sig)).astype(bf16)
        grad_pre = jnp.concatenate([grad_gate, grad_up], axis=1)
        db = plane_reduce(blocks(times_back(grad_pre, ffn_all[layer]).astype(bf16)))
        unit = residual * scale_mid
        grad_mid, gain_grad_ffn = norm_back(db, gain_ffn, unit, scale_mid)
        grad_mid = grad_mid + grad_out.astype(f32)
        go_all = plane_gather(grad_mid.astype(bf16))
        grad_down = collect(rows_product(hidden, flat(gm_all)))
        grad_ffn = collect(rows_product(flat(b_all), grad_pre))
        grad_mixed = blocks(times_back(flat(go_all), out_all[layer]).astype(bf16))
        grad_query, grad_kv = attend_back(query, keyvals, grad_mixed, log_total, bias)
        own_kv = grad_kv[0].astype(f32)
        for s in range(1, depth):
            got = lax.ppermute(grad_kv[s], "fsdp", [(i, i - s) for i in range(s, depth)])
            own_kv = own_kv + got.astype(f32)
        grad_o = rows_product(flat(mixed), flat(go_all))
        grad_o = collect(lax.all_to_all(grad_o, "rep", 0, 0, tiled=True))
        grad_query = grad_query.reshape(2, reps, half, -1, HD)
        grad_key = own_kv[..., :k_width].reshape(2, reps, half, -1, HD)
        grad_query = rotary_back(grad_query, cosine, sine).astype(bf16)
        grad_key = rotary_back(grad_key, cosine, sine).astype(bf16)
        grad_value = own_kv[..., k_width:].astype(bf16)
        grad_qkv = jnp.concatenate([flat(grad_query), flat(grad_key), flat(grad_value)], axis=1)
        da = plane_reduce(blocks(times_back(grad_qkv, qkv_all[layer]).astype(bf16)))
        unit = layer_in * scale_in
        grad_in, gain_grad_attn = norm_back(da, gain_attn, unit, scale_in)
        grad_in = (grad_in + grad_mid).astype(bf16)
        grad_proj = collect(rows_product(flat(a_all), grad_qkv))
        return grad_in, (grad_proj, grad_o, grad_ffn, grad_down), (gain_grad_attn, gain_grad_ffn)

    own_tokens = lax.dynamic_index_in_dim(tokens[0], core, 0, keepdims=False)
    own_cotangent = lax.dynamic_index_in_dim(cotangent[0], core, 0, keepdims=False)
    out0, kept0 = forward(0, own_tokens.astype(f32))
    out1, kept1 = forward(1, out0.astype(f32))
    grad1, weights1, gain1 = backward(1, own_cotangent, kept1)
    grad0, weights0, gain0 = backward(0, grad1, kept0)

    def swapped(zero, one):
        got = lax.ppermute(jnp.where(core == 0, one, zero), "section", SWAP)
        return jnp.where(core == 0, zero, got), jnp.where(core == 0, got, one)

    outputs = jnp.stack(swapped(out0, out1))[None, None]
    input_grads = jnp.stack(swapped(grad0, grad1))[None, None]

    gain_sums = lax.psum(jnp.stack([jnp.stack(gain0), jnp.stack(gain1)]), ("section", "fsdp", "rep"))
    gain_sums = lax.dynamic_index_in_dim(gain_sums, core, 0, keepdims=False)
    piece = width // depth
    gain_sums = lax.dynamic_slice_in_dim(gain_sums, layer_z * piece, piece, axis=1)

    def whole(zero, one):
        pair = jnp.concatenate(swapped(zero, one), axis=0)
        return lax.all_gather(pair, "rep", axis=0, tiled=False)

    proj, outp, ffn, down = (whole(a, b) for a, b in zip(weights0, weights1))

    def side(value):
        return value.transpose(1, 0, 2).reshape(value.shape[1], -1).astype(f32)[None]

    def hidden_side(value):
        value = value.reshape(reps, -1, depth, ff_piece).transpose(1, 2, 0, 3)
        return value.reshape(value.shape[0], -1).astype(f32)[None]

    def stacked(value):
        return value.reshape(-1, value.shape[-1]).astype(f32)[None]

    return (
        outputs,
        input_grads,
        gain_sums[0][None],
        side(proj[..., :q_width]),
        side(proj[..., q_width : q_width + k_width]),
        side(proj[..., q_width + k_width :]),
        stacked(outp),
        gain_sums[1][None],
        hidden_side(ffn[..., :ff_width]),
        hidden_side(ffn[..., ff_width:]),
        stacked(down),
    )


def solution(mesh):
    in_specs = (
        P("rep", None, "fsdp", None),
        P("rep", None, "fsdp"),
        P("rep", None, "fsdp", None),
        P("section", "fsdp"),
        P("section", "fsdp", None),
        P("section", "fsdp", None),
        P("section", "fsdp", None),
        P("section", "fsdp", None),
        P("section", "fsdp"),
        P("section", "fsdp", None),
        P("section", "fsdp", None),
        P("section", "fsdp", None),
    )
    out_specs = (
        P("section", "rep", None, "fsdp", None),
        P("section", "rep", None, "fsdp", None),
        P("section", "fsdp"),
        P("section", "fsdp", None),
        P("section", "fsdp", None),
        P("section", "fsdp", None),
        P("section", "fsdp", None),
        P("section", "fsdp"),
        P("section", "fsdp", None),
        P("section", "fsdp", None),
        P("section", "fsdp", None),
    )
    return jax.shard_map(shards, mesh=mesh, in_specs=in_specs, out_specs=out_specs, check_vma=False)
```

time: 7960 us -> 2600 us (0.33)
  waiting for transfers between devices: 6280 us -> 1240 us
  local copies, waits for them, and re-layouts: 574 us -> 338 us
  other arithmetic: 414 us -> 245 us
  starting transfers between devices: 9.91 us -> 134 us
  matrix products: 595 us -> 472 us
  blocking collectives: 29.8 us -> 129 us
    reduce_scatter x8, waiting for transfers between devices: 3780 us -> 458 us  [collect(): lax.psum_scatter(part, ('fsdp', 'section'), scatter_dimension=0, tiled=True)]
    all_gather x15 -> x12, waiting for transfers between devices: 2430 us -> 137 us  [the longest x4 137 us: whole(): return lax.all_gather(pair, 'rep', axis=0, tiled=False)]
    ppermute x4 -> x86, waiting for transfers between devices: 64.2 us -> 632 us  [the longest x64 458 us: partner(): return lax.ppermute(value, 'rep', [(i, i ^ bit) for i in range(count)])]
    concatenate x1 -> x8, local copies, waits for them, and re-layouts: 186 us -> 12.9 us  [the longest x7 12.7 us: rotary_back(): jnp.concatenate([scaled[..., half_size:], -scaled[..., :half_size]], axis...]
    dynamic_update_slice x59 -> x0, other arithmetic: 166 us -> none  [store_at(): lax.dynamic_update_index_in_dim(buffer, jnp.where(flag, value, previous),...]
    convert_element_type x2 -> x23, local copies, waits for them, and re-layouts: 3.73 us -> 143 us  [the longest x6 124 us: hidden_side(): return value.reshape(value.shape[0], -1).astype(f32)[None]]
    ppermute x4 -> x86, starting transfers between devices: 7.65 us -> 119 us  [the longest x64 60.2 us: partner(): return lax.ppermute(value, 'rep', [(i, i ^ bit) for i in range(count)])]
    dot_general x32 -> x28, matrix products: 453 us -> 366 us  [the longest x8 101 us: rows_product(): lax.dot_general(left, right, (((0,), (0,)), ((), ())), preferred_element_...]
  transfers between devices with their start and end apart: 27 -> 109, of which waited for: 20 -> 60; matrix products, arithmetic and copies ran while one was open for 10% -> 26% of each run, Pallas kernels for 0% -> 0%
where the time goes in v1:
time: 2600 us; the launch traced here: 2580 us
  waiting for transfers between devices  1240 us (48%)
  matrix products  472 us (18%)
  local copies, waits for them, and re-layouts  338 us (13%)
  other arithmetic  245 us (9%)
  starting transfers between devices  134 us (5%)
  blocking collectives  129 us (5%)
    ppermute x64, waiting for transfers between devices, partner(): return lax.ppermute(value, 'rep', [(i, i ^ bit) for i in range(count)])  458 us
    reduce_scatter x8, waiting for transfers between devices, collect(): lax.psum_scatter(part, ('fsdp', 'section'), scatter_dimension=0, tiled=True)  458 us
    all_gather x4, waiting for transfers between devices, whole(): return lax.all_gather(pair, 'rep', axis=0, tiled=False)  137 us
    convert_element_type x6, local copies, waits for them, and re-layouts, hidden_side(): return value.reshape(value.shape[0], -1).astype(f32)[None]  124 us
    dot_general x8, matrix products, times_back(): lax.dot_general(left, weight, (((1,), (1,)), ((), ())), preferred_element...  106 us
    dot_general x8, matrix products, rows_product(): lax.dot_general(left, right, (((0,), (0,)), ((), ())), preferred_element_...  101 us
    dot_general x8, matrix products, times(): return jnp.dot(left, weight, preferred_element_type=f32)  90.8 us
    ppermute x6, waiting for transfers between devices, backward(): lax.ppermute(grad_kv[s], 'fsdp', [(i, i - s) for i in range(s, depth)])  81.7 us
  transfers between devices with their start and end apart: 109, of which 60 were waited for; matrix products, arithmetic and copies ran while one was open for 26% of the time, Pallas kernels for 0%

profile of v1, /device:TPU:1, one launch (start us, length us, event | category | flops | bytes accessed | tf_op | source)
XLA Modules:
  0.0 2580.4 jit_solution(14096648932243541566)
XLA Ops:
  45.1 28.0 %dynamic-slice_reduce_fusion = (bf16[512,4,512]{2,1,0:T(4,128)(2,1)S(1)}, bf16[512,4,512]{2,1,0:T(4,128)(2,1)S(1)}) fusion(bf16[512,4,4,512]{3,2,1,0:T(4,128)(2,1)} %reshape_squeeze.32, s32[]{:T(128)S(6)} %select_n.233, bf16[512,4,4,512]{3,2,1,0:T(4,128)(2,1)} %reshape_squeeze.31), kind=kLoop, calls=%fused_computation.69 | loop fusion | bytes 8388612 | tf_op jit(solution)/shard_map/jit(dynamic_index_in_dim)/dynamic_slice | solution.py:205
  92.1 31.5 %all-gather.6 = bf16[8,2,512]{2,1,0:T(2,128)(2,1)S(1)} all-gather(bf16[1,2,512]{2,1,0:T(2,128)(2,1)S(1)} %maximum_bitcast_fusion.16), channel_id=2, replica_groups=mesh['section'=2,'fsdp'=4,'rep'=4] {'section','fsdp'}, dimensions={0}, use_global_device_ids=true | all-gather | bytes 18432 | tf_op jit(solution)/shard_map/all_gather | solution.py:192
  125.7 33.1 %all-gather.1 = s32[1,1,4096]{2,1,0:T(1,128)S(1)} all-gather(s32[1,1,256]{2,1,0:T(1,128)S(1)} %constant_dynamic-slice_fusion.12), channel_id=3, replica_groups=mesh['section'=2,'fsdp'=4,'rep'=4] {'rep','fsdp'}, dimensions={2}, use_global_device_ids=true | all-gather | bytes 17408 | tf_op jit(solution)/shard_map/all_gather | solution.py:197
  220.7 22.5 collective-permute-done.6
  371.0 21.9 collective-permute-done.16
  395.8 21.5 fusion.194
  531.0 21.9 collective-permute-start.28
  575.2 22.5 collective-permute-done.27
  761.1 23.9 fusion.196
  785.0 21.6 multiply_convert_fusion.3
  806.6 23.0 fusion.26
  922.9 22.0 fusion.3
  944.9 27.7 %fusion.5 = bf16[4,2,4,1024,256]{4,3,2,1,0:T(8,128)(2,1)} fusion(f32[4,2,1024,256,4]{3,2,4,1,0:T(8,128)} %get-tuple-element.175, f32[4,2,1024,256,4]{3,2,4,1,0:T(8,128)} %get-tuple-element.173, f32[4,2,4,256]{3,2,1,0:T(4,128)S(1)} %get-tuple-element.174, f32[4,2,4,256]{3,2,1,0:T(4,128)S(1)} %bitcast.946), kind=kLoop, calls=%fused_computation.9 | loop fusion | flops 33554432 | bytes 83951616 | tf_op jit(solution)/shard_map/convert_element_type | solution.py:154
  1019.6 30.0 %collective-permute-done.55 = bf16[2,4,128,256]{2,3,1,0:T(8,128)(2,1)} collective-permute-done((bf16[2,4,128,256]{2,3,1,0:T(8,128)(2,1)}, bf16[2,4,128,256]{2,3,1,0:T(8,128)(2,1)}, u32[]{:S(2)}, u32[]{:S(2)}) %collective-permute-start.55) | collective-permute-done | bytes 524320 | tf_op jit(solution)/shard_map/ppermute | solution.py:301
  1049.6 24.0 collective-permute-done.56
  1129.5 21.2 collective-permute-done.65
  1153.6 21.1 multiply_convert_fusion.1
  1174.7 23.0 fusion.27
  1269.6 22.9 collective-permute-done.73
  1297.3 24.6 all_to_all.48
  1343.8 22.2 fusion
  1366.0 28.7 %fusion.2 = bf16[4,2,4,1024,256]{4,3,2,1,0:T(8,128)(2,1)} fusion(f32[4,2,1024,256,4]{3,2,4,1,0:T(8,128)} %get-tuple-element.177, f32[4,2,1024,256,4]{3,2,4,1,0:T(8,128)} %get-tuple-element.171, f32[4,2,4,256]{3,2,1,0:T(4,128)S(1)} %get-tuple-element.176, f32[4,2,4,256]{3,2,1,0:T(4,128)S(1)} %bitcast.942), kind=kLoop, calls=%fused_computation.4 | loop fusion | flops 33554432 | bytes 83951616 | tf_op jit(solution)/shard_map/convert_element_type | solution.py:154
  1525.8 25.9 %convolution_convert_fusion = bf16[2048,4096]{1,0:T(8,128)(2,1)} fusion(bf16[1024,2048]{1,0:T(8,128)(2,1)} %bitcast.891, bf16[1024,2048]{1,0:T(8,128)(2,1)} %get-tuple-element.36, bf16[1024,2048]{1,0:T(8,128)(2,1)} %get-tuple-element.35), kind=kOutput, calls=%fused_computation.36 | convolution fusion | flops 17205035008 | bytes 29360128 | tf_op jit(solution)/shard_map/dot_general | solution.py:99
  1551.8 25.6 convolution_convert_fusion.1
  1590.6 36.5 %reduce-scatter.23.cloned.1.call-done = bf16[256,2048]{1,0:T(8,128)(2,1)} async-done(((bf16[2048,2048]{1,0:T(8,128)(2,1)}), bf16[256,2048]{1,0:T(8,128)(2,1)}) %reduce-scatter.23.cloned.1.call-update) | async-done | bytes 1048592 | tf_op jit(solution)/shard_map/reduce_scatter | solution.py:278
  1627.1 90.7 %reduce-scatter.21.cloned.1.call-done = bf16[256,2048]{1,0:T(8,128)(2,1)} async-done(((bf16[2048,2048]{1,0:T(8,128)(2,1)}), bf16[256,2048]{1,0:T(8,128)(2,1)}) %reduce-scatter.21.cloned.1.call-update) | async-done | bytes 1048592 | tf_op jit(solution)/shard_map/reduce_scatter | solution.py:278
  1726.2 161.0 %reduce-scatter.19.cloned.1.call-done = bf16[256,4096]{1,0:T(8,128)(2,1)} async-done(((bf16[2048,4096]{1,0:T(8,128)(2,1)}), bf16[256,4096]{1,0:T(8,128)(2,1)}) %reduce-scatter.19.cloned.1.call-update) | async-done | bytes 2097168 | tf_op jit(solution)/shard_map/reduce_scatter | solution.py:278
  1887.2 169.4 %reduce-scatter.17.cloned.1.call-done = bf16[256,4096]{1,0:T(8,128)(2,1)} async-done(((bf16[2048,4096]{1,0:T(8,128)(2,1)}), bf16[256,4096]{1,0:T(8,128)(2,1)}) %reduce-scatter.17.cloned.1.call-update) | async-done | bytes 2097168 | tf_op jit(solution)/shard_map/reduce_scatter | solution.py:278
  2083.9 32.2 %collective-permute-done.40 = bf16[2,128,2048]{2,1,0:T(8,128)(2,1)S(1)} collective-permute-done((bf16[2,128,2048]{2,1,0:T(8,128)(2,1)S(1)}, bf16[2,128,2048]{2,1,0:T(8,128)(2,1)S(1)}, u32[]{:S(2)}, u32[]{:S(2)}) %collective-permute-start.40) | collective-permute-done | bytes 1048608 | tf_op jit(solution)/shard_map/ppermute | solution.py:21
  2148.5 32.9 %collective-permute-done.79 = bf16[2,128,2048]{2,1,0:T(8,128)(2,1)S(1)} collective-permute-done((bf16[2,128,2048]{2,1,0:T(8,128)(2,1)S(1)}, bf16[2,128,2048]{2,1,0:T(8,128)(2,1)S(1)}, u32[]{:S(2)}, u32[]{:S(2)}) %collective-permute-start.79) | collective-permute-done | bytes 1048608 | tf_op jit(solution)/shard_map/ppermute | solution.py:21
  2215.2 39.7 %psum.7 = f32[2,2,2048]{2,1,0:T(2,128)S(1)} all-reduce(f32[2,2,2048]{2,1,0:T(2,128)S(1)} %pad_maximum_fusion.64), channel_id=1, replica_groups=mesh['section'=2,'fsdp'=4,'rep'=4] {'section','fsdp','rep'}, use_global_device_ids=true, to_apply=%region_19.20 | all-reduce | flops 8192 | bytes 65536 | tf_op jit(solution)/shard_map/psum | solution.py:332
  2295.7 136.7 %all-gather.40.cloned.1.call-done = bf16[2048,4096]{1,0:T(8,128)(2,1)} async-done(((bf16[512,4096]{1,0:T(8,128)(2,1)}), bf16[2048,4096]{1,0:T(8,128)(2,1)}) %all-gather.40.cloned.1.call-update) | async-done | bytes 16777232 | tf_op jit(solution)/shard_map/all_gather | solution.py:339
  (832 shorter events, 1273.0 us)
Async XLA Ops:
  7.2 176.7 %all-gather.22.cloned.1.call-start = ((), (), s32[]{:S(2)}) async-start(), calls=%async_computation.13 | async-start | bytes 2359296 | tf_op jit(solution)/shard_map/all_gather | solution.py:216
  11.9 177.5 %all-gather.20.cloned.1.call-start = ((), (), s32[]{:S(2)}) async-start(), calls=%async_computation.12 | async-start | bytes 3538944 | tf_op jit(solution)/shard_map/all_gather | solution.py:216
  16.0 379.8 %all-gather.24.cloned.1.call-start = ((), (), s32[]{:S(2)}) async-start(), calls=%async_computation.14 | async-start | bytes 18874368 | tf_op jit(solution)/shard_map/all_gather | solution.py:216
  82.3 345.5 %all-gather.26.cloned.1.call-start = ((), (), s32[]{:S(2)}) async-start(), calls=%async_computation.15 | async-start | bytes 9437184 | tf_op jit(solution)/shard_map/all_gather | solution.py:216
  90.8 400.8 %all-gather.30.cloned.1.call-start = ((), (), s32[]{:S(2)}) async-start(), calls=%async_computation.17 | async-start | bytes 2359296 | tf_op jit(solution)/shard_map/all_gather | solution.py:216
  91.4 426.1 %all-gather.28.cloned.1.call-start = ((), (), s32[]{:S(2)}) async-start(), calls=%async_computation.16 | async-start | bytes 3538944 | tf_op jit(solution)/shard_map/all_gather | solution.py:216
  92.0 669.2 %all-gather.32.cloned.1.call-start = ((), (), s32[]{:S(2)}) async-start(), calls=%async_computation.18 | async-start | bytes 18874368 | tf_op jit(solution)/shard_map/all_gather | solution.py:216
  183.9 132.8 %all-to-all-start = ((bf16[4,128,2048]{2,1,0:T(8,128)(2,1)}), bf16[4,128,2048]{2,1,0:T(8,128)(2,1)}, u32[]{:S(2)}, u32[]{:S(2)}) async-start(bf16[4,128,2048]{2,1,0:T(8,128)(2,1)} %bitcast.915), calls=%async_computation | async-start | bytes 4194304 | tf_op jit(solution)/shard_map/all_to_all | solution.py:222
  189.4 595.6 %all-gather.34.cloned.1.call-start = ((), (), s32[]{:S(2)}) async-start(), calls=%async_computation.19 | async-start | bytes 9437184 | tf_op jit(solution)/shard_map/all_gather | solution.py:216
  201.5 41.7 %collective-permute-start.6 = (bf16[2,4,128,256]{2,3,1,0:T(8,128)(2,1)S(1)}, bf16[2,4,128,256]{2,3,1,0:T(8,128)(2,1)}, u32[]{:S(2)}, u32[]{:S(2)}) collective-permute-start(bf16[2,4,128,256]{2,3,1,0:T(8,128)(2,1)S(1)} %pad_maximum_fusion.58), channel_id=1, source_target_pairs={{0,8},{4,12},{1,9},{5,13},{2,10},{6,14},{3,11},{7,15},{16,24},{20,... | collective-permute-start | bytes 1572872 | tf_op jit(solution)/shard_map/ppermute | solution.py:263
  206.3 55.3 %collective-permute-start.5 = (bf16[2,4,128,256]{2,3,1,0:T(8,128)(2,1)S(1)}, bf16[2,4,128,256]{2,3,1,0:T(8,128)(2,1)}, u32[]{:S(2)}, u32[]{:S(2)}) collective-permute-start(bf16[2,4,128,256]{2,3,1,0:T(8,128)(2,1)S(1)} %pad_maximum_fusion.58), channel_id=1, source_target_pairs={{0,4},{4,8},{8,12},{1,5},{5,9},{9,13},{2,6},{6,10},{10,14},{3,7},{... | collective-permute-start | bytes 1572872 | tf_op jit(solution)/shard_map/ppermute | solution.py:263
  491.7 161.7 %all-to-all-start.1 = ((bf16[4,128,2048]{2,1,0:T(8,128)(2,1)}), bf16[4,128,2048]{2,1,0:T(8,128)(2,1)}, u32[]{:S(2)}, u32[]{:S(2)}) async-start(bf16[4,128,2048]{2,1,0:T(8,128)(2,1)} %bitcast.914), calls=%async_computation.1 | async-start | bytes 4194304 | tf_op jit(solution)/shard_map/all_to_all | solution.py:222
  531.0 44.3 %collective-permute-start.28 = (bf16[2,4,128,256]{2,3,1,0:T(8,128)(2,1)}, bf16[2,4,128,256]{2,3,1,0:T(8,128)(2,1)}, u32[]{:S(2)}, u32[]{:S(2)}) collective-permute-start(bf16[2,4,128,256]{2,3,1,0:T(8,128)(2,1)} %pad_maximum_fusion.59), channel_id=1, source_target_pairs={{0,8},{4,12},{1,9},{5,13},{2,10},{6,14},{3,11},{7,15},{16,24},{20,... | collective-permute-start | bytes 1572872 | tf_op jit(solution)/shard_map/ppermute | solution.py:263
  552.8 44.9 %collective-permute-start.27 = (bf16[2,4,128,256]{2,3,1,0:T(8,128)(2,1)}, bf16[2,4,128,256]{2,3,1,0:T(8,128)(2,1)}, u32[]{:S(2)}, u32[]{:S(2)}) collective-permute-start(bf16[2,4,128,256]{2,3,1,0:T(8,128)(2,1)} %pad_maximum_fusion.59), channel_id=1, source_target_pairs={{0,4},{4,8},{8,12},{1,5},{5,9},{9,13},{2,6},{6,10},{10,14},{3,7},{... | collective-permute-start | bytes 1572872 | tf_op jit(solution)/shard_map/ppermute | solution.py:263
  665.8 39.8 %collective-permute-start.43 = (bf16[1,128,2048]{2,1,0:T(8,128)(2,1)S(1)}, bf16[1,128,2048]{2,1,0:T(8,128)(2,1)S(1)}, u32[]{:S(2)}, u32[]{:S(2)}) collective-permute-start(bf16[1,128,2048]{2,1,0:T(8,128)(2,1)S(1)} %get-tuple-element.78), channel_id=1, source_target_pairs={{0,1},{1,0},{2,3},{3,2},{4,5},{5,4},{6,7},{7,6},{8,9},{9,8},{10,11... | collective-permute-start | bytes 1572872 | tf_op jit(solution)/shard_map/ppermute | solution.py:21
  691.8 43.1 %collective-permute-start.46 = (bf16[2,128,2048]{2,1,0:T(8,128)(2,1)S(1)}, bf16[2,128,2048]{2,1,0:T(8,128)(2,1)S(1)}, u32[]{:S(2)}, u32[]{:S(2)}) collective-permute-start(bf16[2,128,2048]{2,1,0:T(8,128)(2,1)S(1)} %get-tuple-element.110), channel_id=1, source_target_pairs={{0,1},{1,0},{2,3},{3,2},{4,5},{5,4},{6,7},{7,6},{8,9},{9,8},{10,11... | collective-permute-start | bytes 3145736 | tf_op jit(solution)/shard_map/ppermute | solution.py:21
  1005.8 43.8 %collective-permute-start.55 = (bf16[2,4,128,256]{2,3,1,0:T(8,128)(2,1)}, bf16[2,4,128,256]{2,3,1,0:T(8,128)(2,1)}, u32[]{:S(2)}, u32[]{:S(2)}) collective-permute-start(bf16[2,4,128,256]{2,3,1,0:T(8,128)(2,1)} %bitcast.193), channel_id=1, source_target_pairs={{4,0},{8,4},{12,8},{5,1},{9,5},{13,9},{6,2},{10,6},{14,10},{7,3},{... | collective-permute-start | bytes 1572872 | tf_op jit(solution)/shard_map/ppermute | solution.py:301
  1007.5 66.1 %collective-permute-start.56 = (bf16[2,4,128,256]{2,3,1,0:T(8,128)(2,1)}, bf16[2,4,128,256]{2,3,1,0:T(8,128)(2,1)}, u32[]{:S(2)}, u32[]{:S(2)}) collective-permute-start(bf16[2,4,128,256]{2,3,1,0:T(8,128)(2,1)} %bitcast.194), channel_id=1, source_target_pairs={{8,0},{12,4},{9,1},{13,5},{10,2},{14,6},{11,3},{15,7},{24,16},{28,... | collective-permute-start | bytes 1572872 | tf_op jit(solution)/shard_map/ppermute | solution.py:301
  1232.8 344.7 %reduce-scatter.15.cloned.1.call-start = ((), (), s32[]{:S(2)}) async-start(), calls=%async_computation.23 | async-start | bytes 2359296 | tf_op jit(solution)/shard_map/reduce_scatter | solution.py:278
  1257.0 320.5 %reduce-scatter.13.cloned.1.call-start = ((), (), s32[]{:S(2)}) async-start(), calls=%async_computation.22 | async-start | bytes 2359296 | tf_op jit(solution)/shard_map/reduce_scatter | solution.py:278
  1321.9 263.7 %reduce-scatter.11.cloned.1.call-start = ((), (), s32[]{:S(2)}) async-start(), calls=%async_computation.21 | async-start | bytes 3538944 | tf_op jit(solution)/shard_map/reduce_scatter | solution.py:278
  1330.6 255.0 %reduce-scatter.9.cloned.1.call-start = ((), (), s32[]{:S(2)}) async-start(), calls=%async_computation.20 | async-start | bytes 3538944 | tf_op jit(solution)/shard_map/reduce_scatter | solution.py:278
  1442.6 42.3 %collective-permute-start.75 = (bf16[2,4,128,256]{2,3,1,0:T(8,128)(2,1)}, bf16[2,4,128,256]{2,3,1,0:T(8,128)(2,1)}, u32[]{:S(2)}, u32[]{:S(2)}) collective-permute-start(bf16[2,4,128,256]{2,3,1,0:T(8,128)(2,1)} %bitcast.255), channel_id=1, source_target_pairs={{8,0},{12,4},{9,1},{13,5},{10,2},{14,6},{11,3},{15,7},{24,16},{28,... | collective-permute-start | bytes 1572872 | tf_op jit(solution)/shard_map/ppermute | solution.py:301
  1497.3 129.8 %reduce-scatter.23.cloned.1.call-start = ((), (), s32[]{:S(2)}) async-start(), calls=%async_computation.27 | async-start | bytes 9437184 | tf_op jit(solution)/shard_map/reduce_scatter | solution.py:278
  1511.6 206.2 %reduce-scatter.21.cloned.1.call-start = ((), (), s32[]{:S(2)}) async-start(), calls=%async_computation.26 | async-start | bytes 9437184 | tf_op jit(solution)/shard_map/reduce_scatter | solution.py:278
  1525.8 361.4 %reduce-scatter.19.cloned.1.call-start = ((), (), s32[]{:S(2)}) async-start(), calls=%async_computation.25 | async-start | bytes 18874368 | tf_op jit(solution)/shard_map/reduce_scatter | solution.py:278
  1551.7 504.8 %reduce-scatter.17.cloned.1.call-start = ((), (), s32[]{:S(2)}) async-start(), calls=%async_computation.24 | async-start | bytes 18874368 | tf_op jit(solution)/shard_map/reduce_scatter | solution.py:278
  1577.4 682.0 %all-gather.38.cloned.1.call-start = ((), (), s32[]{:S(2)}) async-start(), calls=%async_computation.29 | async-start | bytes 2621440 | tf_op jit(solution)/shard_map/all_gather | solution.py:339
  1585.5 678.1 %all-gather.36.cloned.1.call-start = ((), (), s32[]{:S(2)}) async-start(), calls=%async_computation.28 | async-start | bytes 3932160 | tf_op jit(solution)/shard_map/all_gather | solution.py:339
  1590.5 691.5 %all-gather.42.cloned.1.call-start = ((), (), s32[]{:S(2)}) async-start(), calls=%async_computation.31 | async-start | bytes 10485760 | tf_op jit(solution)/shard_map/all_gather | solution.py:339
  1726.2 706.2 %all-gather.40.cloned.1.call-start = ((), (), s32[]{:S(2)}) async-start(), calls=%async_computation.30 | async-start | bytes 20971520 | tf_op jit(solution)/shard_map/all_gather | solution.py:339
  2211.5 44.1 %collective-permute-start.81 = (bf16[256,2048]{1,0:T(8,128)(2,1)}, bf16[256,2048]{1,0:T(8,128)(2,1)S(1)}, u32[]{:S(2)}, u32[]{:S(2)}) collective-permute-start(bf16[256,2048]{1,0:T(8,128)(2,1)} %get-tuple-element.19), channel_id=1, source_target_pairs={{0,16},{16,0},{1,17},{17,1},{2,18},{18,2},{3,19},{19,3},{4,20},{20... | collective-permute-start | bytes 3145736 | tf_op jit(solution)/shard_map/ppermute | solution.py:326
  (188 other events, 3428.0 us)
Sparse Core Ops, SparseCore 0:
  12.1 31.5 all-gather.21
  45.9 37.7 all-gather.19
  85.9 171.4 all-gather.23
  259.4 97.0 all-gather.25
  357.9 27.6 all-gather.29
  387.0 37.7 all-gather.27
  427.0 174.0 all-gather.31
  602.7 94.6 all-gather.33
  1257.1 43.5 reduce-scatter.14
  1322.1 34.8 reduce-scatter.12
  1359.2 39.2 reduce-scatter.10
  1497.4 38.2 reduce-scatter.8
  1538.0 89.0 reduce-scatter.22
  1629.8 87.9 reduce-scatter.20
  1720.5 166.5 reduce-scatter.18
  1890.0 166.5 reduce-scatter.16
  2058.3 45.6 all-gather.37
  2106.2 64.3 all-gather.35
  2173.0 99.6 all-gather.41
  2275.0 157.3 all-gather.39

commit v2 on v1

v2 whole, which is shorter than its diff:
```python
import functools

import jax
import jax.numpy as jnp
from jax import lax
from jax.experimental import pallas as pl
from jax.experimental.pallas import tpu as pltpu
from jax.sharding import PartitionSpec as P

HQ = 32
KVH = 8
HD = 64
FF = 8192

epsilon = 1e-05
rope_base = 500000.0
masked_score = -1e30
bf16 = jnp.bfloat16
f32 = jnp.float32
SWAP = [(0, 1), (1, 0)]


def partner(value, bit):
    count = lax.axis_size("rep")
    return lax.ppermute(value, "rep", [(i, i ^ bit) for i in range(count)])


def bit_list(count):
    found = []
    bit = 1
    while bit < count:
        found.append(bit)
        bit *= 2
    return found


def gather_start(own):
    half = own.shape[0] // 2
    return own[None, :half], own[None, half:]


def gather_step(state, at):
    bits = bit_list(lax.axis_size("rep"))
    first, second = state
    first = jnp.concatenate([first, partner(first, bits[at])], axis=0)
    other = partner(second, bits[-1 - at])
    second = jnp.stack([second, other], axis=1).reshape((-1,) + second.shape[1:])
    return first, second


def gather_rest(state, at):
    for step in range(at, len(bit_list(lax.axis_size("rep")))):
        state = gather_step(state, step)
    return jnp.stack(state)


def plane_gather(own):
    return gather_rest(gather_start(own), 0)


def plane_reduce(parts):
    bits = bit_list(lax.axis_size("rep"))
    first, second = parts[0], parts[1]
    for bit in bits[::-1]:
        keep, away = first[:bit], first[bit:]
        first = keep.astype(f32) + partner(away.astype(bf16), bit).astype(f32)
    for bit in bits:
        pair = second.reshape((-1, 2) + second.shape[1:])
        keep, away = pair[:, 0], pair[:, 1]
        second = keep.astype(f32) + partner(away.astype(bf16), bit).astype(f32)
    return jnp.concatenate([first[0], second[0]], axis=0)


def rope_tables(positions):
    half_size = HD // 2
    frequency = rope_base ** (-(jnp.arange(half_size).astype(f32) * 2.0) / HD)
    angles = positions[..., None] * frequency
    angles = jnp.concatenate([angles, angles], axis=-1)
    return (jnp.cos(angles), jnp.sin(angles))


def rotary(values, cosine_table, sine_table):
    half_size = values.shape[-1] // 2
    turned = jnp.concatenate([-values[..., half_size:], values[..., :half_size]], axis=-1)
    return values * cosine_table + turned * sine_table


def rotary_back(grad_rot, cosine_table, sine_table):
    half_size = grad_rot.shape[-1] // 2
    scaled = grad_rot * sine_table
    return grad_rot * cosine_table + jnp.concatenate(
        [scaled[..., half_size:], -scaled[..., :half_size]], axis=-1
    )


def times(left, weight):
    return jnp.dot(left, weight, preferred_element_type=f32)


def times_back(left, weight):
    return lax.dot_general(
        left, weight, (((1,), (1,)), ((), ())), preferred_element_type=f32
    )


def rows_product(left, right):
    return lax.dot_general(
        left, right, (((0,), (0,)), ((), ())), preferred_element_type=f32
    ).astype(bf16)


def scale_of(values):
    return lax.rsqrt(jnp.mean(values * values, axis=-1, keepdims=True) + epsilon)


def norm_back(grad, gain, unit, scale):
    scaled = gain * grad
    out = scale * (scaled - unit * jnp.mean(scaled * unit, axis=-1, keepdims=True))
    return (out, jnp.sum(grad * unit, axis=0))


def sequence(ref):
    return ref[:, 0].reshape(-1, ref.shape[-1])


def scaled(value):
    return (value.astype(f32) * HD ** (-0.5)).astype(bf16)


def dot(left, right, left_dim, right_dim):
    return lax.dot_general(
        left, right, (((left_dim,), (right_dim,)), ((), ())), preferred_element_type=f32
    )


def attend_kernel(depth, query_ref, bias_ref, *refs):
    mixed_ref, log_ref = refs[depth:]
    keyval = jnp.concatenate([sequence(ref) for ref in refs[:depth]], axis=0)
    query = scaled(sequence(query_ref))
    bias = bias_ref[0].astype(f32)
    k_width = keyval.shape[1] // 2
    heads = query.shape[1] // HD
    group = heads // (k_width // HD)
    columns = []
    for head in range(heads):
        at = head // group * HD
        key = keyval[:, at : at + HD]
        value = keyval[:, k_width + at : k_width + at + HD]
        scores = dot(key, query[:, head * HD : (head + 1) * HD], 1, 1) + bias
        row_max = jnp.max(scores, axis=0, keepdims=True)
        weights = jnp.exp(scores - row_max)
        total = jnp.sum(weights, axis=0, keepdims=True)
        probs = (weights * (1.0 / total)).astype(bf16)
        columns.append(dot(value, probs, 0, 0))
        log_ref[0, head : head + 1, :] = row_max + jnp.log(total)
    mixed = jnp.concatenate(columns, axis=0).T.astype(bf16)
    mixed_ref[:, 0] = mixed.reshape(2, -1, mixed.shape[1])


def attend_back_kernel(depth, query_ref, grad_ref, log_ref, bias_ref, *refs):
    grad_query_ref, grad_refs = refs[depth], refs[depth + 1 :]
    keyval = jnp.concatenate([sequence(ref) for ref in refs[:depth]], axis=0)
    query = scaled(sequence(query_ref))
    grad = sequence(grad_ref)
    bias = bias_ref[0].astype(f32)
    k_width = keyval.shape[1] // 2
    heads = query.shape[1] // HD
    group = heads // (k_width // HD)
    columns, grad_keys, grad_values = [], [], []
    for head in range(heads):
        at = head // group * HD
        key = keyval[:, at : at + HD]
        value = keyval[:, k_width + at : k_width + at + HD]
        own_query = query[:, head * HD : (head + 1) * HD]
        own_grad = grad[:, head * HD : (head + 1) * HD]
        scores = dot(key, own_query, 1, 1) + bias
        probs = jnp.exp(scores - log_ref[0, head : head + 1, :])
        grad_probs = dot(value, own_grad, 1, 1)
        inner = jnp.sum(probs * grad_probs, axis=0, keepdims=True)
        grad_scores = (probs * (grad_probs - inner)).astype(bf16)
        columns.append(dot(key, grad_scores, 0, 0))
        grad_key = dot(grad_scores, own_query, 1, 0)
        grad_value = dot(probs.astype(bf16), own_grad, 1, 0)
        if head % group == 0:
            grad_keys.append(grad_key)
            grad_values.append(grad_value)
        else:
            grad_keys[-1] = grad_keys[-1] + grad_key
            grad_values[-1] = grad_values[-1] + grad_value
    grad_query = jnp.concatenate(columns, axis=0).T * HD ** (-0.5)
    grad_query_ref[:, 0] = grad_query.reshape(2, -1, grad_query.shape[1])
    both = jnp.concatenate(grad_keys + grad_values, axis=1).astype(bf16)
    rows = both.shape[0] // depth
    for step, ref in enumerate(grad_refs):
        part = both[step * rows : (step + 1) * rows]
        ref[:, 0] = part.reshape(2, rows // 2, part.shape[1])


def sequence_spec(array):
    two, _, half, columns = array.shape
    return pl.BlockSpec((two, 1, half, columns), lambda j: (0, j, 0, 0))


def row_spec(array):
    return pl.BlockSpec((1,) + array.shape[1:], lambda j: (j, 0, 0))


def attend(query, keyvals, bias):
    two, reps, half, width = query.shape
    logs = jax.ShapeDtypeStruct((reps, width // HD, two * half), f32)
    cells = reps * width * two * half * bias.shape[1]
    return pl.pallas_call(
        functools.partial(attend_kernel, len(keyvals)),
        grid=(reps,),
        in_specs=[sequence_spec(query), row_spec(bias)] + [sequence_spec(v) for v in keyvals],
        out_specs=[sequence_spec(query), row_spec(logs)],
        out_shape=[jax.ShapeDtypeStruct(query.shape, bf16), logs],
        compiler_params=pltpu.CompilerParams(vmem_limit_bytes=48 << 20),
        cost_estimate=pl.CostEstimate(
            flops=16 * cells, bytes_accessed=8 << 20, transcendentals=cells // HD
        ),
        name="attend",
    )(query, bias, *keyvals)


def attend_back(query, keyvals, grad_mixed, log_total, bias):
    two, reps, half, width = query.shape
    cells = reps * width * two * half * bias.shape[1]
    outs = pl.pallas_call(
        functools.partial(attend_back_kernel, len(keyvals)),
        grid=(reps,),
        in_specs=[sequence_spec(query), sequence_spec(grad_mixed), row_spec(log_total)]
        + [row_spec(bias)]
        + [sequence_spec(v) for v in keyvals],
        out_specs=[sequence_spec(query)] + [sequence_spec(v) for v in keyvals],
        out_shape=[jax.ShapeDtypeStruct(query.shape, f32)]
        + [jax.ShapeDtypeStruct(v.shape, bf16) for v in keyvals],
        compiler_params=pltpu.CompilerParams(vmem_limit_bytes=48 << 20),
        cost_estimate=pl.CostEstimate(
            flops=40 * cells, bytes_accessed=12 << 20, transcendentals=cells // HD
        ),
        name="attend_back",
    )(query, grad_mixed, log_total, bias, *keyvals)
    return outs[0], outs[1:]


def by_core(which, refs, write):
    for at, ref in enumerate(refs):
        pl.when(which == at)(functools.partial(write, ref))


def columns_kernel(info, zero, one_sent, zero_sent, one, out_ref):
    which = info[0] + 2 * pl.program_id(0)
    reps, _, piece = zero.shape[1:]

    def write(ref):
        for rep in range(reps):
            out_ref[:, rep * piece : (rep + 1) * piece] = ref[0, rep ^ info[1]].astype(f32)

    by_core(which, (zero, one_sent, zero_sent, one), write)


def rows_kernel(info, zero, one_sent, zero_sent, one, out_ref):
    which = info[0] + 2 * pl.program_id(1)

    def write(ref):
        out_ref[...] = ref[0, 0].astype(f32)

    by_core(which, (zero, one_sent, zero_sent, one), write)


def proj_kernel(info, zero, one_sent, zero_sent, one, query_ref, key_ref, value_ref):
    which = info[0] + 2 * pl.program_id(0)
    reps = zero.shape[1]

    def write(ref):
        for rep in range(reps):
            block = ref[0, rep ^ info[1]].astype(f32)
            start = 0
            for out_ref in (query_ref, key_ref, value_ref):
                size = out_ref.shape[1] // reps
                out_ref[:, rep * size : (rep + 1) * size] = block[:, start : start + size]
                start += size

    by_core(which, (zero, one_sent, zero_sent, one), write)


def assembled(kernel, grid, half_dim, block, index, out_blocks, out_index, out_shapes, info, four):
    def chosen(at):
        def where_from(*steps):
            taken = steps[-1][0] + 2 * steps[half_dim] == at
            return tuple(jnp.where(taken, v, 0) for v in index(*steps))

        return where_from

    return pl.pallas_call(
        kernel,
        grid_spec=pltpu.PrefetchScalarGridSpec(
            num_scalar_prefetch=1,
            grid=grid,
            in_specs=[pl.BlockSpec(block, chosen(at)) for at in range(4)],
            out_specs=[pl.BlockSpec(b, out_index) for b in out_blocks],
        ),
        out_shape=[jax.ShapeDtypeStruct(v, f32) for v in out_shapes],
        compiler_params=pltpu.CompilerParams(vmem_limit_bytes=40 << 20),
        name=kernel.__name__,
    )(info, *four)


def assemble_columns(info, four, offset, piece, pieces):
    _, reps, rows, _ = four[0].shape
    return assembled(
        columns_kernel,
        (2, 2, pieces),
        0,
        (1, reps, rows, piece),
        lambda k, sub, at, info: (sub, 0, 0, offset + at),
        [(rows, reps * piece)],
        lambda k, sub, at, info: (2 * k + sub, at),
        [(4 * rows, reps * piece * pieces)],
        info,
        four,
    )[0]


def assemble_rows(info, four):
    _, reps, rows, columns = four[0].shape
    return assembled(
        rows_kernel,
        (reps, 2, 2),
        1,
        (1, 1, rows, columns),
        lambda rep, k, sub, info: (sub, rep ^ info[1], 0, 0),
        [(rows, columns)],
        lambda rep, k, sub, info: (4 * rep + 2 * k + sub, 0),
        [(4 * reps * rows, columns)],
        info,
        four,
    )[0]


def assemble_proj(info, four, sizes):
    _, reps, rows, columns = four[0].shape
    return assembled(
        proj_kernel,
        (2, 2),
        0,
        (1, reps, rows, columns),
        lambda k, sub, info: (sub, 0, 0, 0),
        [(rows, reps * size) for size in sizes],
        lambda k, sub, info: (2 * k + sub, 0),
        [(4 * rows, reps * size) for size in sizes],
        info,
        four,
    )


def together(*values):
    return lax.optimization_barrier(values)


def sum_everywhere(value):
    for axis in ("rep", "fsdp", "section"):
        count = lax.axis_size(axis)
        for bit in bit_list(count):
            value = value + lax.ppermute(value, axis, [(i, i ^ bit) for i in range(count)])
    return value


def shards(
    tokens,
    segment_ids,
    cotangent,
    norm_attn,
    w_query,
    w_key,
    w_value,
    w_output,
    norm_ffn,
    w_gate,
    w_up,
    w_down,
):
    core = lax.axis_index("section")
    layer_z = lax.axis_index("fsdp")
    rep = lax.axis_index("rep")
    depth = lax.axis_size("fsdp")
    reps = lax.axis_size("rep")
    rows, width = tokens.shape[2:]
    half = rows // 2
    count = reps * rows
    q_width = HQ * HD // reps
    k_width = KVH * HD // reps
    ff_width = FF // reps
    ff_piece = FF // (reps * depth)

    def back(value, step):
        return lax.ppermute(value, "fsdp", [(i, i + step) for i in range(depth - step)])

    def by_layer(own, got):
        return (jnp.where(core == 0, own, got), jnp.where(core == 0, got, own))

    own_gain = jnp.concatenate([norm_attn, norm_ffn], axis=0)
    turned = jnp.stack(
        [own_gain]
        + [
            lax.ppermute(own_gain, "fsdp", [(i, (i + s) % depth) for i in range(depth)])
            for s in range(1, depth)
        ]
    )
    own_gain = jnp.concatenate(
        [
            lax.dynamic_index_in_dim(turned, (layer_z - k + depth) % depth, 0, keepdims=False)
            for k in range(depth)
        ],
        axis=1,
    ).astype(f32)
    gains = by_layer(own_gain, lax.ppermute(own_gain, "section", SWAP))

    plane_ids = lax.dynamic_index_in_dim(segment_ids[0], core, 0, keepdims=True)
    for bit in bit_list(reps):
        plane_ids = jnp.concatenate([plane_ids, partner(plane_ids, bit)], axis=0)
    ids = [plane_ids] + [back(plane_ids, step) for step in range(1, depth)]

    def split(cut, total):
        size = total // 2
        got = lax.ppermute(cut((1 - core) * size, size), "section", SWAP)
        return by_layer(cut(core * size, size), got)

    def spread(pieces):
        return [lax.all_gather(v, ("fsdp", "section"), axis=0, tiled=True) for v in pieces]

    def qkv_cut(row, size):
        parts = ((w_query, q_width), (w_key, k_width), (w_value, k_width))
        return jnp.concatenate(
            [lax.dynamic_slice(w[0], (row, rep * n), (size, n)) for w, n in parts], axis=1
        )

    def ffn_cut(row, size):
        return jnp.concatenate(
            [
                lax.dynamic_slice(
                    w[0], (row, k * reps * ff_piece + rep * ff_piece), (size, ff_piece)
                )
                for w in (w_gate, w_up)
                for k in range(depth)
            ],
            axis=1,
        )

    out_rows = w_output.shape[1] // reps

    def attn_cut(row, size):
        height = out_rows * size // w_query.shape[1]
        first = rep * out_rows + row * out_rows // w_query.shape[1]
        out = lax.dynamic_slice_in_dim(w_output[0], first, height)
        return jnp.concatenate([qkv_cut(row, size), out.reshape(size, -1)], axis=1)

    def all_ffn_cut(row, size):
        height = ff_piece * size // w_gate.shape[1]
        first = rep * ff_piece + row * ff_piece // w_gate.shape[1]
        down = lax.dynamic_slice_in_dim(w_down[0], first, height)
        return jnp.concatenate([ffn_cut(row, size), down.reshape(size, -1)], axis=1)

    attn_all = spread(split(attn_cut, w_query.shape[1]))
    qkv_width = q_width + 2 * k_width
    qkv_all = [v[:, :qkv_width] for v in attn_all]
    out_all = [
        lax.all_to_all(v[:, qkv_width:].reshape(-1, width), "rep", 0, 0, tiled=True)
        for v in attn_all
    ]
    both_all = spread(split(all_ffn_cut, w_gate.shape[1]))
    ffn_all = [v[:, : 2 * ff_width] for v in both_all]
    down_all = [v[:, 2 * ff_width :].reshape(ff_width, width) for v in both_all]

    starts = jnp.zeros((reps, rows), jnp.int32)
    biases = []
    within = jnp.arange(rows)
    for step in range(depth):
        key_ids, here = ids[step][:, :, None], plane_ids[:, None, :]
        exists = layer_z >= step
        starts = starts + jnp.sum((exists & (key_ids < here)).astype(jnp.int32), axis=1)
        allowed = exists & (key_ids == here)
        if step == 0:
            allowed = allowed & (within[:, None] <= within[None, :])
        biases.append(jnp.where(allowed, 0.0, masked_score).astype(bf16))
    bias = jnp.concatenate(biases, axis=1)
    cosine, sine = rope_tables((layer_z * rows + within - starts).astype(f32))

    def by_half(table):
        return table.reshape(reps, 2, half, 1, HD).transpose(1, 0, 2, 3, 4)

    cosine, sine = by_half(cosine), by_half(sine)

    def flat(value):
        return value.reshape(count, -1)

    def blocks(value):
        return value.reshape(2, reps, half, -1)

    def forward(layer, layer_in):
        gain_attn, gain_ffn = gains[layer][0], gains[layer][1]
        scale_in = scale_of(layer_in)
        a_all = plane_gather((layer_in * scale_in * gain_attn).astype(bf16))
        qkv = times(flat(a_all), qkv_all[layer])
        query = qkv[:, :q_width].reshape(2, reps, half, -1, HD)
        key = qkv[:, q_width : q_width + k_width].reshape(2, reps, half, -1, HD)
        query = blocks(rotary(query, cosine, sine).astype(bf16))
        key = blocks(rotary(key, cosine, sine).astype(bf16))
        value = blocks(qkv[:, q_width + k_width :].astype(bf16))
        keyval = jnp.concatenate([key, value], axis=-1)
        keyvals = [keyval] + [
            back(keyval, step) for step in range(1, depth)
        ]
        mixed, log_total = attend(query, keyvals, bias)
        residual = layer_in + plane_reduce(blocks(times(flat(mixed), out_all[layer]).astype(bf16)))
        scale_mid = scale_of(residual)
        b_all = plane_gather((residual * scale_mid * gain_ffn).astype(bf16))
        pre = times(flat(b_all), ffn_all[layer])
        gate, up = pre[:, :ff_width], pre[:, ff_width:]
        hidden = (jax.nn.silu(gate) * up).astype(bf16)
        out = residual + plane_reduce(blocks(times(hidden, down_all[layer]).astype(bf16)))
        kept = (layer_in, scale_in, a_all, query, keyvals, mixed, log_total)
        return out.astype(bf16), kept + (residual, scale_mid, b_all, gate, up, hidden)

    def core_sum(part):
        cube = part.reshape(depth, 2, -1, part.shape[1])
        mine = lax.dynamic_index_in_dim(cube, core, 1, keepdims=False)
        sent = lax.dynamic_index_in_dim(cube, 1 - core, 1, keepdims=False)
        got = lax.ppermute(sent, "section", SWAP)
        total = (mine.astype(f32) + got.astype(f32)).astype(bf16)
        return total.reshape(-1, part.shape[1])

    def collect(total):
        return lax.psum_scatter(total, "fsdp", scatter_dimension=0, tiled=True)

    def backward(layer, grad_out, kept, earlier):
        (layer_in, scale_in, a_all, query, keyvals, mixed, log_total) = kept[:7]
        (residual, scale_mid, b_all, gate, up, hidden) = kept[7:]
        gain_attn, gain_ffn = gains[layer][0], gains[layer][1]
        last = earlier is not None
        if last:
            old_proj, old_o, old_ffn, old_down = earlier
            grad_out, old_ffn = together(grad_out, old_ffn)
        gm_all = flat(plane_gather(grad_out))
        gm_all, part_down = together(gm_all, rows_product(hidden, gm_all))
        if last:
            gm_all, old_ffn, old_down = together(gm_all, old_ffn, old_down)
            ffn_state = gather_step(gather_start(old_ffn), 0)
            down_state = gather_step(gather_start(old_down), 0)
        grad_hidden = times_back(gm_all, down_all[layer])
        sig = jax.nn.sigmoid(gate)
        grad_gate = (grad_hidden * up * (sig * (1.0 + gate * (1.0 - sig)))).astype(bf16)
        grad_up = (grad_hidden * (gate * sig)).astype(bf16)
        grad_pre = jnp.concatenate([grad_gate, grad_up], axis=1)
        grad_pre, part_down = together(grad_pre, core_sum(part_down))
        own_down = collect(part_down)
        if last:
            grad_pre, *states = together(grad_pre, *ffn_state, *down_state)
            ffn_state, down_state = states[:2], states[2:]
            whole_down = gather_rest(down_state, 1)
        db = blocks(times_back(grad_pre, ffn_all[layer]).astype(bf16))
        db, grad_pre = together(db, grad_pre)
        if last:
            db, whole_down, old_o, old_proj = together(db, whole_down, old_o, old_proj)
        db = plane_reduce(db)
        unit = residual * scale_mid
        grad_mid, gain_grad_ffn = norm_back(db, gain_ffn, unit, scale_mid)
        grad_mid = grad_mid + grad_out.astype(f32)
        go = grad_mid.astype(bf16)
        go, part_ffn = together(go, core_sum(rows_product(flat(b_all), grad_pre)))
        own_ffn = collect(part_ffn)
        go_all = flat(plane_gather(go))
        grad_mixed = blocks(times_back(go_all, out_all[layer]).astype(bf16))
        part_o = lax.all_to_all(rows_product(flat(mixed), go_all), "rep", 0, 0, tiled=True)
        if last:
            tied = together(grad_mixed, old_o, old_proj, *ffn_state)
            grad_mixed, old_o, old_proj, ffn_state = tied[0], tied[1], tied[2], tied[3:]
            wholes = (
                plane_gather(old_proj),
                plane_gather(old_o),
                gather_rest(ffn_state, 1),
                whole_down,
            )
        grad_query, grad_kv = attend_back(query, keyvals, grad_mixed, log_total, bias)
        grad_query, own_down, *grad_kv = together(grad_query, own_down, *grad_kv)
        own_kv = grad_kv[0].astype(f32)
        for s in range(1, depth):
            got = lax.ppermute(grad_kv[s], "fsdp", [(i, i - s) for i in range(s, depth)])
            own_kv = own_kv + got.astype(f32)
        own_o = collect(core_sum(part_o))
        grad_query = grad_query.reshape(2, reps, half, -1, HD)
        grad_key = own_kv[..., :k_width].reshape(2, reps, half, -1, HD)
        grad_query = rotary_back(grad_query, cosine, sine).astype(bf16)
        grad_key = rotary_back(grad_key, cosine, sine).astype(bf16)
        grad_value = own_kv[..., k_width:].astype(bf16)
        grad_qkv = jnp.concatenate([flat(grad_query), flat(grad_key), flat(grad_value)], axis=1)
        da = blocks(times_back(grad_qkv, qkv_all[layer]).astype(bf16))
        da, grad_qkv = together(da, grad_qkv)
        if last:
            da, *wholes = together(da, *wholes)
            sent = [lax.ppermute(v, "section", [(0, 1)]) for v in wholes]
            own_down = plane_gather(own_down)
        da = plane_reduce(da)
        unit = layer_in * scale_in
        grad_in, gain_grad_attn = norm_back(da, gain_attn, unit, scale_in)
        grad_in = (grad_in + grad_mid).astype(bf16)
        grad_in, part_proj = together(grad_in, core_sum(rows_product(flat(a_all), grad_qkv)))
        own_proj = collect(part_proj)
        gain_grads = jnp.stack([gain_grad_attn, gain_grad_ffn])
        if not last:
            return grad_in, (own_proj, own_o, own_ffn, own_down), gain_grads, None
        tied = together(grad_in, own_ffn, own_o, own_down, *sent)
        grad_in, own_ffn, own_o, own_down, sent = tied[0], tied[1], tied[2], tied[3], tied[4:]
        sums = (plane_gather(own_proj), plane_gather(own_o), plane_gather(own_ffn), own_down)
        return grad_in, sums, gain_grads, list(zip(wholes, sent))

    own_tokens = lax.dynamic_index_in_dim(tokens[0], core, 0, keepdims=False)
    own_cotangent = lax.dynamic_index_in_dim(cotangent[0], core, 0, keepdims=False)
    out0, kept0 = forward(0, own_tokens.astype(f32))
    out1, kept1 = forward(1, out0.astype(f32))
    grad1, sums1, gain1, _ = backward(1, own_cotangent, kept1, None)
    grad0, whole0, gain0, whole1 = backward(0, grad1, kept0, sums1)

    def swapped(zero, one):
        got = lax.ppermute(jnp.where(core == 0, one, zero), "section", SWAP)
        return jnp.where(core == 0, zero, got), jnp.where(core == 0, got, one)

    outputs = jnp.stack(swapped(out0, out1))[None, None]
    input_grads = jnp.stack(swapped(grad0, grad1))[None, None]

    gain_sums = sum_everywhere(jnp.concatenate([gain0, gain1], axis=0))
    gain_sums = gain_sums.reshape(2, 2, depth, -1)
    gain_sums = lax.dynamic_index_in_dim(gain_sums, core, 0, keepdims=False)
    gain_sums = lax.dynamic_index_in_dim(gain_sums, layer_z, 1, keepdims=False)

    info = jnp.stack([core, rep]).astype(jnp.int32)

    def four(zero, one):
        return (zero, one[1], lax.ppermute(zero, "section", [(1, 0)]), one[0])

    proj, outp, ffn, down = (four(a, b) for a, b in zip(whole0, whole1))
    grad_gate = assemble_columns(info, ffn, 0, ff_piece, depth)
    grad_up = assemble_columns(info, ffn, depth, ff_piece, depth)
    grad_down = assemble_rows(info, down)
    grad_output = assemble_rows(info, outp)
    grad_query, grad_key, grad_value = assemble_proj(info, proj, (q_width, k_width, k_width))
    return (
        outputs,
        input_grads,
        gain_sums[0][None],
        grad_query[None],
        grad_key[None],
        grad_value[None],
        grad_output[None],
        gain_sums[1][None],
        grad_gate[None],
        grad_up[None],
        grad_down[None],
    )


def solution(mesh):
    in_specs = (
        P("rep", None, "fsdp", None),
        P("rep", None, "fsdp"),
        P("rep", None, "fsdp", None),
        P("section", "fsdp"),
        P("section", "fsdp", None),
        P("section", "fsdp", None),
        P("section", "fsdp", None),
        P("section", "fsdp", None),
        P("section", "fsdp"),
        P("section", "fsdp", None),
        P("section", "fsdp", None),
        P("section", "fsdp", None),
    )
    out_specs = (
        P("section", "rep", None, "fsdp", None),
        P("section", "rep", None, "fsdp", None),
        P("section", "fsdp"),
        P("section", "fsdp", None),
        P("section", "fsdp", None),
        P("section", "fsdp", None),
        P("section", "fsdp", None),
        P("section", "fsdp"),
        P("section", "fsdp", None),
        P("section", "fsdp", None),
        P("section", "fsdp", None),
    )
    return jax.shard_map(shards, mesh=mesh, in_specs=in_specs, out_specs=out_specs, check_vma=False)
```

time: 2600 us -> 1980 us (0.76)
  waiting for transfers between devices: 1240 us -> 781 us
  matrix products: 472 us -> 281 us
  Pallas kernels: 0 us -> 189 us
  local copies, waits for them, and re-layouts: 338 us -> 189 us
  blocking collectives: 129 us -> 24.5 us
  starting transfers between devices: 134 us -> 230 us
    reduce_scatter x8, waiting for transfers between devices: 458 us -> 23.4 us  [collect(): return lax.psum_scatter(total, 'fsdp', scatter_dimension=0, tiled=True)]
    pallas_call x0 -> x9, Pallas kernels: none -> 189 us  [the longest x2 67 us: attend_back(): pl.pallas_call(functools.partial(attend_back_kernel, len(keyvals)), grid=...]
    dot_general x12 -> x0, matrix products: 175 us -> none  [the longest x2 44.1 us: attend_back(): jnp.einsum('jtkgd,jskd->jkgst', go, kv[1], preferred_element_type=f32)]
    convert_element_type x15 -> x0, local copies, waits for them, and re-layouts: 140 us -> none  [the longest x6 124 us: hidden_side(): return value.reshape(value.shape[0], -1).astype(f32)[None]]
    all_gather x4 -> x0, waiting for transfers between devices: 137 us -> none  [whole(): return lax.all_gather(pair, 'rep', axis=0, tiled=False)]
    ppermute x10 -> x36, starting transfers between devices: 36.5 us -> 127 us  [the longest x8 41.5 us: core_sum(): got = lax.ppermute(sent, 'section', SWAP)]
    ppermute x64 -> x98, waiting for transfers between devices: 458 us -> 531 us  [partner(): return lax.ppermute(value, 'rep', [(i, i ^ bit) for i in range(count)])]
    all_gather x2 -> x0, blocking collectives: 64.7 us -> none  [the longest x1 33.1 us: shards(): lax.all_gather(own_ids, ('rep', 'fsdp'), axis=0, tiled=True)]
  transfers between devices with their start and end apart: 109 -> 157, of which waited for: 60 -> 77; matrix products, arithmetic and copies ran while one was open for 26% -> 29% of each run, Pallas kernels for 0% -> 8%
where the time goes in v2:
time: 1980 us; the launch traced here: 1970 us
  waiting for transfers between devices  781 us (39%)
  matrix products  281 us (14%)
  other arithmetic  253 us (13%)
  starting transfers between devices  230 us (12%)
  local copies, waits for them, and re-layouts  189 us (10%)
  Pallas kernels  189 us (10%)
  blocking collectives  24.5 us (1%)
    ppermute x98, waiting for transfers between devices, partner(): return lax.ppermute(value, 'rep', [(i, i ^ bit) for i in range(count)])  531 us
    dot_general x8, matrix products, times_back(): lax.dot_general(left, weight, (((1,), (1,)), ((), ())), preferred_element...  115 us
    ppermute x6, waiting for transfers between devices, backward(): lax.ppermute(grad_kv[s], 'fsdp', [(i, i - s) for i in range(s, depth)])  97.7 us
    dot_general x8, matrix products, times(): return jnp.dot(left, weight, preferred_element_type=f32)  85.2 us
    dot_general x8, matrix products, rows_product(): lax.dot_general(left, right, (((0,), (0,)), ((), ())), preferred_element_...  81.5 us
    ppermute x98, starting transfers between devices, partner(): return lax.ppermute(value, 'rep', [(i, i ^ bit) for i in range(count)])  79.3 us
    ppermute x9, waiting for transfers between devices, back(): lax.ppermute(value, 'fsdp', [(i, i + step) for i in range(depth - step)])  68.7 us
    pallas_call x2, Pallas kernels, attend_back(): pl.pallas_call(functools.partial(attend_back_kernel, len(keyvals)), grid=...  67 us
  transfers between devices with their start and end apart: 157, of which 77 were waited for; matrix products, arithmetic and copies ran while one was open for 29% of the time, Pallas kernels for 8%

profile of v2, /device:TPU:1, one launch (start us, length us, event | category | flops | bytes accessed | tf_op | source)
XLA Modules:
  0.0 1966.6 jit_solution(4737315421900915568)
XLA Ops:
  151.1 22.5 %collective-permute-done.16.refs_3_ = bf16[2,4,128,256]{3,2,1,0:T(8,128)(2,1)S(1)} collective-permute-done((bf16[2,4,128,256]{3,2,1,0:T(8,128)(2,1)S(1)}, bf16[2,4,128,256]{3,2,1,0:T(8,128)(2,1)S(1)}, u32[]{:S(2)}, u32[]{:S(2)}) %collective-permute-start.16) | collective-permute-done | bytes 524320 | tf_op jit(solution)/shard_map/ppermute | solution.py:398
  173.6 28.7 %attend.2 = (bf16[2,4,128,512]{3,2,1,0:T(8,128)(2,1)S(1)}, f32[4,8,256]{2,1,0:T(8,128)S(1)}) custom-call(bf16[2,4,128,512]{3,2,1,0:T(8,128)(2,1)S(1)} %add_convert_fusion.3.query_ref, bf16[4,1024,256]{2,1,0:T(8,128)(2,1)} %pad_maximum_fusion.17.bias_ref, bf16[2,4,128,256]{3,2,1,0:T(8,128)(2,1)S(1)} %pad_maximum_fusion.65.refs_0_, ...), custom_call_target="tpu_custom_call" | custom-call | flops 8589934592 | bytes 8388608 | tf_op jit(solution)/shard_map/attend/pallas_call | solution.py:212
  209.4 18.4 collective-permute-done.19
  254.4 20.7 %collective-permute-done.24 = bf16[2,128,2048]{2,1,0:T(8,128)(2,1)S(1)} collective-permute-done((bf16[2,128,2048]{2,1,0:T(8,128)(2,1)S(1)}, bf16[2,128,2048]{2,1,0:T(8,128)(2,1)S(1)}, u32[]{:S(2)}, u32[]{:S(2)}) %collective-permute-start.24) | collective-permute-done | bytes 1048608 | tf_op jit(solution)/shard_map/ppermute | solution.py:25
  278.0 43.6 %all-gather.7.cloned.1.call-done = bf16[2048,6144]{1,0:T(8,128)(2,1)} async-done(((bf16[256,6144]{1,0:T(8,128)(2,1)}), bf16[2048,6144]{1,0:T(8,128)(2,1)}) %all-gather.7.cloned.1.call-update) | async-done | bytes 25165840 | tf_op jit(solution)/shard_map/all_gather | solution.py:431
  321.6 21.5 %fusion.8 = f32[1024,4096]{1,0:T(8,128)S(1)} fusion(bf16[1024,2048]{1,0:T(8,128)(2,1)} %bitcast.838, bf16[2048,6144]{1,0:T(8,128)(2,1)} %all-gather.7.cloned.1.call-done), kind=kOutput, calls=%fused_computation.12 | convolution fusion | flops 17179869184 | bytes 37748736 | tf_op jit(solution)/shard_map/dot_general | solution.py:97
  365.5 21.7 %collective-permute-done.28 = bf16[2,128,2048]{2,1,0:T(8,128)(2,1)S(1)} collective-permute-done((bf16[2,128,2048]{2,1,0:T(8,128)(2,1)S(1)}, bf16[2,128,2048]{2,1,0:T(8,128)(2,1)S(1)}, u32[]{:S(2)}, u32[]{:S(2)}) %collective-permute-start.28) | collective-permute-done | bytes 1048608 | tf_op jit(solution)/shard_map/ppermute | solution.py:25
  506.5 22.5 %collective-permute-done.36.refs_3_ = bf16[2,4,128,256]{3,2,1,0:T(8,128)(2,1)S(1)} collective-permute-done((bf16[2,4,128,256]{3,2,1,0:T(8,128)(2,1)S(1)}, bf16[2,4,128,256]{3,2,1,0:T(8,128)(2,1)S(1)}, u32[]{:S(2)}, u32[]{:S(2)}) %collective-permute-start.36) | collective-permute-done | bytes 524320 | tf_op jit(solution)/shard_map/ppermute | solution.py:398
  529.0 28.7 %attend.3 = (bf16[2,4,128,512]{3,2,1,0:T(8,128)(2,1)S(1)}, f32[4,8,256]{2,1,0:T(8,128)S(1)}) custom-call(bf16[2,4,128,512]{3,2,1,0:T(8,128)(2,1)S(1)} %add_convert_fusion.2.query_ref, bf16[4,1024,256]{2,1,0:T(8,128)(2,1)} %pad_maximum_fusion.17.bias_ref, bf16[2,4,128,256]{3,2,1,0:T(8,128)(2,1)S(1)} %pad_maximum_fusion.66.refs_0_, ...), custom_call_target="tpu_custom_call" | custom-call | flops 8589934592 | bytes 8388608 | tf_op jit(solution)/shard_map/attend/pallas_call | solution.py:212
  659.6 21.5 %fusion.4 = f32[1024,4096]{1,0:T(8,128)S(1)} fusion(bf16[1024,2048]{1,0:T(8,128)(2,1)} %bitcast.847, bf16[2048,6144]{1,0:T(8,128)(2,1)} %all-gather.11.cloned.1.call-done), kind=kOutput, calls=%fused_computation.8 | convolution fusion | flops 17179869184 | bytes 37748736 | tf_op jit(solution)/shard_map/dot_general | solution.py:97
  702.7 22.6 %collective-permute-start.54 = (bf16[4,256,2048]{2,1,0:T(8,128)(2,1)}, bf16[4,256,2048]{2,1,0:T(8,128)(2,1)}, u32[]{:S(2)}, u32[]{:S(2)}) collective-permute-start(bf16[4,256,2048]{2,1,0:T(8,128)(2,1)} %dynamic-slice_bitcast_fusion.3), channel_id=1, source_target_pairs={{0,16},{16,0},{1,17},{17,1},{2,18},{18,2},{3,19},{19,3},{4,20},{20... | collective-permute-start | bytes 12582920 | tf_op jit(solution)/shard_map/ppermute | solution.py:530
  725.3 21.0 %multiply_convert_fusion.3 = (bf16[1024,2048]{1,0:T(8,128)(2,1)}, bf16[1024,2048]{1,0:T(8,128)(2,1)}) fusion(f32[1024,4096]{1,0:T(8,128)} %copy-done.40, bf16[1024,2048]{1,0:T(8,128)(2,1)} %bitcast.845, bf16[2048,6144]{1,0:T(8,128)(2,1)} %all-gather.11.cloned.1.call-done), kind=kOutput, calls=%fused_computation.27 | convolution fusion | flops 8617197568 | bytes 37748736 | tf_op jit(solution)/shard_map/dot_general | solution.py:101
  762.0 24.2 %fusion.25 = bf16[1024,2048]{1,0:T(8,128)(2,1)} fusion(bf16[1024,4096]{1,0:T(8,128)(2,1)} %pad_maximum_fusion, bf16[2048,6144]{1,0:T(8,128)(2,1)} %all-gather.11.cloned.1.call-done), kind=kOutput, calls=%fused_computation.63 | convolution fusion | flops 17181966336 | bytes 29360128 | tf_op jit(solution)/shard_map/dot_general | solution.py:101
  786.1 23.8 %convolution_convert_fusion.1 = bf16[2048,4096]{1,0:T(8,128)(2,1)} fusion(bf16[1024,2048]{1,0:T(8,128)(2,1)S(1)} %bitcast.848, bf16[1024,4096]{1,0:T(8,128)(2,1)} %pad_maximum_fusion), kind=kOutput, calls=%fused_computation.5 | convolution fusion | flops 17188257792 | bytes 29360128 | tf_op jit(solution)/shard_map/dot_general | solution.py:107
  821.5 22.7 %collective-permute-done.57 = bf16[2,128,2048]{2,1,0:T(8,128)(2,1)S(1)} collective-permute-done((bf16[2,128,2048]{2,1,0:T(8,128)(2,1)S(1)}, bf16[2,128,2048]{2,1,0:T(8,128)(2,1)S(1)}, u32[]{:S(2)}, u32[]{:S(2)}) %collective-permute-start.57) | collective-permute-done | bytes 1048608 | tf_op jit(solution)/shard_map/ppermute | solution.py:25
  917.2 33.4 %attend_back.2 = (f32[2,4,128,512]{3,2,1,0:T(8,128)}, bf16[2,4,128,256]{3,2,1,0:T(8,128)(2,1)S(1)}, bf16[2,4,128,256]{3,2,1,0:T(8,128)(2,1)S(1)}, bf16[2,4,128,2...) custom-call(bf16[2,4,128,512]{3,2,1,0:T(8,128)(2,1)S(1)} %copy-done.8, bf16[2,4,128,512]{3,2,1,0:T(8,128)(2,1)} %bitcast.947, ...), custom_call_target="tpu_custom_call" | custom-call | flops 21474836480 | bytes 12582912 | tf_op jit(solution)/shard_map/attend_back/pallas_call | solution.py:229
  984.7 30.2 %collective-permute-done.66 = bf16[2,4,128,256]{3,2,1,0:T(8,128)(2,1)} collective-permute-done((bf16[2,4,128,256]{3,2,1,0:T(8,128)(2,1)}, bf16[2,4,128,256]{3,2,1,0:T(8,128)(2,1)}, u32[]{:S(2)}, u32[]{:S(2)}) %collective-permute-start.66) | collective-permute-done | bytes 524320 | tf_op jit(solution)/shard_map/ppermute | solution.py:589
  1015.0 28.2 %collective-permute-done.64 = bf16[2,4,128,256]{3,2,1,0:T(8,128)(2,1)} collective-permute-done((bf16[2,4,128,256]{3,2,1,0:T(8,128)(2,1)}, bf16[2,4,128,256]{3,2,1,0:T(8,128)(2,1)}, u32[]{:S(2)}, u32[]{:S(2)}) %collective-permute-start.64) | collective-permute-done | bytes 524320 | tf_op jit(solution)/shard_map/ppermute | solution.py:589
  1067.9 15.8 collective-permute-done.69
  1131.0 18.4 collective-permute-done.75
  1181.6 21.1 %multiply_convert_fusion.1 = (bf16[1024,2048]{1,0:T(8,128)(2,1)}, bf16[1024,2048]{1,0:T(8,128)(2,1)}) fusion(f32[1024,4096]{1,0:T(8,128)} %copy-done.39, bf16[1024,2048]{1,0:T(8,128)(2,1)} %bitcast.844, bf16[2048,6144]{1,0:T(8,128)(2,1)} %all-gather.7.cloned.1.call-done), kind=kOutput, calls=%fused_computation.24 | convolution fusion | flops 8617197568 | bytes 37748736 | tf_op jit(solution)/shard_map/dot_general | solution.py:101
  1231.9 24.0 %fusion.22 = bf16[1024,2048]{1,0:T(8,128)(2,1)} fusion(bf16[1024,4096]{1,0:T(8,128)(2,1)} %pad_maximum_fusion.1, bf16[2048,6144]{1,0:T(8,128)(2,1)} %all-gather.7.cloned.1.call-done), kind=kOutput, calls=%fused_computation.62 | convolution fusion | flops 17181966336 | bytes 29360128 | tf_op jit(solution)/shard_map/dot_general | solution.py:101
  1255.9 23.9 %convolution_convert_fusion = bf16[2048,4096]{1,0:T(8,128)(2,1)} fusion(bf16[1024,2048]{1,0:T(8,128)(2,1)S(1)} %bitcast.839, bf16[1024,4096]{1,0:T(8,128)(2,1)} %pad_maximum_fusion.1), kind=kOutput, calls=%fused_computation.4 | convolution fusion | flops 17188257792 | bytes 29360128 | tf_op jit(solution)/shard_map/dot_general | solution.py:107
  1290.8 22.9 %collective-permute-done.82 = bf16[2,128,2048]{2,1,0:T(8,128)(2,1)S(1)} collective-permute-done((bf16[2,128,2048]{2,1,0:T(8,128)(2,1)S(1)}, bf16[2,128,2048]{2,1,0:T(8,128)(2,1)S(1)}, u32[]{:S(2)}, u32[]{:S(2)}) %collective-permute-start.82) | collective-permute-done | bytes 1048608 | tf_op jit(solution)/shard_map/ppermute | solution.py:25
  1320.8 21.6 %collective-permute-done.86 = bf16[2,128,2048]{2,1,0:T(8,128)(2,1)S(1)} collective-permute-done((bf16[2,128,2048]{2,1,0:T(8,128)(2,1)S(1)}, bf16[2,128,2048]{2,1,0:T(8,128)(2,1)S(1)}, u32[]{:S(2)}, u32[]{:S(2)}) %collective-permute-start.86) | collective-permute-done | bytes 1048608 | tf_op jit(solution)/shard_map/ppermute | solution.py:25
  1385.6 21.7 %collective-permute-done.92 = bf16[2,128,2048]{2,1,0:T(8,128)(2,1)S(1)} collective-permute-done((bf16[2,128,2048]{2,1,0:T(8,128)(2,1)S(1)}, bf16[2,128,2048]{2,1,0:T(8,128)(2,1)S(1)}, u32[]{:S(2)}, u32[]{:S(2)}) %collective-permute-start.92) | collective-permute-done | bytes 1048608 | tf_op jit(solution)/shard_map/ppermute | solution.py:25
  1412.2 24.5 %all_to_all.42 = bf16[4,128,2048]{2,1,0:T(8,128)(2,1)S(1)} all-to-all(bf16[4,128,2048]{2,1,0:T(8,128)(2,1)S(1)} %bitcast.877), channel_id=1, replica_groups=mesh['section'=2,'fsdp'=4,'rep'=4] {'rep'}, dimensions={0} | all-to-all | bytes 4194304 | tf_op jit(solution)/shard_map/all_to_all | solution.py:575
  1453.7 33.5 %attend_back.3 = (f32[2,4,128,512]{3,2,1,0:T(8,128)}, bf16[2,4,128,256]{3,2,1,0:T(8,128)(2,1)S(1)}, bf16[2,4,128,256]{3,2,1,0:T(8,128)(2,1)S(1)}, bf16[2,4,128,2...) custom-call(bf16[2,4,128,512]{3,2,1,0:T(8,128)(2,1)S(1)} %copy-done.6, bf16[2,4,128,512]{3,2,1,0:T(8,128)(2,1)} %bitcast.946, ...), custom_call_target="tpu_custom_call" | custom-call | flops 21474836480 | bytes 12582912 | tf_op jit(solution)/shard_map/attend_back/pallas_call | solution.py:229
  1528.0 26.6 %collective-permute-done.94 = bf16[2,4,128,256]{3,2,1,0:T(8,128)(2,1)} collective-permute-done((bf16[2,4,128,256]{3,2,1,0:T(8,128)(2,1)S(1)}, bf16[2,4,128,256]{3,2,1,0:T(8,128)(2,1)}, u32[]{:S(2)}, u32[]{:S(2)}) %collective-permute-start.94) | collective-permute-done | bytes 524320 | tf_op jit(solution)/shard_map/ppermute | solution.py:589
  1716.4 60.3 %collective-permute-done.47 = bf16[2,128,2048]{2,1,0:T(8,128)(2,1)S(1)} collective-permute-done((bf16[2,128,2048]{2,1,0:T(8,128)(2,1)S(1)}, bf16[2,128,2048]{2,1,0:T(8,128)(2,1)S(1)}, u32[]{:S(2)}, u32[]{:S(2)}) %collective-permute-start.47) | collective-permute-done | bytes 1048608 | tf_op jit(solution)/shard_map/ppermute | solution.py:25
  1821.7 20.0 %reduce-scatter.23.cloned.1.call-done = bf16[256,768]{1,0:T(8,128)(2,1)} async-done(((bf16[1024,768]{1,0:T(8,128)(2,1)}), bf16[256,768]{1,0:T(8,128)(2,1)}) %reduce-scatter.23.cloned.1.call-update) | async-done | bytes 393232 | tf_op jit(solution)/shard_map/reduce_scatter | solution.py:535
  1911.3 17.5 rows_kernel.3
  (994 shorter events, 1140.5 us)
Async XLA Ops:
  7.2 89.7 %all-gather.5.cloned.1.call-start = ((), (), s32[]{:S(2)}) async-start(), calls=%async_computation.12 | async-start | bytes 5898240 | tf_op jit(solution)/shard_map/all_gather | solution.py:431
  14.3 307.3 %all-gather.7.cloned.1.call-start = ((), (), s32[]{:S(2)}) async-start(), calls=%async_computation.13 | async-start | bytes 28311552 | tf_op jit(solution)/shard_map/all_gather | solution.py:431
  34.3 383.3 %all-gather.9.cloned.1.call-start = ((), (), s32[]{:S(2)}) async-start(), calls=%async_computation.14 | async-start | bytes 5898240 | tf_op jit(solution)/shard_map/all_gather | solution.py:431
  35.1 624.6 %all-gather.11.cloned.1.call-start = ((), (), s32[]{:S(2)}) async-start(), calls=%async_computation.15 | async-start | bytes 28311552 | tf_op jit(solution)/shard_map/all_gather | solution.py:431
  110.0 63.5 %collective-permute-start.16 = (bf16[2,4,128,256]{3,2,1,0:T(8,128)(2,1)S(1)}, bf16[2,4,128,256]{3,2,1,0:T(8,128)(2,1)S(1)}, u32[]{:S(2)}, u32[]{:S(2)}) collective-permute-start(bf16[2,4,128,256]{3,2,1,0:T(8,128)(2,1)S(1)} %pad_maximum_fusion.65.refs_0_), channel_id=1, source_target_pairs={{0,12},{1,13},{2,14},{3,15},{16,28},{17,29},{18,30},{19,31}} | collective-permute-start | bytes 1572872 | tf_op jit(solution)/shard_map/ppermute | solution.py:398
  125.0 78.3 %all-to-all-start = ((bf16[4,128,2048]{2,1,0:T(8,128)(2,1)}), bf16[4,128,2048]{2,1,0:T(8,128)(2,1)}, u32[]{:S(2)}, u32[]{:S(2)}) async-start(bf16[4,128,2048]{2,1,0:T(8,128)(2,1)} %all_to_all.28), calls=%async_computation | async-start | bytes 4194304 | tf_op jit(solution)/shard_map/all_to_all | solution.py:469
  425.1 134.6 %all-to-all-start.1 = ((bf16[4,128,2048]{2,1,0:T(8,128)(2,1)}), bf16[4,128,2048]{2,1,0:T(8,128)(2,1)}, u32[]{:S(2)}, u32[]{:S(2)}) async-start(bf16[4,128,2048]{2,1,0:T(8,128)(2,1)} %all_to_all.31), calls=%async_computation.1 | async-start | bytes 4194304 | tf_op jit(solution)/shard_map/all_to_all | solution.py:469
  429.5 523.5 %reduce-scatter.9.cloned.1.call-start = ((), (), s32[]{:S(2)}) async-start(), calls=%async_computation.16 | async-start | bytes 5242880 | tf_op jit(solution)/shard_map/reduce_scatter | solution.py:535
  476.1 52.9 %collective-permute-start.36 = (bf16[2,4,128,256]{3,2,1,0:T(8,128)(2,1)S(1)}, bf16[2,4,128,256]{3,2,1,0:T(8,128)(2,1)S(1)}, u32[]{:S(2)}, u32[]{:S(2)}) collective-permute-start(bf16[2,4,128,256]{3,2,1,0:T(8,128)(2,1)S(1)} %pad_maximum_fusion.66.refs_0_), channel_id=1, source_target_pairs={{0,12},{1,13},{2,14},{3,15},{16,28},{17,29},{18,30},{19,31}} | collective-permute-start | bytes 1572872 | tf_op jit(solution)/shard_map/ppermute | solution.py:398
  817.9 295.5 %reduce-scatter.11.cloned.1.call-start = ((), (), s32[]{:S(2)}) async-start(), calls=%async_computation.17 | async-start | bytes 10485760 | tf_op jit(solution)/shard_map/reduce_scatter | solution.py:535
  953.0 61.9 %collective-permute-start.66 = (bf16[2,4,128,256]{3,2,1,0:T(8,128)(2,1)}, bf16[2,4,128,256]{3,2,1,0:T(8,128)(2,1)}, u32[]{:S(2)}, u32[]{:S(2)}) collective-permute-start(bf16[2,4,128,256]{3,2,1,0:T(8,128)(2,1)} %copy-done.17), channel_id=1, source_target_pairs={{12,0},{13,1},{14,2},{15,3},{28,16},{29,17},{30,18},{31,19}} | collective-permute-start | bytes 1572872 | tf_op jit(solution)/shard_map/ppermute | solution.py:589
  954.4 60.5 %collective-permute-start.65 = (bf16[2,4,128,256]{3,2,1,0:T(8,128)(2,1)}, bf16[2,4,128,256]{3,2,1,0:T(8,128)(2,1)}, u32[]{:S(2)}, u32[]{:S(2)}) collective-permute-start(bf16[2,4,128,256]{3,2,1,0:T(8,128)(2,1)} %copy-done.16), channel_id=1, source_target_pairs={{8,0},{12,4},{9,1},{13,5},{10,2},{14,6},{11,3},{15,7},{24,16},{28,... | collective-permute-start | bytes 1572872 | tf_op jit(solution)/shard_map/ppermute | solution.py:589
  955.7 87.4 %collective-permute-start.64 = (bf16[2,4,128,256]{3,2,1,0:T(8,128)(2,1)}, bf16[2,4,128,256]{3,2,1,0:T(8,128)(2,1)}, u32[]{:S(2)}, u32[]{:S(2)}) collective-permute-start(bf16[2,4,128,256]{3,2,1,0:T(8,128)(2,1)} %copy-done.15), channel_id=1, source_target_pairs={{4,0},{8,4},{12,8},{5,1},{9,5},{13,9},{6,2},{10,6},{14,10},{7,3},{... | collective-permute-start | bytes 1572872 | tf_op jit(solution)/shard_map/ppermute | solution.py:589
  976.7 112.9 %all-to-all-start.2 = ((bf16[4,128,2048]{2,1,0:T(8,128)(2,1)}), bf16[4,128,2048]{2,1,0:T(8,128)(2,1)}, u32[]{:S(2)}, u32[]{:S(2)}) async-start(bf16[4,128,2048]{2,1,0:T(8,128)(2,1)} %bitcast.876), calls=%async_computation.4 | async-start | bytes 4194304 | tf_op jit(solution)/shard_map/all_to_all | solution.py:575
  981.2 335.6 %reduce-scatter.13.cloned.1.call-start = ((), (), s32[]{:S(2)}) async-start(), calls=%async_computation.18 | async-start | bytes 1310720 | tf_op jit(solution)/shard_map/reduce_scatter | solution.py:535
  1110.0 206.8 %reduce-scatter.15.cloned.1.call-start = ((), (), s32[]{:S(2)}) async-start(), calls=%async_computation.19 | async-start | bytes 1966080 | tf_op jit(solution)/shard_map/reduce_scatter | solution.py:535
  1131.0 356.3 %reduce-scatter.17.cloned.1.call-start = ((), (), s32[]{:S(2)}) async-start(), calls=%async_computation.20 | async-start | bytes 5242880 | tf_op jit(solution)/shard_map/reduce_scatter | solution.py:535
  1287.8 74.2 %collective-permute-start.88 = (bf16[4,256,4096]{2,1,0:T(8,128)(2,1)}, bf16[4,256,4096]{2,1,0:T(8,128)(2,1)}, u32[]{:S(2)}, u32[]{:S(2)}) collective-permute-start(bf16[4,256,4096]{2,1,0:T(8,128)(2,1)} %dynamic-slice_bitcast_fusion), channel_id=1, source_target_pairs={{0,16},{16,0},{1,17},{17,1},{2,18},{18,2},{3,19},{19,3},{4,20},{20... | collective-permute-start | bytes 25165832 | tf_op jit(solution)/shard_map/ppermute | solution.py:530
  1346.4 337.2 %reduce-scatter.21.cloned.1.call-start = ((), (), s32[]{:S(2)}) async-start(), calls=%async_computation.22 | async-start | bytes 1310720 | tf_op jit(solution)/shard_map/reduce_scatter | solution.py:535
  1444.8 238.8 %reduce-scatter.19.cloned.1.call-start = ((), (), s32[]{:S(2)}) async-start(), calls=%async_computation.21 | async-start | bytes 10485760 | tf_op jit(solution)/shard_map/reduce_scatter | solution.py:535
  1445.5 396.2 %reduce-scatter.23.cloned.1.call-start = ((), (), s32[]{:S(2)}) async-start(), calls=%async_computation.23 | async-start | bytes 1966080 | tf_op jit(solution)/shard_map/reduce_scatter | solution.py:535
  1488.7 66.0 %collective-permute-start.94 = (bf16[2,4,128,256]{3,2,1,0:T(8,128)(2,1)S(1)}, bf16[2,4,128,256]{3,2,1,0:T(8,128)(2,1)}, u32[]{:S(2)}, u32[]{:S(2)}) collective-permute-start(bf16[2,4,128,256]{3,2,1,0:T(8,128)(2,1)S(1)} %get-tuple-element.152), channel_id=1, source_target_pairs={{8,0},{12,4},{9,1},{13,5},{10,2},{14,6},{11,3},{15,7},{24,16},{28,... | collective-permute-start | bytes 1572872 | tf_op jit(solution)/shard_map/ppermute | solution.py:589
  1523.8 61.6 %collective-permute-start.105 = (bf16[2,128,4096]{2,1,0:T(8,128)(2,1)}, bf16[2,128,4096]{2,1,0:T(8,128)(2,1)}, u32[]{:S(2)}, u32[]{:S(2)}) collective-permute-start(bf16[2,128,4096]{2,1,0:T(8,128)(2,1)} %maximum_bitcast_fusion.10), channel_id=1, source_target_pairs={{0,1},{1,0},{2,3},{3,2},{4,5},{5,4},{6,7},{7,6},{8,9},{9,8},{10,11... | collective-permute-start | bytes 6291464 | tf_op jit(solution)/shard_map/ppermute | solution.py:25
  1526.4 64.2 %collective-permute-start.104 = (bf16[2,128,4096]{2,1,0:T(8,128)(2,1)}, bf16[2,128,4096]{2,1,0:T(8,128)(2,1)}, u32[]{:S(2)}, u32[]{:S(2)}) collective-permute-start(bf16[2,128,4096]{2,1,0:T(8,128)(2,1)} %pad_maximum_fusion.27), channel_id=1, source_target_pairs={{0,2},{1,3},{2,0},{3,1},{4,6},{5,7},{6,4},{7,5},{8,10},{9,11},{10,... | collective-permute-start | bytes 6291464 | tf_op jit(solution)/shard_map/ppermute | solution.py:25
  1526.7 55.4 %collective-permute-start.99 = (bf16[2,128,768]{2,1,0:T(8,128)(2,1)}, bf16[2,128,768]{2,1,0:T(8,128)(2,1)}, u32[]{:S(2)}, u32[]{:S(2)}) collective-permute-start(bf16[2,128,768]{2,1,0:T(8,128)(2,1)} %get-tuple-element.331), channel_id=1, source_target_pairs={{0,1},{1,0},{2,3},{3,2},{4,5},{5,4},{6,7},{7,6},{8,9},{9,8},{10,11... | collective-permute-start | bytes 1179656 | tf_op jit(solution)/shard_map/ppermute | solution.py:25
  1602.8 80.8 %collective-permute-start.118 = (bf16[2,4,128,4096]{3,2,1,0:T(8,128)(2,1)}, bf16[2,4,128,4096]{3,2,1,0:T(8,128)(2,1)}, u32[]{:S(2)}, u32[]{:S(2)}) collective-permute-start(bf16[2,4,128,4096]{3,2,1,0:T(8,128)(2,1)} %pad_maximum_fusion.2.one), channel_id=1, source_target_pairs={{0,16},{1,17},{2,18},{3,19},{4,20},{5,21},{6,22},{7,23},{8,24},{9,... | collective-permute-start | bytes 25165832 | tf_op jit(solution)/shard_map/ppermute | solution.py:602
  1710.2 68.2 %collective-permute-start.139 = (bf16[2,128,4096]{2,1,0:T(8,128)(2,1)}, bf16[2,128,4096]{2,1,0:T(8,128)(2,1)}, u32[]{:S(2)}, u32[]{:S(2)}) collective-permute-start(bf16[2,128,4096]{2,1,0:T(8,128)(2,1)} %get-tuple-element.241), channel_id=1, source_target_pairs={{0,1},{1,0},{2,3},{3,2},{4,5},{5,4},{6,7},{7,6},{8,9},{9,8},{10,11... | collective-permute-start | bytes 6291464 | tf_op jit(solution)/shard_map/ppermute | solution.py:25
  1710.8 65.9 %collective-permute-start.47 = (bf16[2,128,2048]{2,1,0:T(8,128)(2,1)S(1)}, bf16[2,128,2048]{2,1,0:T(8,128)(2,1)S(1)}, u32[]{:S(2)}, u32[]{:S(2)}) collective-permute-start(bf16[2,128,2048]{2,1,0:T(8,128)(2,1)S(1)} %slice_bitcast_fusion.13), channel_id=1, source_target_pairs={{0,1},{1,0},{2,3},{3,2},{4,5},{5,4},{6,7},{7,6},{8,9},{9,8},{10,11... | collective-permute-start | bytes 3145736 | tf_op jit(solution)/shard_map/ppermute | solution.py:25
  1713.4 69.9 %collective-permute-start.137 = (bf16[2,128,4096]{2,1,0:T(8,128)(2,1)}, bf16[2,128,4096]{2,1,0:T(8,128)(2,1)}, u32[]{:S(2)}, u32[]{:S(2)}) collective-permute-start(bf16[2,128,4096]{2,1,0:T(8,128)(2,1)} %pad_maximum_fusion.34), channel_id=1, source_target_pairs={{0,2},{1,3},{2,0},{3,1},{4,6},{5,7},{6,4},{7,5},{8,10},{9,11},{10,... | collective-permute-start | bytes 6291464 | tf_op jit(solution)/shard_map/ppermute | solution.py:25
  1715.0 89.2 %collective-permute-start.45 = (bf16[2,128,2048]{2,1,0:T(8,128)(2,1)}, bf16[2,128,2048]{2,1,0:T(8,128)(2,1)}, u32[]{:S(2)}, u32[]{:S(2)}) collective-permute-start(bf16[2,128,2048]{2,1,0:T(8,128)(2,1)} %bitcast.134), channel_id=1, source_target_pairs={{0,2},{1,3},{2,0},{3,1},{4,6},{5,7},{6,4},{7,5},{8,10},{9,11},{10,... | collective-permute-start | bytes 3145736 | tf_op jit(solution)/shard_map/ppermute | solution.py:25
  1794.6 134.3 %collective-permute-start.140 = (bf16[2,4,128,4096]{3,2,1,0:T(8,128)(2,1)}, bf16[2,4,128,4096]{3,2,1,0:T(8,128)(2,1)}, u32[]{:S(2)}, u32[]{:S(2)}) collective-permute-start(bf16[2,4,128,4096]{3,2,1,0:T(8,128)(2,1)} %pad_maximum_fusion.3.zero), channel_id=1, source_target_pairs={{16,0},{17,1},{18,2},{19,3},{20,4},{21,5},{22,6},{23,7},{24,8},{25... | collective-permute-start | bytes 25165832 | tf_op jit(solution)/shard_map/ppermute | solution.py:640
  1856.5 54.8 %collective-permute-start.141 = (bf16[2,4,128,2048]{3,2,1,0:T(8,128)(2,1)}, bf16[2,4,128,2048]{3,2,1,0:T(8,128)(2,1)}, u32[]{:S(2)}, u32[]{:S(2)}) collective-permute-start(bf16[2,4,128,2048]{3,2,1,0:T(8,128)(2,1)} %pad_maximum_fusion.14.zero), channel_id=1, source_target_pairs={{16,0},{17,1},{18,2},{19,3},{20,4},{21,5},{22,6},{23,7},{24,8},{25... | collective-permute-start | bytes 12582920 | tf_op jit(solution)/shard_map/ppermute | solution.py:640
  (275 other events, 4681.4 us)
Sparse Core Ops, SparseCore 0:
  14.4 58.5 all-gather.4
  75.3 246.3 all-gather.6
  323.3 71.3 all-gather.8
  396.2 246.1 all-gather.10
  818.0 109.3 reduce-scatter.8
  930.3 183.0 reduce-scatter.10
  1115.8 33.1 reduce-scatter.12
  1151.3 33.9 reduce-scatter.14
  1346.5 81.9 reduce-scatter.16
  1444.9 28.8 reduce-scatter.20
  1476.8 181.3 reduce-scatter.18
  1778.5 63.1 reduce-scatter.22

commit v3 on v2

--- a/solution.py
+++ b/solution.py
@@ -75,21 +75,10 @@
     half_size = HD // 2
     frequency = rope_base ** (-(jnp.arange(half_size).astype(f32) * 2.0) / HD)
     angles = positions[..., None] * frequency
-    angles = jnp.concatenate([angles, angles], axis=-1)
-    return (jnp.cos(angles), jnp.sin(angles))
-
-
-def rotary(values, cosine_table, sine_table):
-    half_size = values.shape[-1] // 2
-    turned = jnp.concatenate([-values[..., half_size:], values[..., :half_size]], axis=-1)
-    return values * cosine_table + turned * sine_table
-
-
-def rotary_back(grad_rot, cosine_table, sine_table):
-    half_size = grad_rot.shape[-1] // 2
-    scaled = grad_rot * sine_table
-    return grad_rot * cosine_table + jnp.concatenate(
-        [scaled[..., half_size:], -scaled[..., :half_size]], axis=-1
+    cosine, sine = jnp.cos(angles), jnp.sin(angles)
+    return (
+        jnp.concatenate([cosine] * 4, axis=-1),
+        jnp.concatenate([-sine, sine] * 2, axis=-1),
     )
 
 
@@ -101,12 +90,6 @@
     return lax.dot_general(
         left, weight, (((1,), (1,)), ((), ())), preferred_element_type=f32
     )
-
-
-def rows_product(left, right):
-    return lax.dot_general(
-        left, right, (((0,), (0,)), ((), ())), preferred_element_type=f32
-    ).astype(bf16)
 
 
 def scale_of(values):
@@ -244,6 +227,103 @@
     return outs[0], outs[1:]
 
 
+def turned_pair(value):
+    lane = lax.broadcasted_iota(jnp.int32, value.shape, 1)
+    half = HD // 2
+    ahead = pltpu.roll(value, value.shape[1] - half, 1)
+    behind = pltpu.roll(value, half, 1)
+    return jnp.where(lane % HD < half, ahead, behind)
+
+
+def widened(table, width):
+    return jnp.concatenate([table] * (width // table.shape[1]), axis=1)
+
+
+def rows_of(ref):
+    return ref[0].reshape(-1, ref.shape[-1])
+
+
+def project_kernel(k_width, a_ref, weight_ref, cosine_ref, sine_ref, query_ref, keyval_ref):
+    mixed = dot(rows_of(a_ref), weight_ref[...], 1, 0)
+    width = mixed.shape[1]
+    cosine = widened(rows_of(cosine_ref), width)
+    sine = widened(rows_of(sine_ref), width)
+    rotated = mixed * cosine + turned_pair(mixed) * sine
+    lane = lax.broadcasted_iota(jnp.int32, mixed.shape, 1)
+    rotated = jnp.where(lane < width - k_width, rotated, mixed).astype(bf16)
+    q_width = query_ref.shape[-1]
+    query_ref[0] = rotated[:, :q_width].reshape(query_ref.shape[1:])
+    keyval_ref[0] = rotated[:, q_width:].reshape(keyval_ref.shape[1:])
+
+
+def project_back_kernel(k_width, grad_ref, weight_ref, cosine_ref, sine_ref, *refs):
+    parts, (joined_ref, out_ref) = refs[:-2], refs[-2:]
+    keyval = rows_of(parts[0]).astype(f32)
+    for part in parts[1:]:
+        keyval = keyval + rows_of(part).astype(f32)
+    joined = jnp.concatenate([rows_of(grad_ref), keyval], axis=1)
+    width = joined.shape[1]
+    cosine = widened(rows_of(cosine_ref), width)
+    sine = widened(rows_of(sine_ref), width)
+    rotated = joined * cosine - turned_pair(joined) * sine
+    lane = lax.broadcasted_iota(jnp.int32, joined.shape, 1)
+    rotated = jnp.where(lane < width - k_width, rotated, joined).astype(bf16)
+    joined_ref[0] = rotated.reshape(joined_ref.shape[1:])
+    out = dot(rotated, weight_ref[...], 1, 1).astype(bf16)
+    out_ref[0] = out.reshape(out_ref.shape[1:])
+
+
+def half_spec(array):
+    return pl.BlockSpec((1,) + array.shape[1:], lambda i: (i, 0, 0, 0))
+
+
+def all_spec(array):
+    return pl.BlockSpec(array.shape, lambda i: (0, 0))
+
+
+def project(a_all, weight, cosine, sine, q_width, k_width):
+    shape = a_all.shape[:3]
+    outs = [
+        jax.ShapeDtypeStruct(shape + (q_width,), bf16),
+        jax.ShapeDtypeStruct(shape + (2 * k_width,), bf16),
+    ]
+    cells = a_all.size * weight.shape[1]
+    return pl.pallas_call(
+        functools.partial(project_kernel, k_width),
+        grid=(2,),
+        in_specs=[half_spec(a_all), all_spec(weight), half_spec(cosine), half_spec(sine)],
+        out_specs=[half_spec(v) for v in outs],
+        out_shape=outs,
+        compiler_params=pltpu.CompilerParams(vmem_limit_bytes=40 << 20),
+        cost_estimate=pl.CostEstimate(
+            flops=2 * cells, bytes_accessed=10 << 20, transcendentals=0
+        ),
+        name="project",
+    )(a_all, weight, cosine, sine)
+
+
+def project_back(grad_query, parts, weight, cosine, sine, k_width):
+    shape = grad_query.shape[:3]
+    outs = [
+        jax.ShapeDtypeStruct(shape + (weight.shape[1],), bf16),
+        jax.ShapeDtypeStruct(shape + (weight.shape[0],), bf16),
+    ]
+    cells = outs[0].size * weight.shape[0]
+    return pl.pallas_call(
+        functools.partial(project_back_kernel, k_width),
+        grid=(2,),
+        in_specs=[half_spec(grad_query), all_spec(weight), half_spec(cosine), half_spec(sine)]
+        + [half_spec(v) for v in parts],
+        out_specs=[half_spec(v) for v in outs],
+        out_shape=outs,
+        compiler_params=pltpu.CompilerParams(vmem_limit_bytes=48 << 20),
+        cost_estimate=pl.CostEstimate(
+            flops=2 * cells, bytes_accessed=14 << 20, transcendentals=0
+        ),
+        name="project_back",
+    )(grad_query, weight, cosine, sine, *parts)
+
+
 def by_core(which, refs, write):
     for at, ref in enumerate(refs):
         pl.when(which == at)(functools.partial(write, ref))
@@ -261,10 +341,11 @@
 
 
 def rows_kernel(info, zero, one_sent, zero_sent, one, out_ref):
-    which = info[0] + 2 * pl.program_id(1)
+    which = info[0] + 2 * pl.program_id(0)
 
     def write(ref):
-        out_ref[...] = ref[0, 0].astype(f32)
+        for rep in range(out_ref.shape[0]):
+            out_ref[rep, 0] = ref[0, rep ^ info[1]].astype(f32)
 
     by_core(which, (zero, one_sent, zero_sent, one), write)
 
@@ -289,7 +370,7 @@
     def chosen(at):
         def where_from(*steps):
             taken = steps[-1][0] + 2 * steps[half_dim] == at
-            return tuple(jnp.where(taken, v, 0) for v in index(*steps))
+            return tuple(jnp.where(taken, v, 0) for v in index(at % 2, *steps))
 
         return where_from
 
@@ -307,14 +388,14 @@
     )(info, *four)
 
 
-def assemble_columns(info, four, offset, piece, pieces):
+def assemble_columns(info, four, offsets, piece, pieces):
     _, reps, rows, _ = four[0].shape
     return assembled(
         columns_kernel,
         (2, 2, pieces),
         0,
         (1, reps, rows, piece),
-        lambda k, sub, at, info: (sub, 0, 0, offset + at),
+        lambda layer, k, sub, at, info: (sub, 0, 0, offsets[layer] + at),
         [(rows, reps * piece)],
         lambda k, sub, at, info: (2 * k + sub, at),
         [(4 * rows, reps * piece * pieces)],
@@ -327,16 +408,16 @@
     _, reps, rows, columns = four[0].shape
     return assembled(
         rows_kernel,
-        (reps, 2, 2),
-        1,
-        (1, 1, rows, columns),
-        lambda rep, k, sub, info: (sub, rep ^ info[1], 0, 0),
-        [(rows, columns)],
-        lambda rep, k, sub, info: (4 * rep + 2 * k + sub, 0),
-        [(4 * reps * rows, columns)],
+        (2, 2),
+        0,
+        (1, reps, rows, columns),
+        lambda layer, k, sub, info: (sub, 0, 0, 0),
+        [(reps, 1, rows, columns)],
+        lambda k, sub, info: (0, 2 * k + sub, 0, 0),
+        [(reps, 4, rows, columns)],
         info,
         four,
-    )[0]
+    )[0].reshape(-1, columns)
 
 
 def assemble_proj(info, four, sizes):
@@ -346,7 +427,7 @@
         (2, 2),
         0,
         (1, reps, rows, columns),
-        lambda k, sub, info: (sub, 0, 0, 0),
+        lambda layer, k, sub, info: (sub, 0, 0, 0),
         [(rows, reps * size) for size in sizes],
         lambda k, sub, info: (2 * k + sub, 0),
         [(4 * rows, reps * size) for size in sizes],
@@ -357,14 +438,6 @@
 
 def together(*values):
     return lax.optimization_barrier(values)
-
-
-def sum_everywhere(value):
-    for axis in ("rep", "fsdp", "section"):
-        count = lax.axis_size(axis)
-        for bit in bit_list(count):
-            value = value + lax.ppermute(value, axis, [(i, i ^ bit) for i in range(count)])
-    return value
 
 
 def shards(
@@ -488,7 +561,7 @@
     cosine, sine = rope_tables((layer_z * rows + within - starts).astype(f32))
 
     def by_half(table):
-        return table.reshape(reps, 2, half, 1, HD).transpose(1, 0, 2, 3, 4)
+        return table.reshape(reps, 2, half, 2 * HD).transpose(1, 0, 2, 3)
 
     cosine, sine = by_half(cosine), by_half(sine)
 
@@ -502,13 +575,7 @@
         gain_attn, gain_ffn = gains[layer][0], gains[layer][1]
         scale_in = scale_of(layer_in)
         a_all = plane_gather((layer_in * scale_in * gain_attn).astype(bf16))
-        qkv = times(flat(a_all), qkv_all[layer])
-        query = qkv[:, :q_width].reshape(2, reps, half, -1, HD)
-        key = qkv[:, q_width : q_width + k_width].reshape(2, reps, half, -1, HD)
-        query = blocks(rotary(query, cosine, sine).astype(bf16))
-        key = blocks(rotary(key, cosine, sine).astype(bf16))
-        value = blocks(qkv[:, q_width + k_width :].astype(bf16))
-        keyval = jnp.concatenate([key, value], axis=-1)
+        query, keyval = project(a_all, qkv_all[layer], cosine, sine, q_width, k_width)
         keyvals = [keyval] + [
             back(keyval, step) for step in range(1, depth)
         ]
@@ -523,137 +590,188 @@
         kept = (layer_in, scale_in, a_all, query, keyvals, mixed, log_total)
         return out.astype(bf16), kept + (residual, scale_mid, b_all, gate, up, hidden)
 
-    def core_sum(part):
-        cube = part.reshape(depth, 2, -1, part.shape[1])
-        mine = lax.dynamic_index_in_dim(cube, core, 1, keepdims=False)
-        sent = lax.dynamic_index_in_dim(cube, 1 - core, 1, keepdims=False)
-        got = lax.ppermute(sent, "section", SWAP)
-        total = (mine.astype(f32) + got.astype(f32)).astype(bf16)
-        return total.reshape(-1, part.shape[1])
+    def core_product(left, right, extra=None):
+        size = left.shape[1] // (2 * depth)
+
+        def half_of(value, which):
+            return jnp.concatenate(
+                [
+                    lax.dynamic_slice_in_dim(value, (2 * k + which) * size, size, axis=1)
+                    for k in range(depth)
+                ],
+                axis=1,
+            )
+
+        def product(which, right):
+            found = dot(half_of(left, which), right, 0, 0)
+            if extra is None:
+                return found
+            more = half_of(extra, which).T
+            more = jnp.pad(more, ((0, 0), (0, 128 - more.shape[1])))
+            return jnp.concatenate([found, more], axis=1)
+
+        def finish(right, sent):
+            got = lax.ppermute(sent, "section", SWAP)
+            return (product(core, right) + got.astype(f32)).astype(bf16)
+
+        return product(1 - core, right).astype(bf16), finish
+
+    info = jnp.stack([core, rep]).astype(jnp.int32)
 
     def collect(total):
         return lax.psum_scatter(total, "fsdp", scatter_dimension=0, tiled=True)
 
-    def backward(layer, grad_out, kept, earlier):
+    def backward(layer, grad_out, kept, earlier, ready):
         (layer_in, scale_in, a_all, query, keyvals, mixed, log_total) = kept[:7]
         (residual, scale_mid, b_all, gate, up, hidden) = kept[7:]
         gain_attn, gain_ffn = gains[layer][0], gains[layer][1]
         last = earlier is not None
         if last:
-            old_proj, old_o, old_ffn, old_down = earlier
-            grad_out, old_ffn = together(grad_out, old_ffn)
-        gm_all = flat(plane_gather(grad_out))
-        gm_all, part_down = together(gm_all, rows_product(hidden, gm_all))
-        if last:
-            gm_all, old_ffn, old_down = together(gm_all, old_ffn, old_down)
+            old_rest, old_gate, old_up, old_down = earlier
+            tall = old_up.shape[0]
+
+            def in_one(*values):
+                return jnp.concatenate([v.reshape(tall, -1) for v in values], axis=1)
+
+            state = gather_step(gather_start(grad_out), 0)
+            *state, old_gate, old_up, old_down = together(*state, old_gate, old_up, old_down)
+            old_ffn = in_one(old_gate, old_up, old_down)
+            gm_all = flat(gather_rest(state, 1))
+            sent_down, finish = core_product(hidden, gm_all)
+            gm_all, sent_down, old_ffn = together(gm_all, sent_down, old_ffn)
             ffn_state = gather_step(gather_start(old_ffn), 0)
-            down_state = gather_step(gather_start(old_down), 0)
+        else:
+            gm_all = flat(plane_gather(grad_out))
+            sent_down, finish = core_product(hidden, gm_all)
+            gm_all, sent_down, *ready = together(gm_all, sent_down, *ready)
         grad_hidden = times_back(gm_all, down_all[layer])
         sig = jax.nn.sigmoid(gate)
         grad_gate = (grad_hidden * up * (sig * (1.0 + gate * (1.0 - sig)))).astype(bf16)
         grad_up = (grad_hidden * (gate * sig)).astype(bf16)
         grad_pre = jnp.concatenate([grad_gate, grad_up], axis=1)
-        grad_pre, part_down = together(grad_pre, core_sum(part_down))
+        part_down = finish(gm_all, sent_down)
+        if last:
+            grad_pre, *ffn_state = together(grad_pre, *ffn_state)
         own_down = collect(part_down)
-        if last:
-            grad_pre, *states = together(grad_pre, *ffn_state, *down_state)
-            ffn_state, down_state = states[:2], states[2:]
-            whole_down = gather_rest(down_state, 1)
         db = blocks(times_back(grad_pre, ffn_all[layer]).astype(bf16))
-        db, grad_pre = together(db, grad_pre)
-        if last:
-            db, whole_down, old_o, old_proj = together(db, whole_down, old_o, old_proj)
+        db, grad_gate, grad_up = together(db, grad_gate, grad_up)
         db = plane_reduce(db)
+        sent_gate, finish_gate = core_product(flat(b_all), grad_gate)
+        sent_up, finish_up = core_product(flat(b_all), grad_up)
         unit = residual * scale_mid
         grad_mid, gain_grad_ffn = norm_back(db, gain_ffn, unit, scale_mid)
         grad_mid = grad_mid + grad_out.astype(f32)
         go = grad_mid.astype(bf16)
-        go, part_ffn = together(go, core_sum(rows_product(flat(b_all), grad_pre)))
-        own_ffn = collect(part_ffn)
         go_all = flat(plane_gather(go))
+        go_all, part_gate, part_up = together(
+            go_all, finish_gate(grad_gate, sent_gate), finish_up(grad_up, sent_up)
+        )
+        own_gate, own_up = collect(part_gate), collect(part_up)
         grad_mixed = blocks(times_back(go_all, out_all[layer]).astype(bf16))
-        part_o = lax.all_to_all(rows_product(flat(mixed), go_all), "rep", 0, 0, tiled=True)
         if last:
-            tied = together(grad_mixed, old_o, old_proj, *ffn_state)
-            grad_mixed, old_o, old_proj, ffn_state = tied[0], tied[1], tied[2], tied[3:]
-            wholes = (
-                plane_gather(old_proj),
-                plane_gather(old_o),
-                gather_rest(ffn_state, 1),
-                whole_down,
+            grad_mixed, own_down, old_rest, *ffn_state = together(
+                grad_mixed, own_down, old_rest, *ffn_state
             )
+            ffn_state = gather_step(ffn_state, 1)
+            rest_state = gather_step(gather_start(old_rest), 0)
+        else:
+            grad_mixed, own_down = together(grad_mixed, own_down)
         grad_query, grad_kv = attend_back(query, keyvals, grad_mixed, log_total, bias)
-        grad_query, own_down, *grad_kv = together(grad_query, own_down, *grad_kv)
-        own_kv = grad_kv[0].astype(f32)
-        for s in range(1, depth):
-            got = lax.ppermute(grad_kv[s], "fsdp", [(i, i - s) for i in range(s, depth)])
-            own_kv = own_kv + got.astype(f32)
-        own_o = collect(core_sum(part_o))
-        grad_query = grad_query.reshape(2, reps, half, -1, HD)
-        grad_key = own_kv[..., :k_width].reshape(2, reps, half, -1, HD)
-        grad_query = rotary_back(grad_query, cosine, sine).astype(bf16)
-        grad_key = rotary_back(grad_key, cosine, sine).astype(bf16)
-        grad_value = own_kv[..., k_width:].astype(bf16)
-        grad_qkv = jnp.concatenate([flat(grad_query), flat(grad_key), flat(grad_value)], axis=1)
-        da = blocks(times_back(grad_qkv, qkv_all[layer]).astype(bf16))
-        da, grad_qkv = together(da, grad_qkv)
-        if last:
-            da, *wholes = together(da, *wholes)
-            sent = [lax.ppermute(v, "section", [(0, 1)]) for v in wholes]
-            own_down = plane_gather(own_down)
-        da = plane_reduce(da)
-        unit = layer_in * scale_in
-        grad_in, gain_grad_attn = norm_back(da, gain_attn, unit, scale_in)
-        grad_in = (grad_in + grad_mid).astype(bf16)
-        grad_in, part_proj = together(grad_in, core_sum(rows_product(flat(a_all), grad_qkv)))
-        own_proj = collect(part_proj)
-        gain_grads = jnp.stack([gain_grad_attn, gain_grad_ffn])
+        grad_query, go_all, *grad_kv = together(grad_query, go_all, *grad_kv)
+        grad_kv = [grad_kv[0]] + [
+            lax.ppermute(grad_kv[step], "fsdp", [(i, i - step) for i in range(step, depth)])
+            for step in range(1, depth)
+        ]
+        sent_o, finish = core_product(flat(mixed), go_all)
+        part_o = lax.all_to_all(finish(go_all, sent_o), "rep", 0, 0, tiled=True)
+        grad_qkv, da = project_back(grad_query, grad_kv, qkv_all[layer], cosine, sine, k_width)
+        grad_qkv = flat(grad_qkv)
+
+        def input_side(da):
+            unit = layer_in * scale_in
+            grad_in, gain_grad_attn = norm_back(da, gain_attn, unit, scale_in)
+            grad_in = (grad_in + grad_mid).astype(bf16)
+            gain_grads = jnp.stack([gain_grad_attn, gain_grad_ffn])
+            sent_proj, finish = core_product(flat(a_all), grad_qkv, gain_grads)
+            part_proj = finish(grad_qkv, sent_proj)
+            aside = part_o.reshape(part_proj.shape[0], -1)
+            return grad_in, jnp.concatenate([part_proj, aside], axis=1)
+
         if not last:
-            return grad_in, (own_proj, own_o, own_ffn, own_down), gain_grads, None
-        tied = together(grad_in, own_ffn, own_o, own_down, *sent)
-        grad_in, own_ffn, own_o, own_down, sent = tied[0], tied[1], tied[2], tied[3], tied[4:]
-        sums = (plane_gather(own_proj), plane_gather(own_o), plane_gather(own_ffn), own_down)
-        return grad_in, sums, gain_grads, list(zip(wholes, sent))
+            da, grad_qkv, part_o, own_gate = together(da, grad_qkv, part_o, own_gate)
+            grad_in, part_rest = input_side(plane_reduce(da))
+            return grad_in, (collect(part_rest), own_gate, own_up, own_down), ready
+
+        def four(zero, ones):
+            return (zero, ones[1], lax.ppermute(zero, "section", [(1, 0)]), ones[0])
+
+        def cut_out(pair, first, like):
+            size = like.size // (tall * reps)
+            part = [v[..., first : first + size].reshape(like.shape) for v in pair]
+            return part, first + size
+
+        da, *states = together(da, *ffn_state, *rest_state)
+        old_ffn = gather_rest(states[:2], 2)
+        old_rest = gather_rest(states[2:], 1)
+        da, own_gate, own_down = together(plane_reduce(da), own_gate, own_down)
+        grad_in, part_rest = input_side(da)
+        gate_state = gather_step(gather_start(own_gate), 0)
+        down_state = gather_step(gather_start(own_down), 0)
+        part_rest, own_up, *states = together(part_rest, own_up, *gate_state, *down_state)
+        own_rest = collect(part_rest)
+        zero_gate, zero_down = gather_rest(states[:2], 1), gather_rest(states[2:], 1)
+        up_state = gather_step(gather_start(own_up), 0)
+        zero_gate, zero_down, old_ffn, own_rest, *up_state = together(
+            zero_gate, zero_down, old_ffn, own_rest, *up_state
+        )
+        zero_up = gather_rest(up_state, 1)
+        zero_rest = plane_gather(own_rest)
+        old_ffn = (old_ffn, lax.ppermute(old_ffn, "section", [(0, 1)]))
+        old_rest = (old_rest, lax.ppermute(old_rest, "section", [(0, 1)]))
+        grad_gate = assemble_columns(info, four(zero_gate, old_ffn), (0, 0), ff_piece, depth)
+        old_down, _ = cut_out(old_ffn, 2 * own_up.shape[1], zero_down)
+        grad_down = assemble_rows(info, four(zero_down, old_down))
+        grad_gate, grad_down, zero_up, zero_rest, *old_rest = together(
+            grad_gate, grad_down, zero_up, zero_rest, *old_rest
+        )
+        grad_up = assemble_columns(info, four(zero_up, old_ffn), (0, depth), ff_piece, depth)
+        rest = four(zero_rest, old_rest)
+        proj_width = own_rest.shape[1] - out_rows * width // (2 * tall)
+        proj = [v[..., :proj_width] for v in rest]
+        outs = [v[..., proj_width:].reshape(2, reps, -1, width) for v in rest]
+        grad_output = assemble_rows(info, outs)
+        projections = assemble_proj(info, proj, (q_width, k_width, k_width))
+        return grad_in, proj, (*projections, grad_output, grad_gate, grad_up, grad_down)
 
     own_tokens = lax.dynamic_index_in_dim(tokens[0], core, 0, keepdims=False)
     own_cotangent = lax.dynamic_index_in_dim(cotangent[0], core, 0, keepdims=False)
     out0, kept0 = forward(0, own_tokens.astype(f32))
     out1, kept1 = forward(1, out0.astype(f32))
-    grad1, sums1, gain1, _ = backward(1, own_cotangent, kept1, None)
-    grad0, whole0, gain0, whole1 = backward(0, grad1, kept0, sums1)
 
     def swapped(zero, one):
         got = lax.ppermute(jnp.where(core == 0, one, zero), "section", SWAP)
         return jnp.where(core == 0, zero, got), jnp.where(core == 0, got, one)
 
-    outputs = jnp.stack(swapped(out0, out1))[None, None]
+    grad1, sums1, outputs = backward(1, own_cotangent, kept1, None, swapped(out0, out1))
+    grad0, proj, weight_grads = backward(0, grad1, kept0, sums1, None)
+    outputs = jnp.stack(outputs)[None, None]
     input_grads = jnp.stack(swapped(grad0, grad1))[None, None]
-
-    gain_sums = sum_everywhere(jnp.concatenate([gain0, gain1], axis=0))
-    gain_sums = gain_sums.reshape(2, 2, depth, -1)
-    gain_sums = lax.dynamic_index_in_dim(gain_sums, core, 0, keepdims=False)
-    gain_sums = lax.dynamic_index_in_dim(gain_sums, layer_z, 1, keepdims=False)
-
-    info = jnp.stack([core, rep]).astype(jnp.int32)
-
-    def four(zero, one):
-        return (zero, one[1], lax.ppermute(zero, "section", [(1, 0)]), one[0])
-
-    proj, outp, ffn, down = (four(a, b) for a, b in zip(whole0, whole1))
-    grad_gate = assemble_columns(info, ffn, 0, ff_piece, depth)
-    grad_up = assemble_columns(info, ffn, depth, ff_piece, depth)
-    grad_down = assemble_rows(info, down)
-    grad_output = assemble_rows(info, outp)
-    grad_query, grad_key, grad_value = assemble_proj(info, proj, (q_width, k_width, k_width))
+    grad_query, grad_key, grad_value, grad_output, grad_gate, grad_up, grad_down = weight_grads
+    gain_parts = [jnp.sum(v[..., qkv_width : qkv_width + 2].astype(f32), axis=1) for v in proj]
+    gain_halves = (
+        jnp.where(core == 0, gain_parts[0], gain_parts[1]),
+        jnp.where(core == 0, gain_parts[2], gain_parts[3]),
+    )
+    gain_sums = jnp.concatenate(gain_halves, axis=0).reshape(-1, 2)
     return (
         outputs,
         input_grads,
-        gain_sums[0][None],
+        gain_sums[:, 0][None],
         grad_query[None],
         grad_key[None],
         grad_value[None],
         grad_output[None],
-        gain_sums[1][None],
+        gain_sums[:, 1][None],
         grad_gate[None],
         grad_up[None],
         grad_down[None],

time: 1980 us -> 1930 us (0.975)
  other arithmetic: 253 us -> 178 us
  waiting for transfers between devices: 781 us -> 830 us
  blocking collectives: 24.5 us -> 0 us
  local copies, waits for them, and re-layouts: 189 us -> 166 us
    convert_element_type x18 -> x3, other arithmetic: 61.7 us -> 5.7 us  [the longest x2 5.07 us: finish(): return (product(core, right) + got.astype(f32)).astype(bf16)]
    ppermute x9, waiting for transfers between devices: 68.7 us -> 113 us  [back(): lax.ppermute(value, 'fsdp', [(i, i + step) for i in range(depth - step)])]
    dot_general x8 -> x20, matrix products: 81.5 us -> 122 us  [dot(): lax.dot_general(left, right, (((left_dim,), (right_dim,)), ((), ())), pre...]
    ppermute x27 -> x22, starting transfers between devices: 89.2 us -> 55.5 us  [the longest x4 25.5 us: four(): return (zero, ones[1], lax.ppermute(zero, 'section', [(1, 0)]), ones[0])]
    pallas_call x0 -> x4, Pallas kernels: none -> 26.4 us  [the longest x2 17.2 us: project_back(): pl.pallas_call(functools.partial(project_back_kernel, k_width), grid=(2,)...]
    squeeze x8 -> x0, local copies, waits for them, and re-layouts: 25.3 us -> none  [core_sum(): sent = lax.dynamic_index_in_dim(cube, 1 - core, 1, keepdims=False)]
    all_to_all x1 -> x0, blocking collectives: 24.5 us -> none  [backward(): lax.all_to_all(rows_product(flat(mixed), go_all), 'rep', 0, 0, tiled=True)]
    dot_general x8 -> x6, matrix products: 115 us -> 98.1 us  [times_back(): lax.dot_general(left, weight, (((1,), (1,)), ((), ())), preferred_element...]
  transfers between devices with their start and end apart: 157 -> 145, of which waited for: 77 -> 70; matrix products, arithmetic and copies ran while one was open for 29% -> 30% of each run, Pallas kernels for 8% -> 10%
where the time goes in v3:
time: 1930 us; the launch traced here: 1910 us
  waiting for transfers between devices  830 us (43%)
  matrix products  298 us (15%)
  starting transfers between devices  226 us (12%)
  Pallas kernels  198 us (10%)
  other arithmetic  178 us (9%)
  local copies, waits for them, and re-layouts  166 us (9%)
    ppermute x90, waiting for transfers between devices, partner(): return lax.ppermute(value, 'rep', [(i, i ^ bit) for i in range(count)])  537 us
    dot_general x20, matrix products, dot(): lax.dot_general(left, right, (((left_dim,), (right_dim,)), ((), ())), pre...  122 us
    ppermute x9, waiting for transfers between devices, back(): lax.ppermute(value, 'fsdp', [(i, i + step) for i in range(depth - step)])  113 us
    ppermute x6, waiting for transfers between devices, backward(): lax.ppermute(grad_kv[step], 'fsdp', [(i, i - step) for i in range(step, d...  106 us
    dot_general x6, matrix products, times_back(): lax.dot_general(left, weight, (((1,), (1,)), ((), ())), preferred_element...  98.1 us
    ppermute x90, starting transfers between devices, partner(): return lax.ppermute(value, 'rep', [(i, i ^ bit) for i in range(count)])  88.6 us
    dot_general x6, matrix products, times(): return jnp.dot(left, weight, preferred_element_type=f32)  77.8 us
    pallas_call x2, Pallas kernels, attend_back(): pl.pallas_call(functools.partial(attend_back_kernel, len(keyvals)), grid=...  67.8 us
  transfers between devices with their start and end apart: 145, of which 70 were waited for; matrix products, arithmetic and copies ran while one was open for 30% of the time, Pallas kernels for 10%

profile of v3, /device:TPU:1, one launch (start us, length us, event | category | flops | bytes accessed | tf_op | source)
XLA Modules:
  0.0 1912.9 jit_solution(3557557612641724506)
XLA Ops:
  75.1 17.0 collective-permute-done.11
  135.7 22.5 %collective-permute-done.19.refs_2_ = bf16[2,4,128,256]{3,2,1,0:T(8,128)(2,1)S(1)} collective-permute-done((bf16[2,4,128,256]{3,2,1,0:T(8,128)(2,1)S(1)}, bf16[2,4,128,256]{3,2,1,0:T(8,128)(2,1)S(1)}, u32[]{:S(2)}, u32[]{:S(2)}) %collective-permute-start.19) | collective-permute-done | bytes 524320 | tf_op jit(solution)/shard_map/ppermute | solution.py:471
  158.2 22.5 %collective-permute-done.20.refs_3_ = bf16[2,4,128,256]{3,2,1,0:T(8,128)(2,1)S(1)} collective-permute-done((bf16[2,4,128,256]{3,2,1,0:T(8,128)(2,1)S(1)}, bf16[2,4,128,256]{3,2,1,0:T(8,128)(2,1)S(1)}, u32[]{:S(2)}, u32[]{:S(2)}) %collective-permute-start.20) | collective-permute-done | bytes 524320 | tf_op jit(solution)/shard_map/ppermute | solution.py:471
  180.7 28.3 %attend.2 = (bf16[2,4,128,512]{3,2,1,0:T(8,128)(2,1)S(1)}, f32[4,8,256]{2,1,0:T(8,128)S(1)}) custom-call(bf16[2,4,128,512]{3,2,1,0:T(8,128)(2,1)S(1)} %get-tuple-element.112.query_ref, bf16[4,1024,256]{2,1,0:T(8,128)(2,1)} %pad_maximum_fusion.23.bias_ref, bf16[2,4,128,256]{3,2,1,0:T(8,128)(2,1)S(1)} %get-tuple-element.113.refs_0_, ...), custom_call_target="tpu_custom_call" | custom-call | flops 8589934592 | bytes 8388608 | tf_op jit(solution)/shard_map/attend/pallas_call | solution.py:195
  218.9 18.5 collective-permute-done.21
  265.0 21.0 %collective-permute-done.28 = bf16[2,128,2048]{2,1,0:T(8,128)(2,1)S(1)} collective-permute-done((bf16[2,128,2048]{2,1,0:T(8,128)(2,1)S(1)}, bf16[2,128,2048]{2,1,0:T(8,128)(2,1)S(1)}, u32[]{:S(2)}, u32[]{:S(2)}) %collective-permute-start.28) | collective-permute-done | bytes 1048608 | tf_op jit(solution)/shard_map/ppermute | solution.py:25
  288.9 32.7 %all-gather.7.cloned.1.call-done = bf16[2048,6144]{1,0:T(8,128)(2,1)} async-done(((bf16[256,6144]{1,0:T(8,128)(2,1)}), bf16[2048,6144]{1,0:T(8,128)(2,1)}) %all-gather.7.cloned.1.call-update) | async-done | bytes 25165840 | tf_op jit(solution)/shard_map/all_gather | solution.py:504
  321.6 21.9 %fusion.6 = f32[1024,4096]{1,0:T(8,128)S(1)} fusion(bf16[1024,2048]{1,0:T(8,128)(2,1)} %bitcast.648, bf16[2048,6144]{1,0:T(8,128)(2,1)} %all-gather.7.cloned.1.call-done), kind=kOutput, calls=%fused_computation.6 | convolution fusion | flops 17179869184 | bytes 37748736 | tf_op jit(solution)/shard_map/dot_general | solution.py:86
  365.9 21.4 %collective-permute-done.30 = bf16[2,128,2048]{2,1,0:T(8,128)(2,1)S(1)} collective-permute-done((bf16[2,128,2048]{2,1,0:T(8,128)(2,1)S(1)}, bf16[2,128,2048]{2,1,0:T(8,128)(2,1)S(1)}, u32[]{:S(2)}, u32[]{:S(2)}) %collective-permute-start.30) | collective-permute-done | bytes 1048608 | tf_op jit(solution)/shard_map/ppermute | solution.py:25
  477.4 21.6 %collective-permute-done.39.refs_2_ = bf16[2,4,128,256]{3,2,1,0:T(8,128)(2,1)S(1)} collective-permute-done((bf16[2,4,128,256]{3,2,1,0:T(8,128)(2,1)S(1)}, bf16[2,4,128,256]{3,2,1,0:T(8,128)(2,1)S(1)}, u32[]{:S(2)}, u32[]{:S(2)}) %collective-permute-start.39) | collective-permute-done | bytes 524320 | tf_op jit(solution)/shard_map/ppermute | solution.py:471
  499.1 22.5 %collective-permute-done.40.refs_3_ = bf16[2,4,128,256]{3,2,1,0:T(8,128)(2,1)S(1)} collective-permute-done((bf16[2,4,128,256]{3,2,1,0:T(8,128)(2,1)S(1)}, bf16[2,4,128,256]{3,2,1,0:T(8,128)(2,1)S(1)}, u32[]{:S(2)}, u32[]{:S(2)}) %collective-permute-start.40) | collective-permute-done | bytes 524320 | tf_op jit(solution)/shard_map/ppermute | solution.py:471
  521.5 28.5 %attend.3 = (bf16[2,4,128,512]{3,2,1,0:T(8,128)(2,1)S(1)}, f32[4,8,256]{2,1,0:T(8,128)S(1)}) custom-call(bf16[2,4,128,512]{3,2,1,0:T(8,128)(2,1)S(1)} %get-tuple-element.115.query_ref, bf16[4,1024,256]{2,1,0:T(8,128)(2,1)} %pad_maximum_fusion.23.bias_ref, bf16[2,4,128,256]{3,2,1,0:T(8,128)(2,1)S(1)} %get-tuple-element.116.refs_0_, ...), custom_call_target="tpu_custom_call" | custom-call | flops 8589934592 | bytes 8388608 | tf_op jit(solution)/shard_map/attend/pallas_call | solution.py:195
  616.9 21.3 %collective-permute-done = bf16[1,128,2048]{2,1,0:T(8,128)(2,1)} collective-permute-done((bf16[1,128,2048]{2,1,0:T(8,128)(2,1)}, bf16[1,128,2048]{2,1,0:T(8,128)(2,1)}, u32[]{:S(2)}, u32[]{:S(2)}) %collective-permute-start) | collective-permute-done | bytes 524320 | tf_op jit(solution)/shard_map/ppermute | solution.py:25
  667.1 21.5 %fusion.2 = f32[1024,4096]{1,0:T(8,128)S(1)} fusion(bf16[1024,2048]{1,0:T(8,128)(2,1)} %bitcast.650, bf16[2048,6144]{1,0:T(8,128)(2,1)} %all-gather.11.cloned.1.call-done), kind=kOutput, calls=%fused_computation.2 | convolution fusion | flops 17179869184 | bytes 37748736 | tf_op jit(solution)/shard_map/dot_general | solution.py:86
  739.3 18.9 collective-permute-start.53
  769.6 21.1 %multiply_convert_fusion.3 = (bf16[1024,2048]{1,0:T(8,128)(2,1)}, bf16[1024,2048]{1,0:T(8,128)(2,1)}) fusion(f32[1024,4096]{1,0:T(8,128)} %copy-done.61, bf16[1024,2048]{1,0:T(8,128)(2,1)} %bitcast.689, bf16[2048,6144]{1,0:T(8,128)(2,1)} %all-gather.11.cloned.1.call-done), kind=kOutput, calls=%fused_computation.22 | convolution fusion | flops 8617197568 | bytes 37748736 | tf_op jit(solution)/shard_map/dot_general | solution.py:90
  790.7 22.8 %fusion.30 = bf16[1024,2048]{1,0:T(8,128)(2,1)S(1)} fusion(bf16[2048,6144]{1,0:T(8,128)(2,1)} %all-gather.11.cloned.1.call-done, bf16[1024,2048]{1,0:T(8,128)(2,1)} %get-tuple-element.123, bf16[1024,2048]{1,0:T(8,128)(2,1)} %get-tuple-element.122), kind=kOutput, calls=%fused_computation.61 | convolution fusion | flops 17198743552 | bytes 29360128 | tf_op jit(solution)/shard_map/dot_general | solution.py:90
  882.3 22.1 %collective-permute-done.61 = bf16[2,128,2048]{2,1,0:T(8,128)(2,1)S(1)} collective-permute-done((bf16[2,128,2048]{2,1,0:T(8,128)(2,1)S(1)}, bf16[2,128,2048]{2,1,0:T(8,128)(2,1)S(1)}, u32[]{:S(2)}, u32[]{:S(2)}) %collective-permute-start.61) | collective-permute-done | bytes 1048608 | tf_op jit(solution)/shard_map/ppermute | solution.py:25
  936.7 27.2 %reduce-scatter.9.cloned.1.call-done = bf16[256,2048]{1,0:T(8,128)(2,1)} async-done(((bf16[1024,2048]{1,0:T(8,128)(2,1)}), bf16[256,2048]{1,0:T(8,128)(2,1)}) %reduce-scatter.9.cloned.1.call-update) | async-done | bytes 1048592 | tf_op jit(solution)/shard_map/reduce_scatter | solution.py:622
  965.1 33.8 %attend_back.2 = (f32[2,4,128,512]{3,2,1,0:T(8,128)}, bf16[2,4,128,256]{3,2,1,0:T(8,128)(2,1)S(1)}, bf16[2,4,128,256]{3,2,1,0:T(8,128)(2,1)S(1)}, bf16[2,4,128,2...) custom-call(bf16[2,4,128,512]{3,2,1,0:T(8,128)(2,1)S(1)} %copy-done.47, bf16[2,4,128,512]{3,2,1,0:T(8,128)(2,1)} %bitcast.767, ...), custom_call_target="tpu_custom_call" | custom-call | flops 21474836480 | bytes 12582912 | tf_op jit(solution)/shard_map/attend_back/pallas_call | solution.py:212
  1016.4 31.2 %collective-permute-done.65.refs_1_ = bf16[2,4,128,256]{3,2,1,0:T(8,128)(2,1)S(1)} collective-permute-done((bf16[2,4,128,256]{3,2,1,0:T(8,128)(2,1)S(1)}, bf16[2,4,128,256]{3,2,1,0:T(8,128)(2,1)S(1)}, u32[]{:S(2)}, u32[]{:S(2)}) %collective-permute-start.65) | collective-permute-done | bytes 524320 | tf_op jit(solution)/shard_map/ppermute | solution.py:682
  1047.6 40.6 %collective-permute-done.66.refs_2_ = bf16[2,4,128,256]{3,2,1,0:T(8,128)(2,1)} collective-permute-done((bf16[2,4,128,256]{3,2,1,0:T(8,128)(2,1)S(1)}, bf16[2,4,128,256]{3,2,1,0:T(8,128)(2,1)}, u32[]{:S(2)}, u32[]{:S(2)}) %collective-permute-start.66) | collective-permute-done | bytes 524320 | tf_op jit(solution)/shard_map/ppermute | solution.py:682
  1207.8 20.9 %multiply_convert_fusion.1 = (bf16[1024,2048]{1,0:T(8,128)(2,1)}, bf16[1024,2048]{1,0:T(8,128)(2,1)}) fusion(f32[1024,4096]{1,0:T(8,128)} %copy-done.60, bf16[1024,2048]{1,0:T(8,128)(2,1)} %bitcast.692, bf16[2048,6144]{1,0:T(8,128)(2,1)} %all-gather.7.cloned.1.call-done), kind=kOutput, calls=%fused_computation.17 | convolution fusion | flops 8617197568 | bytes 37748736 | tf_op jit(solution)/shard_map/dot_general | solution.py:90
  1249.7 23.0 %fusion.21 = bf16[1024,2048]{1,0:T(8,128)(2,1)S(1)} fusion(bf16[1024,4096]{1,0:T(8,128)(2,1)} %pad_maximum_fusion.1, bf16[2048,6144]{1,0:T(8,128)(2,1)} %all-gather.7.cloned.1.call-done), kind=kOutput, calls=%fused_computation.50 | convolution fusion | flops 17181966336 | bytes 29360128 | tf_op jit(solution)/shard_map/dot_general | solution.py:90
  1339.8 20.7 %collective-permute-done.86 = bf16[2,128,2048]{2,1,0:T(8,128)(2,1)S(1)} collective-permute-done((bf16[2,128,2048]{2,1,0:T(8,128)(2,1)S(1)}, bf16[2,128,2048]{2,1,0:T(8,128)(2,1)S(1)}, u32[]{:S(2)}, u32[]{:S(2)}) %collective-permute-start.86) | collective-permute-done | bytes 1048608 | tf_op jit(solution)/shard_map/ppermute | solution.py:25
  1399.2 34.0 %attend_back.3 = (f32[2,4,128,512]{3,2,1,0:T(8,128)}, bf16[2,4,128,256]{3,2,1,0:T(8,128)(2,1)S(1)}, bf16[2,4,128,256]{3,2,1,0:T(8,128)(2,1)}, bf16[2,4,128,256]{3,2,1,0:T(8,128)(2,1)}, bf16[2,4,128,256]{3,2,1,0:T(8,128)(2,1)}) custom-call(bf16[2,4,128,512]{3,2,1,0:T(8,128)(2,1)S(1)} %copy-done.45, bf16[2,4,128,512]{3,2,1,0:T(8,128)(2,1)} %bitcast.766, ...), custom_call_target="tpu_custom_call" | custom-call | flops 21474836480 | bytes 12582912 | tf_op jit(solution)/shard_map/attend_back/pallas_call | solution.py:212
  1436.6 31.1 %collective-permute-done.96 = bf16[1,128,1408]{2,1,0:T(8,128)(2,1)S(1)} collective-permute-done((bf16[1,128,1408]{2,1,0:T(8,128)(2,1)S(1)}, bf16[1,128,1408]{2,1,0:T(8,128)(2,1)S(1)}, u32[]{:S(2)}, u32[]{:S(2)}) %collective-permute-start.96) | collective-permute-done | bytes 360480 | tf_op jit(solution)/shard_map/ppermute | solution.py:25
  1475.0 34.5 %collective-permute-done.92.refs_2_ = bf16[2,4,128,256]{3,2,1,0:T(8,128)(2,1)S(1)} collective-permute-done((bf16[2,4,128,256]{3,2,1,0:T(8,128)(2,1)}, bf16[2,4,128,256]{3,2,1,0:T(8,128)(2,1)S(1)}, u32[]{:S(2)}, u32[]{:S(2)}) %collective-permute-start.92) | collective-permute-done | bytes 524320 | tf_op jit(solution)/shard_map/ppermute | solution.py:682
  1650.2 19.1 %collective-permute-done.112 = bf16[2,128,2048]{2,1,0:T(8,128)(2,1)S(1)} collective-permute-done((bf16[2,128,2048]{2,1,0:T(8,128)(2,1)}, bf16[2,128,2048]{2,1,0:T(8,128)(2,1)S(1)}, u32[]{:S(2)}, u32[]{:S(2)}) %collective-permute-start.112) | collective-permute-done | bytes 1048608 | tf_op jit(solution)/shard_map/ppermute | solution.py:25
  1670.9 20.8 %collective-permute-done.110 = bf16[2,128,2048]{2,1,0:T(8,128)(2,1)S(1)} collective-permute-done((bf16[2,128,2048]{2,1,0:T(8,128)(2,1)}, bf16[2,128,2048]{2,1,0:T(8,128)(2,1)S(1)}, u32[]{:S(2)}, u32[]{:S(2)}) %collective-permute-start.110) | collective-permute-done | bytes 1048608 | tf_op jit(solution)/shard_map/ppermute | solution.py:25
  1726.1 27.2 %collective-permute-done.122 = bf16[1,128,1408]{2,1,0:T(8,128)(2,1)S(1)} collective-permute-done((bf16[1,128,1408]{2,1,0:T(8,128)(2,1)S(1)}, bf16[1,128,1408]{2,1,0:T(8,128)(2,1)S(1)}, u32[]{:S(2)}, u32[]{:S(2)}) %collective-permute-start.122) | collective-permute-done | bytes 360480 | tf_op jit(solution)/shard_map/ppermute | solution.py:25
  1758.3 16.3 collective-permute-done.119
  (997 shorter events, 1108.5 us)
Async XLA Ops:
  7.2 88.6 %all-gather.5.cloned.1.call-start = ((), (), s32[]{:S(2)}) async-start(), calls=%async_computation.12 | async-start | bytes 5898240 | tf_op jit(solution)/shard_map/all_gather | solution.py:504
  14.3 307.3 %all-gather.7.cloned.1.call-start = ((), (), s32[]{:S(2)}) async-start(), calls=%async_computation.13 | async-start | bytes 28311552 | tf_op jit(solution)/shard_map/all_gather | solution.py:504
  34.3 383.0 %all-gather.9.cloned.1.call-start = ((), (), s32[]{:S(2)}) async-start(), calls=%async_computation.14 | async-start | bytes 5898240 | tf_op jit(solution)/shard_map/all_gather | solution.py:504
  35.1 632.0 %all-gather.11.cloned.1.call-start = ((), (), s32[]{:S(2)}) async-start(), calls=%async_computation.15 | async-start | bytes 28311552 | tf_op jit(solution)/shard_map/all_gather | solution.py:504
  100.0 111.4 %all-to-all-start = ((bf16[4,128,2048]{2,1,0:T(8,128)(2,1)}), bf16[4,128,2048]{2,1,0:T(8,128)(2,1)}, u32[]{:S(2)}, u32[]{:S(2)}) async-start(bf16[4,128,2048]{2,1,0:T(8,128)(2,1)} %all_to_all.30), calls=%async_computation | async-start | bytes 4194304 | tf_op jit(solution)/shard_map/all_to_all | solution.py:542
  115.5 65.1 %collective-permute-start.20 = (bf16[2,4,128,256]{3,2,1,0:T(8,128)(2,1)S(1)}, bf16[2,4,128,256]{3,2,1,0:T(8,128)(2,1)S(1)}, u32[]{:S(2)}, u32[]{:S(2)}) collective-permute-start(bf16[2,4,128,256]{3,2,1,0:T(8,128)(2,1)S(1)} %get-tuple-element.113.refs_0_), channel_id=1, source_target_pairs={{0,12},{1,13},{2,14},{3,15},{16,28},{17,29},{18,30},{19,31}} | collective-permute-start | bytes 1572872 | tf_op jit(solution)/shard_map/ppermute | solution.py:471
  421.6 132.6 %all-to-all-start.1 = ((bf16[4,128,2048]{2,1,0:T(8,128)(2,1)}), bf16[4,128,2048]{2,1,0:T(8,128)(2,1)}, u32[]{:S(2)}, u32[]{:S(2)}) async-start(bf16[4,128,2048]{2,1,0:T(8,128)(2,1)} %all_to_all.33), calls=%async_computation.1 | async-start | bytes 4194304 | tf_op jit(solution)/shard_map/all_to_all | solution.py:542
  426.1 537.7 %reduce-scatter.9.cloned.1.call-start = ((), (), s32[]{:S(2)}) async-start(), calls=%async_computation.16 | async-start | bytes 5242880 | tf_op jit(solution)/shard_map/reduce_scatter | solution.py:622
  640.4 71.8 %collective-permute-start.1 = (bf16[2,128,2048]{2,1,0:T(8,128)(2,1)}, bf16[2,128,2048]{2,1,0:T(8,128)(2,1)}, u32[]{:S(2)}, u32[]{:S(2)}) collective-permute-start(bf16[2,128,2048]{2,1,0:T(8,128)(2,1)} %pad_maximum_fusion.43), channel_id=1, source_target_pairs={{0,2},{1,3},{2,0},{3,1},{4,6},{5,7},{6,4},{7,5},{8,10},{9,11},{10,... | collective-permute-start | bytes 3145736 | tf_op jit(solution)/shard_map/ppermute | solution.py:25
  768.2 74.4 %collective-permute-start.64 = (bf16[1024,2048]{1,0:T(8,128)(2,1)}, bf16[1024,2048]{1,0:T(8,128)(2,1)}, u32[]{:S(2)}, u32[]{:S(2)}) collective-permute-start(bf16[1024,2048]{1,0:T(8,128)(2,1)} %convolution_convert_fusion.7), channel_id=1, source_target_pairs={{0,16},{16,0},{1,17},{17,1},{2,18},{18,2},{3,19},{19,3},{4,20},{20... | collective-permute-start | bytes 12582920 | tf_op jit(solution)/shard_map/ppermute | solution.py:614
  823.0 84.8 %collective-permute-start.63 = (bf16[1024,2048]{1,0:T(8,128)(2,1)}, bf16[1024,2048]{1,0:T(8,128)(2,1)}, u32[]{:S(2)}, u32[]{:S(2)}) collective-permute-start(bf16[1024,2048]{1,0:T(8,128)(2,1)} %convolution_convert_fusion.5), channel_id=1, source_target_pairs={{0,16},{16,0},{1,17},{17,1},{2,18},{18,2},{3,19},{19,3},{4,20},{20... | collective-permute-start | bytes 12582920 | tf_op jit(solution)/shard_map/ppermute | solution.py:614
  851.9 247.2 %reduce-scatter.11.cloned.1.call-start = ((), (), s32[]{:S(2)}) async-start(), calls=%async_computation.17 | async-start | bytes 5242880 | tf_op jit(solution)/shard_map/reduce_scatter | solution.py:622
  927.5 232.6 %reduce-scatter.13.cloned.1.call-start = ((), (), s32[]{:S(2)}) async-start(), calls=%async_computation.18 | async-start | bytes 5242880 | tf_op jit(solution)/shard_map/reduce_scatter | solution.py:622
  1004.4 83.9 %collective-permute-start.66 = (bf16[2,4,128,256]{3,2,1,0:T(8,128)(2,1)S(1)}, bf16[2,4,128,256]{3,2,1,0:T(8,128)(2,1)}, u32[]{:S(2)}, u32[]{:S(2)}) collective-permute-start(bf16[2,4,128,256]{3,2,1,0:T(8,128)(2,1)S(1)} %copy-done.37), channel_id=1, source_target_pairs={{8,0},{12,4},{9,1},{13,5},{10,2},{14,6},{11,3},{15,7},{24,16},{28,... | collective-permute-start | bytes 1572872 | tf_op jit(solution)/shard_map/ppermute | solution.py:682
  1005.7 82.6 %collective-permute-start.67 = (bf16[2,4,128,256]{3,2,1,0:T(8,128)(2,1)S(1)}, bf16[2,4,128,256]{3,2,1,0:T(8,128)(2,1)}, u32[]{:S(2)}, u32[]{:S(2)}) collective-permute-start(bf16[2,4,128,256]{3,2,1,0:T(8,128)(2,1)S(1)} %copy-done.35), channel_id=1, source_target_pairs={{12,0},{13,1},{14,2},{15,3},{28,16},{29,17},{30,18},{31,19}} | collective-permute-start | bytes 1572872 | tf_op jit(solution)/shard_map/ppermute | solution.py:682
  1012.1 86.9 %all-to-all-start.2 = ((bf16[4,64,2048]{2,1,0:T(8,128)(2,1)}), bf16[4,64,2048]{2,1,0:T(8,128)(2,1)}, u32[]{:S(2)}, u32[]{:S(2)}) async-start(bf16[4,64,2048]{2,1,0:T(8,128)(2,1)} %bitcast.716), calls=%async_computation.3 | async-start | bytes 2097152 | tf_op jit(solution)/shard_map/all_to_all | solution.py:686
  1016.4 376.7 %reduce-scatter.17.cloned.1.call-start = ((), (), s32[]{:S(2)}) async-start(), calls=%async_computation.20 | async-start | bytes 3604480 | tf_op jit(solution)/shard_map/reduce_scatter | solution.py:622
  1163.5 73.1 %collective-permute-start.90 = (bf16[1024,896]{1,0:T(8,128)(2,1)}, bf16[1024,896]{1,0:T(8,128)(2,1)}, u32[]{:S(2)}, u32[]{:S(2)}) collective-permute-start(bf16[1024,896]{1,0:T(8,128)(2,1)} %fusion.138), channel_id=1, source_target_pairs={{0,16},{16,0},{1,17},{17,1},{2,18},{18,2},{3,19},{19,3},{4,20},{20... | collective-permute-start | bytes 5505032 | tf_op jit(solution)/shard_map/ppermute | solution.py:614
  1202.4 99.2 %collective-permute-start.89 = (bf16[1024,2048]{1,0:T(8,128)(2,1)}, bf16[1024,2048]{1,0:T(8,128)(2,1)}, u32[]{:S(2)}, u32[]{:S(2)}) collective-permute-start(bf16[1024,2048]{1,0:T(8,128)(2,1)} %convolution_convert_fusion.4), channel_id=1, source_target_pairs={{0,16},{16,0},{1,17},{17,1},{2,18},{18,2},{3,19},{19,3},{4,20},{20... | collective-permute-start | bytes 12582920 | tf_op jit(solution)/shard_map/ppermute | solution.py:614
  1241.5 151.6 %reduce-scatter.15.cloned.1.call-start = ((), (), s32[]{:S(2)}) async-start(), calls=%async_computation.19 | async-start | bytes 5242880 | tf_op jit(solution)/shard_map/reduce_scatter | solution.py:622
  1282.2 81.6 %collective-permute-start.88 = (bf16[1024,2048]{1,0:T(8,128)(2,1)}, bf16[1024,2048]{1,0:T(8,128)(2,1)}, u32[]{:S(2)}, u32[]{:S(2)}) collective-permute-start(bf16[1024,2048]{1,0:T(8,128)(2,1)} %convolution_convert_fusion.2), channel_id=1, source_target_pairs={{0,16},{16,0},{1,17},{17,1},{2,18},{18,2},{3,19},{19,3},{4,20},{20... | collective-permute-start | bytes 12582920 | tf_op jit(solution)/shard_map/ppermute | solution.py:614
  1310.3 267.4 %reduce-scatter.19.cloned.1.call-start = ((), (), s32[]{:S(2)}) async-start(), calls=%async_computation.21 | async-start | bytes 5242880 | tf_op jit(solution)/shard_map/reduce_scatter | solution.py:622
  1383.5 249.1 %reduce-scatter.21.cloned.1.call-start = ((), (), s32[]{:S(2)}) async-start(), calls=%async_computation.22 | async-start | bytes 5242880 | tf_op jit(solution)/shard_map/reduce_scatter | solution.py:622
  1393.1 125.0 %collective-permute-start.95 = (bf16[2,128,6144]{2,1,0:T(8,128)(2,1)}, bf16[2,128,6144]{2,1,0:T(8,128)(2,1)}, u32[]{:S(2)}, u32[]{:S(2)}) collective-permute-start(bf16[2,128,6144]{2,1,0:T(8,128)(2,1)} %maximum_bitcast_fusion), channel_id=1, source_target_pairs={{0,1},{1,0},{2,3},{3,2},{4,5},{5,4},{6,7},{7,6},{8,9},{9,8},{10,11... | collective-permute-start | bytes 9437192 | tf_op jit(solution)/shard_map/ppermute | solution.py:25
  1396.9 70.8 %collective-permute-start.96 = (bf16[1,128,1408]{2,1,0:T(8,128)(2,1)S(1)}, bf16[1,128,1408]{2,1,0:T(8,128)(2,1)S(1)}, u32[]{:S(2)}, u32[]{:S(2)}) collective-permute-start(bf16[1,128,1408]{2,1,0:T(8,128)(2,1)S(1)} %get-tuple-element.401), channel_id=1, source_target_pairs={{0,1},{1,0},{2,3},{3,2},{4,5},{5,4},{6,7},{7,6},{8,9},{9,8},{10,11... | collective-permute-start | bytes 1081352 | tf_op jit(solution)/shard_map/ppermute | solution.py:25
  1397.6 126.7 %collective-permute-start.94 = (bf16[2,128,6144]{2,1,0:T(8,128)(2,1)}, bf16[2,128,6144]{2,1,0:T(8,128)(2,1)}, u32[]{:S(2)}, u32[]{:S(2)}) collective-permute-start(bf16[2,128,6144]{2,1,0:T(8,128)(2,1)} %pad_maximum_fusion.16), channel_id=1, source_target_pairs={{0,2},{1,3},{2,0},{3,1},{4,6},{5,7},{6,4},{7,5},{8,10},{9,11},{10,... | collective-permute-start | bytes 9437192 | tf_op jit(solution)/shard_map/ppermute | solution.py:25
  1435.3 74.3 %collective-permute-start.92 = (bf16[2,4,128,256]{3,2,1,0:T(8,128)(2,1)}, bf16[2,4,128,256]{3,2,1,0:T(8,128)(2,1)S(1)}, u32[]{:S(2)}, u32[]{:S(2)}) collective-permute-start(bf16[2,4,128,256]{3,2,1,0:T(8,128)(2,1)} %get-tuple-element.173), channel_id=1, source_target_pairs={{8,0},{12,4},{9,1},{13,5},{10,2},{14,6},{11,3},{15,7},{24,16},{28,... | collective-permute-start | bytes 1572872 | tf_op jit(solution)/shard_map/ppermute | solution.py:682
  1568.3 132.6 %reduce-scatter.23.cloned.1.call-start = ((), (), s32[]{:S(2)}) async-start(), calls=%async_computation.23 | async-start | bytes 3604480 | tf_op jit(solution)/shard_map/reduce_scatter | solution.py:622
  1700.9 103.0 %collective-permute-start.115 = (bf16[2,4,128,6144]{3,2,1,0:T(8,128)(2,1)}, bf16[2,4,128,6144]{3,2,1,0:T(8,128)(2,1)}, u32[]{:S(2)}, u32[]{:S(2)}) collective-permute-start(bf16[2,4,128,6144]{3,2,1,0:T(8,128)(2,1)} %pad_maximum_fusion.one), channel_id=1, source_target_pairs={{0,16},{1,17},{2,18},{3,19},{4,20},{5,21},{6,22},{7,23},{8,24},{9,... | collective-permute-start | bytes 37748744 | tf_op jit(solution)/shard_map/ppermute | solution.py:729
  1705.9 100.9 %collective-permute-start.116 = (bf16[2,4,128,2048]{3,2,1,0:T(8,128)(2,1)}, bf16[2,4,128,2048]{3,2,1,0:T(8,128)(2,1)S(1)}, u32[]{:S(2)}, u32[]{:S(2)}) collective-permute-start(bf16[2,4,128,2048]{3,2,1,0:T(8,128)(2,1)} %pad_maximum_fusion.12.zero), channel_id=1, source_target_pairs={{16,0},{17,1},{18,2},{19,3},{20,4},{21,5},{22,6},{23,7},{24,8},{25... | collective-permute-start | bytes 12582920 | tf_op jit(solution)/shard_map/ppermute | solution.py:706
  1715.7 106.3 %collective-permute-start.117 = (bf16[2,4,128,2048]{3,2,1,0:T(8,128)(2,1)}, bf16[2,4,128,2048]{3,2,1,0:T(8,128)(2,1)S(1)}, u32[]{:S(2)}, u32[]{:S(2)}) collective-permute-start(bf16[2,4,128,2048]{3,2,1,0:T(8,128)(2,1)} %pad_maximum_fusion.13.zero), channel_id=1, source_target_pairs={{16,0},{17,1},{18,2},{19,3},{20,4},{21,5},{22,6},{23,7},{24,8},{25... | collective-permute-start | bytes 12582920 | tf_op jit(solution)/shard_map/ppermute | solution.py:706
  1756.7 75.4 %collective-permute-start.126 = (bf16[2,4,128,1408]{3,2,1,0:T(8,128)(2,1)}, bf16[2,4,128,1408]{3,2,1,0:T(8,128)(2,1)}, u32[]{:S(2)}, u32[]{:S(2)}) collective-permute-start(bf16[2,4,128,1408]{3,2,1,0:T(8,128)(2,1)} %pad_maximum_fusion.20), channel_id=1, source_target_pairs={{0,16},{1,17},{2,18},{3,19},{4,20},{5,21},{6,22},{7,23},{8,24},{9,... | collective-permute-start | bytes 8650760 | tf_op jit(solution)/shard_map/ppermute | solution.py:730
  (305 other events, 5178.6 us)
Sparse Core Ops, SparseCore 0:
  14.4 58.6 all-gather.4
  75.3 246.2 all-gather.6
  323.3 71.3 all-gather.8
  396.8 246.1 all-gather.10
  852.0 111.8 reduce-scatter.8
  966.1 99.4 reduce-scatter.10
  1067.8 88.9 reduce-scatter.12
  1241.6 52.5 reduce-scatter.16
  1310.4 75.6 reduce-scatter.14
  1388.3 100.1 reduce-scatter.18
  1490.9 89.0 reduce-scatter.20
  1632.8 53.6 reduce-scatter.22

commit v4 on v3

--- a/solution.py
+++ b/solution.py
@@ -48,10 +48,14 @@
     return first, second
 
 
-def gather_rest(state, at):
+def gather_pair(state, at):
     for step in range(at, len(bit_list(lax.axis_size("rep")))):
         state = gather_step(state, step)
-    return jnp.stack(state)
+    return list(state)
+
+
+def gather_rest(state, at):
+    return jnp.stack(gather_pair(state, at))
 
 
 def plane_gather(own):
@@ -324,52 +328,60 @@
     )(grad_query, weight, cosine, sine, *parts)
 
 
-def by_core(which, refs, write):
+def by_place(info, refs, write):
+    which = info[0] + 2 * pl.program_id(0) + 4 * pl.program_id(1)
     for at, ref in enumerate(refs):
         pl.when(which == at)(functools.partial(write, ref))
 
 
-def columns_kernel(info, zero, one_sent, zero_sent, one, out_ref):
-    which = info[0] + 2 * pl.program_id(0)
-    reps, _, piece = zero.shape[1:]
+def columns_kernel(piece, info, *refs):
+    out_ref = refs[8]
+    reps, _, taken = refs[0].shape
+
+    def write(ref):
+        for at in range(taken // piece):
+            for rep in range(reps):
+                start = (at * reps + rep) * piece
+                found = ref[rep ^ info[1], :, at * piece : (at + 1) * piece]
+                out_ref[:, start : start + piece] = found.astype(f32)
+
+    by_place(info, refs[:8], write)
+
+
+def rows_kernel(info, *refs):
+    out_ref = refs[8]
+
+    def write(ref):
+        for rep in range(out_ref.shape[0]):
+            out_ref[rep, 0] = ref[rep ^ info[1]].astype(f32)
+
+    by_place(info, refs[:8], write)
+
+
+def rest_kernel(proj_width, info, *refs):
+    outs, output_ref = refs[8:11], refs[11]
+    reps, rows, width = refs[0].shape
+    height, piece = output_ref.shape[2], width - proj_width
 
     def write(ref):
         for rep in range(reps):
-            out_ref[:, rep * piece : (rep + 1) * piece] = ref[0, rep ^ info[1]].astype(f32)
-
-    by_core(which, (zero, one_sent, zero_sent, one), write)
-
-
-def rows_kernel(info, zero, one_sent, zero_sent, one, out_ref):
-    which = info[0] + 2 * pl.program_id(0)
-
-    def write(ref):
-        for rep in range(out_ref.shape[0]):
-            out_ref[rep, 0] = ref[0, rep ^ info[1]].astype(f32)
-
-    by_core(which, (zero, one_sent, zero_sent, one), write)
-
-
-def proj_kernel(info, zero, one_sent, zero_sent, one, query_ref, key_ref, value_ref):
-    which = info[0] + 2 * pl.program_id(0)
-    reps = zero.shape[1]
-
-    def write(ref):
-        for rep in range(reps):
-            block = ref[0, rep ^ info[1]].astype(f32)
+            block = ref[rep ^ info[1]].astype(f32)
             start = 0
-            for out_ref in (query_ref, key_ref, value_ref):
+            for out_ref in outs:
                 size = out_ref.shape[1] // reps
                 out_ref[:, rep * size : (rep + 1) * size] = block[:, start : start + size]
                 start += size
-
-    by_core(which, (zero, one_sent, zero_sent, one), write)
-
-
-def assembled(kernel, grid, half_dim, block, index, out_blocks, out_index, out_shapes, info, four):
+            for at in range(rows // height):
+                part = block[at * height : (at + 1) * height, proj_width:]
+                output_ref[rep, 0, :, at * piece : (at + 1) * piece] = part
+
+    by_place(info, refs[:8], write)
+
+
+def assembled(kernel, grid, block, index, out_blocks, out_index, out_shapes, info, eight):
     def chosen(at):
         def where_from(*steps):
-            taken = steps[-1][0] + 2 * steps[half_dim] == at
+            taken = steps[-1][0] + 2 * steps[0] + 4 * steps[1] == at
             return tuple(jnp.where(taken, v, 0) for v in index(at % 2, *steps))
 
         return where_from
@@ -379,61 +391,61 @@
         grid_spec=pltpu.PrefetchScalarGridSpec(
             num_scalar_prefetch=1,
             grid=grid,
-            in_specs=[pl.BlockSpec(block, chosen(at)) for at in range(4)],
-            out_specs=[pl.BlockSpec(b, out_index) for b in out_blocks],
+            in_specs=[pl.BlockSpec(block, chosen(at)) for at in range(8)],
+            out_specs=[pl.BlockSpec(b, f) for b, f in zip(out_blocks, out_index)],
         ),
         out_shape=[jax.ShapeDtypeStruct(v, f32) for v in out_shapes],
-        compiler_params=pltpu.CompilerParams(vmem_limit_bytes=40 << 20),
-        name=kernel.__name__,
-    )(info, *four)
-
-
-def assemble_columns(info, four, offsets, piece, pieces):
-    _, reps, rows, _ = four[0].shape
+        compiler_params=pltpu.CompilerParams(vmem_limit_bytes=56 << 20),
+        name="assemble",
+    )(info, *eight)
+
+
+def assemble_columns(info, eight, offsets, piece, pieces):
+    reps, rows, _ = eight[0].shape
+    step = 2 if pieces % 2 == 0 else 1
     return assembled(
-        columns_kernel,
-        (2, 2, pieces),
-        0,
-        (1, reps, rows, piece),
-        lambda layer, k, sub, at, info: (sub, 0, 0, offsets[layer] + at),
-        [(rows, reps * piece)],
-        lambda k, sub, at, info: (2 * k + sub, at),
+        functools.partial(columns_kernel, piece),
+        (2, 2, pieces // step),
+        (reps, rows, step * piece),
+        lambda layer, k, sub, at, info: (0, 0, offsets[layer] // step + at),
+        [(rows, step * reps * piece)],
+        [lambda k, sub, at, info: (2 * k + sub, at)],
         [(4 * rows, reps * piece * pieces)],
         info,
-        four,
+        eight,
     )[0]
 
 
-def assemble_rows(info, four):
-    _, reps, rows, columns = four[0].shape
+def assemble_rows(info, eight):
+    reps, rows, columns = eight[0].shape
     return assembled(
         rows_kernel,
         (2, 2),
-        0,
-        (1, reps, rows, columns),
-        lambda layer, k, sub, info: (sub, 0, 0, 0),
+        (reps, rows, columns),
+        lambda layer, k, sub, info: (0, 0, 0),
         [(reps, 1, rows, columns)],
-        lambda k, sub, info: (0, 2 * k + sub, 0, 0),
+        [lambda k, sub, info: (0, 2 * k + sub, 0, 0)],
         [(reps, 4, rows, columns)],
         info,
-        four,
+        eight,
     )[0].reshape(-1, columns)
 
 
-def assemble_proj(info, four, sizes):
-    _, reps, rows, columns = four[0].shape
-    return assembled(
-        proj_kernel,
+def assemble_rest(info, eight, sizes, proj_width, height, width):
+    reps, rows, columns = eight[0].shape
+    outs = assembled(
+        functools.partial(rest_kernel, proj_width),
         (2, 2),
-        0,
-        (1, reps, rows, columns),
-        lambda layer, k, sub, info: (sub, 0, 0, 0),
-        [(rows, reps * size) for size in sizes],
-        lambda k, sub, info: (2 * k + sub, 0),
-        [(4 * rows, reps * size) for size in sizes],
+        (reps, rows, columns),
+        lambda layer, k, sub, info: (0, 0, 0),
+        [(rows, reps * size) for size in sizes] + [(reps, 1, height, width // 2)],
+        [lambda k, sub, info: (2 * k + sub, 0)] * len(sizes)
+        + [lambda k, sub, info: (0, k, 0, sub)],
+        [(4 * rows, reps * size) for size in sizes] + [(reps, 2, height, width)],
         info,
-        four,
+        eight,
     )
+    return (*outs[:-1], outs[-1].reshape(-1, width))
 
 
 def together(*values):
@@ -630,12 +642,9 @@
             old_rest, old_gate, old_up, old_down = earlier
             tall = old_up.shape[0]
 
-            def in_one(*values):
-                return jnp.concatenate([v.reshape(tall, -1) for v in values], axis=1)
-
             state = gather_step(gather_start(grad_out), 0)
-            *state, old_gate, old_up, old_down = together(*state, old_gate, old_up, old_down)
-            old_ffn = in_one(old_gate, old_up, old_down)
+            *state, old_gate, old_up = together(*state, old_gate, old_up)
+            old_ffn = jnp.concatenate([old_gate, old_up], axis=1)
             gm_all = flat(gather_rest(state, 1))
             sent_down, finish = core_product(hidden, gm_all)
             gm_all, sent_down, old_ffn = together(gm_all, sent_down, old_ffn)
@@ -676,6 +685,7 @@
             rest_state = gather_step(gather_start(old_rest), 0)
         else:
             grad_mixed, own_down = together(grad_mixed, own_down)
+        own_down = gather_pair(gather_start(own_down), 0)
         grad_query, grad_kv = attend_back(query, keyvals, grad_mixed, log_total, bias)
         grad_query, go_all, *grad_kv = together(grad_query, go_all, *grad_kv)
         grad_kv = [grad_kv[0]] + [
@@ -694,54 +704,69 @@
             gain_grads = jnp.stack([gain_grad_attn, gain_grad_ffn])
             sent_proj, finish = core_product(flat(a_all), grad_qkv, gain_grads)
             part_proj = finish(grad_qkv, sent_proj)
-            aside = part_o.reshape(part_proj.shape[0], -1)
+            pieces = part_proj.shape[0] // part_o.shape[0]
+            aside = part_o.reshape(depth, -1, pieces, width // pieces).transpose(0, 2, 1, 3)
+            aside = aside.reshape(part_proj.shape[0], -1)
             return grad_in, jnp.concatenate([part_proj, aside], axis=1)
 
         if not last:
-            da, grad_qkv, part_o, own_gate = together(da, grad_qkv, part_o, own_gate)
+            da, grad_qkv, part_o, own_gate, *own_down = together(
+                da, grad_qkv, part_o, own_gate, *own_down
+            )
             grad_in, part_rest = input_side(plane_reduce(da))
             return grad_in, (collect(part_rest), own_gate, own_up, own_down), ready
 
-        def four(zero, ones):
-            return (zero, ones[1], lax.ppermute(zero, "section", [(1, 0)]), ones[0])
-
-        def cut_out(pair, first, like):
-            size = like.size // (tall * reps)
-            part = [v[..., first : first + size].reshape(like.shape) for v in pair]
-            return part, first + size
-
-        da, *states = together(da, *ffn_state, *rest_state)
-        old_ffn = gather_rest(states[:2], 2)
-        old_rest = gather_rest(states[2:], 1)
-        da, own_gate, own_down = together(plane_reduce(da), own_gate, own_down)
+        def send(pair):
+            return [lax.ppermute(v, "section", [(0, 1)]) for v in pair]
+
+        def eight(zero, one, one_sent):
+            found = []
+            for sub in range(2):
+                got = lax.ppermute(zero[sub], "section", [(1, 0)])
+                found += [zero[sub], one_sent[sub], got, one[sub]]
+            return found
+
+        da, *states = together(da, *own_down, *ffn_state, *rest_state)
+        zero_down = states[:2]
+        old_ffn, old_rest = gather_pair(states[2:4], 2), gather_pair(states[4:], 1)
+        olds_sent = send(old_ffn) + send(old_down)
+        da, own_gate = together(plane_reduce(da), own_gate)
         grad_in, part_rest = input_side(da)
         gate_state = gather_step(gather_start(own_gate), 0)
-        down_state = gather_step(gather_start(own_down), 0)
-        part_rest, own_up, *states = together(part_rest, own_up, *gate_state, *down_state)
+        tied = together(part_rest, own_up, *gate_state, *olds_sent, *old_rest)
+        part_rest, own_up = tied[:2]
+        gate_state, olds_sent, old_rest = tied[2:4], tied[4:8], tied[8:]
+        ffn_sent, down_sent = olds_sent[:2], olds_sent[2:]
         own_rest = collect(part_rest)
-        zero_gate, zero_down = gather_rest(states[:2], 1), gather_rest(states[2:], 1)
+        rest_sent = send(old_rest)
+        zero_gate = gather_pair(gate_state, 1)
         up_state = gather_step(gather_start(own_up), 0)
-        zero_gate, zero_down, old_ffn, own_rest, *up_state = together(
-            zero_gate, zero_down, old_ffn, own_rest, *up_state
+        own_rest, *tied = together(own_rest, *zero_gate, *up_state, *rest_sent)
+        zero_gate, up_state, rest_sent = tied[:2], tied[2:4], tied[4:]
+        zero_up, zero_rest = gather_pair(up_state, 1), gather_pair(gather_start(own_rest), 0)
+        places = eight(zero_gate, old_ffn, ffn_sent)
+        grad_gate = assemble_columns(info, places, (0, 0), ff_piece, depth)
+        grad_down = assemble_rows(info, eight(zero_down, old_down, down_sent))
+        grad_gate, grad_down, *tied = together(grad_gate, grad_down, *zero_up, *zero_rest)
+        zero_up, zero_rest = tied[:2], tied[2:]
+        places = eight(zero_up, old_ffn, ffn_sent)
+        grad_up = assemble_columns(info, places, (0, depth), ff_piece, depth)
+        height = out_rows // 2
+        proj_width = own_rest.shape[1] - height * width // tall
+        places = eight(zero_rest, old_rest, rest_sent)
+        sizes = (q_width, k_width, k_width)
+        rest = assemble_rest(info, places, sizes, proj_width, height, width)
+        gain_parts = [
+            jnp.sum(v[..., qkv_width : qkv_width + 2].astype(f32), axis=0) for v in places
+        ]
+        gain_sums = jnp.concatenate(
+            [
+                jnp.where(core == 0, gain_parts[at], gain_parts[at + 1])
+                for at in (0, 4, 2, 6)
+            ],
+            axis=0,
         )
-        zero_up = gather_rest(up_state, 1)
-        zero_rest = plane_gather(own_rest)
-        old_ffn = (old_ffn, lax.ppermute(old_ffn, "section", [(0, 1)]))
-        old_rest = (old_rest, lax.ppermute(old_rest, "section", [(0, 1)]))
-        grad_gate = assemble_columns(info, four(zero_gate, old_ffn), (0, 0), ff_piece, depth)
-        old_down, _ = cut_out(old_ffn, 2 * own_up.shape[1], zero_down)
-        grad_down = assemble_rows(info, four(zero_down, old_down))
-        grad_gate, grad_down, zero_up, zero_rest, *old_rest = together(
-            grad_gate, grad_down, zero_up, zero_rest, *old_rest
-        )
-        grad_up = assemble_columns(info, four(zero_up, old_ffn), (0, depth), ff_piece, depth)
-        rest = four(zero_rest, old_rest)
-        proj_width = own_rest.shape[1] - out_rows * width // (2 * tall)
-        proj = [v[..., :proj_width] for v in rest]
-        outs = [v[..., proj_width:].reshape(2, reps, -1, width) for v in rest]
-        grad_output = assemble_rows(info, outs)
-        projections = assemble_proj(info, proj, (q_width, k_width, k_width))
-        return grad_in, proj, (*projections, grad_output, grad_gate, grad_up, grad_down)
+        return grad_in, gain_sums, (*rest, grad_gate, grad_up, grad_down)
 
     own_tokens = lax.dynamic_index_in_dim(tokens[0], core, 0, keepdims=False)
     own_cotangent = lax.dynamic_index_in_dim(cotangent[0], core, 0, keepdims=False)
@@ -753,16 +778,10 @@
         return jnp.where(core == 0, zero, got), jnp.where(core == 0, got, one)
 
     grad1, sums1, outputs = backward(1, own_cotangent, kept1, None, swapped(out0, out1))
-    grad0, proj, weight_grads = backward(0, grad1, kept0, sums1, None)
+    grad0, gain_sums, weight_grads = backward(0, grad1, kept0, sums1, None)
     outputs = jnp.stack(outputs)[None, None]
     input_grads = jnp.stack(swapped(grad0, grad1))[None, None]
     grad_query, grad_key, grad_value, grad_output, grad_gate, grad_up, grad_down = weight_grads
-    gain_parts = [jnp.sum(v[..., qkv_width : qkv_width + 2].astype(f32), axis=1) for v in proj]
-    gain_halves = (
-        jnp.where(core == 0, gain_parts[0], gain_parts[1]),
-        jnp.where(core == 0, gain_parts[2], gain_parts[3]),
-    )
-    gain_sums = jnp.concatenate(gain_halves, axis=0).reshape(-1, 2)
     return (
         outputs,
         input_grads,

time: 1930 us -> 1870 us (0.969)
  waiting for transfers between devices: 830 us -> 788 us
  local copies, waits for them, and re-layouts: 166 us -> 143 us
    ppermute x90 -> x94, waiting for transfers between devices: 537 us -> 457 us  [partner(): return lax.ppermute(value, 'rep', [(i, i ^ bit) for i in range(count)])]
    ppermute x6, waiting for transfers between devices: 106 us -> 136 us  [backward(): lax.ppermute(grad_kv[step], 'fsdp', [(i, i - step) for i in range(step, d...]
    slice x10 -> x0, local copies, waits for them, and re-layouts: 26 us -> none  [the longest x4 9.22 us: backward(): proj = [v[..., :proj_width] for v in rest]]
    another operation x29 -> x18, other arithmetic: 45.5 us -> 20.2 us  [the longest x16 20.1 us: gather_rest(): return jnp.stack(gather_pair(state, at))]
    ppermute x6 -> x14, starting transfers between devices: 28.4 us -> 40.2 us  [the longest x8 32.2 us: eight(): got = lax.ppermute(zero[sub], 'section', [(1, 0)])]
    pallas_call x5 -> x4, Pallas kernels: 46.7 us -> 51.6 us  [assembled(): pl.pallas_call(kernel, grid_spec=pltpu.PrefetchScalarGridSpec(num_scalar_...]
    unnamed x389 -> x392, local copies, waits for them, and re-layouts: 54 us -> 55.4 us
    ppermute x90 -> x94, starting transfers between devices: 88.6 us -> 88.3 us  [partner(): return lax.ppermute(value, 'rep', [(i, i ^ bit) for i in range(count)])]
  transfers between devices with their start and end apart: 145 -> 157, of which waited for: 70 -> 68; matrix products, arithmetic and copies ran while one was open for 30% -> 29% of each run, Pallas kernels for 10% -> 10%
where the time goes in v4:
time: 1870 us; the launch traced here: 1860 us
  waiting for transfers between devices  788 us (42%)
  matrix products  299 us (16%)
  starting transfers between devices  244 us (13%)
  Pallas kernels  202 us (11%)
  other arithmetic  169 us (9%)
  local copies, waits for them, and re-layouts  143 us (8%)
    ppermute x94, waiting for transfers between devices, partner(): return lax.ppermute(value, 'rep', [(i, i ^ bit) for i in range(count)])  457 us
    ppermute x6, waiting for transfers between devices, backward(): lax.ppermute(grad_kv[step], 'fsdp', [(i, i - step) for i in range(step, d...  136 us
    dot_general x20, matrix products, dot(): lax.dot_general(left, right, (((left_dim,), (right_dim,)), ((), ())), pre...  122 us
    ppermute x9, waiting for transfers between devices, back(): lax.ppermute(value, 'fsdp', [(i, i + step) for i in range(depth - step)])  113 us
    dot_general x6, matrix products, times_back(): lax.dot_general(left, weight, (((1,), (1,)), ((), ())), preferred_element...  99.5 us
    ppermute x94, starting transfers between devices, partner(): return lax.ppermute(value, 'rep', [(i, i ^ bit) for i in range(count)])  88.3 us
    dot_general x6, matrix products, times(): return jnp.dot(left, weight, preferred_element_type=f32)  77.8 us
    pallas_call x2, Pallas kernels, attend_back(): pl.pallas_call(functools.partial(attend_back_kernel, len(keyvals)), grid=...  68.3 us
  transfers between devices with their start and end apart: 157, of which 68 were waited for; matrix products, arithmetic and copies ran while one was open for 29% of the time, Pallas kernels for 10%

profile of v4, /device:TPU:1, one launch (start us, length us, event | category | flops | bytes accessed | tf_op | source)
XLA Modules:
  0.0 1863.6 jit_solution(7590365674719104769)
XLA Ops:
  75.5 16.9 collective-permute-done.11
  119.7 16.0 collective-permute-done.18.refs_1_
  135.8 22.5 %collective-permute-done.19.refs_2_ = bf16[2,4,128,256]{3,2,1,0:T(8,128)(2,1)S(1)} collective-permute-done((bf16[2,4,128,256]{3,2,1,0:T(8,128)(2,1)S(1)}, bf16[2,4,128,256]{3,2,1,0:T(8,128)(2,1)S(1)}, u32[]{:S(2)}, u32[]{:S(2)}) %collective-permute-start.19) | collective-permute-done | bytes 524320 | tf_op jit(solution)/shard_map/ppermute | solution.py:483
  158.2 22.5 %collective-permute-done.20.refs_3_ = bf16[2,4,128,256]{3,2,1,0:T(8,128)(2,1)S(1)} collective-permute-done((bf16[2,4,128,256]{3,2,1,0:T(8,128)(2,1)S(1)}, bf16[2,4,128,256]{3,2,1,0:T(8,128)(2,1)S(1)}, u32[]{:S(2)}, u32[]{:S(2)}) %collective-permute-start.20) | collective-permute-done | bytes 524320 | tf_op jit(solution)/shard_map/ppermute | solution.py:483
  180.7 28.3 %attend.2 = (bf16[2,4,128,512]{3,2,1,0:T(8,128)(2,1)S(1)}, f32[4,8,256]{2,1,0:T(8,128)S(1)}) custom-call(bf16[2,4,128,512]{3,2,1,0:T(8,128)(2,1)S(1)} %get-tuple-element.120.query_ref, bf16[4,1024,256]{2,1,0:T(8,128)(2,1)} %pad_maximum_fusion.15.bias_ref, bf16[2,4,128,256]{3,2,1,0:T(8,128)(2,1)S(1)} %get-tuple-element.121.refs_0_, ...), custom_call_target="tpu_custom_call" | custom-call | flops 8589934592 | bytes 8388608 | tf_op jit(solution)/shard_map/attend/pallas_call | solution.py:199
  218.8 18.4 collective-permute-done.21
  265.2 21.1 %collective-permute-done.28 = bf16[2,128,2048]{2,1,0:T(8,128)(2,1)S(1)} collective-permute-done((bf16[2,128,2048]{2,1,0:T(8,128)(2,1)S(1)}, bf16[2,128,2048]{2,1,0:T(8,128)(2,1)S(1)}, u32[]{:S(2)}, u32[]{:S(2)}) %collective-permute-start.28) | collective-permute-done | bytes 1048608 | tf_op jit(solution)/shard_map/ppermute | solution.py:25
  289.3 33.1 %all-gather.7.cloned.1.call-done = bf16[2048,6144]{1,0:T(8,128)(2,1)} async-done(((bf16[256,6144]{1,0:T(8,128)(2,1)}), bf16[2048,6144]{1,0:T(8,128)(2,1)}) %all-gather.7.cloned.1.call-update) | async-done | bytes 25165840 | tf_op jit(solution)/shard_map/all_gather | solution.py:516
  322.4 21.9 %fusion.6 = f32[1024,4096]{1,0:T(8,128)S(1)} fusion(bf16[1024,2048]{1,0:T(8,128)(2,1)} %bitcast.640, bf16[2048,6144]{1,0:T(8,128)(2,1)} %all-gather.7.cloned.1.call-done), kind=kOutput, calls=%fused_computation.6 | convolution fusion | flops 17179869184 | bytes 37748736 | tf_op jit(solution)/shard_map/dot_general | solution.py:90
  366.8 21.5 %collective-permute-done.30 = bf16[2,128,2048]{2,1,0:T(8,128)(2,1)S(1)} collective-permute-done((bf16[2,128,2048]{2,1,0:T(8,128)(2,1)S(1)}, bf16[2,128,2048]{2,1,0:T(8,128)(2,1)S(1)}, u32[]{:S(2)}, u32[]{:S(2)}) %collective-permute-start.30) | collective-permute-done | bytes 1048608 | tf_op jit(solution)/shard_map/ppermute | solution.py:25
  478.5 21.6 %collective-permute-done.39.refs_2_ = bf16[2,4,128,256]{3,2,1,0:T(8,128)(2,1)S(1)} collective-permute-done((bf16[2,4,128,256]{3,2,1,0:T(8,128)(2,1)S(1)}, bf16[2,4,128,256]{3,2,1,0:T(8,128)(2,1)S(1)}, u32[]{:S(2)}, u32[]{:S(2)}) %collective-permute-start.39) | collective-permute-done | bytes 524320 | tf_op jit(solution)/shard_map/ppermute | solution.py:483
  500.1 22.5 %collective-permute-done.40.refs_3_ = bf16[2,4,128,256]{3,2,1,0:T(8,128)(2,1)S(1)} collective-permute-done((bf16[2,4,128,256]{3,2,1,0:T(8,128)(2,1)S(1)}, bf16[2,4,128,256]{3,2,1,0:T(8,128)(2,1)S(1)}, u32[]{:S(2)}, u32[]{:S(2)}) %collective-permute-start.40) | collective-permute-done | bytes 524320 | tf_op jit(solution)/shard_map/ppermute | solution.py:483
  522.5 28.5 %attend.3 = (bf16[2,4,128,512]{3,2,1,0:T(8,128)(2,1)S(1)}, f32[4,8,256]{2,1,0:T(8,128)S(1)}) custom-call(bf16[2,4,128,512]{3,2,1,0:T(8,128)(2,1)S(1)} %get-tuple-element.123.query_ref, bf16[4,1024,256]{2,1,0:T(8,128)(2,1)} %pad_maximum_fusion.15.bias_ref, bf16[2,4,128,256]{3,2,1,0:T(8,128)(2,1)S(1)} %get-tuple-element.124.refs_0_, ...), custom_call_target="tpu_custom_call" | custom-call | flops 8589934592 | bytes 8388608 | tf_op jit(solution)/shard_map/attend/pallas_call | solution.py:199
  617.9 20.8 %collective-permute-done = bf16[1,128,2048]{2,1,0:T(8,128)(2,1)} collective-permute-done((bf16[1,128,2048]{2,1,0:T(8,128)(2,1)S(1)}, bf16[1,128,2048]{2,1,0:T(8,128)(2,1)}, u32[]{:S(2)}, u32[]{:S(2)}) %collective-permute-start) | collective-permute-done | bytes 524320 | tf_op jit(solution)/shard_map/ppermute | solution.py:25
  644.6 16.6 collective-permute-done.48
  667.5 21.5 %fusion.2 = f32[1024,4096]{1,0:T(8,128)S(1)} fusion(bf16[1024,2048]{1,0:T(8,128)(2,1)} %bitcast.642, bf16[2048,6144]{1,0:T(8,128)(2,1)} %all-gather.11.cloned.1.call-done), kind=kOutput, calls=%fused_computation.2 | convolution fusion | flops 17179869184 | bytes 37748736 | tf_op jit(solution)/shard_map/dot_general | solution.py:90
  739.0 19.4 %collective-permute-start.53 = (bf16[256,2048]{1,0:T(8,128)(2,1)S(1)}, bf16[256,2048]{1,0:T(8,128)(2,1)S(1)}, u32[]{:S(2)}, u32[]{:S(2)}) collective-permute-start(bf16[256,2048]{1,0:T(8,128)(2,1)S(1)} %get-tuple-element.247), channel_id=1, source_target_pairs={{0,16},{16,0},{1,17},{17,1},{2,18},{18,2},{3,19},{19,3},{4,20},{20... | collective-permute-start | bytes 3145736 | tf_op jit(solution)/shard_map/ppermute | solution.py:777
  769.9 21.1 %multiply_convert_fusion.3 = (bf16[1024,2048]{1,0:T(8,128)(2,1)}, bf16[1024,2048]{1,0:T(8,128)(2,1)}) fusion(f32[1024,4096]{1,0:T(8,128)} %copy-done.54, bf16[1024,2048]{1,0:T(8,128)(2,1)} %bitcast.685, bf16[2048,6144]{1,0:T(8,128)(2,1)} %all-gather.11.cloned.1.call-done), kind=kOutput, calls=%fused_computation.21 | convolution fusion | flops 8617197568 | bytes 37748736 | tf_op jit(solution)/shard_map/dot_general | solution.py:94
  791.0 22.8 %fusion.30 = bf16[1024,2048]{1,0:T(8,128)(2,1)S(1)} fusion(bf16[2048,6144]{1,0:T(8,128)(2,1)} %all-gather.11.cloned.1.call-done, bf16[1024,2048]{1,0:T(8,128)(2,1)} %get-tuple-element.131, bf16[1024,2048]{1,0:T(8,128)(2,1)} %get-tuple-element.130), kind=kOutput, calls=%fused_computation.57 | convolution fusion | flops 17198743552 | bytes 29360128 | tf_op jit(solution)/shard_map/dot_general | solution.py:94
  823.1 15.9 collective-permute-done.54
  884.8 21.8 %collective-permute-done.61 = bf16[2,128,2048]{2,1,0:T(8,128)(2,1)S(1)} collective-permute-done((bf16[2,128,2048]{2,1,0:T(8,128)(2,1)S(1)}, bf16[2,128,2048]{2,1,0:T(8,128)(2,1)S(1)}, u32[]{:S(2)}, u32[]{:S(2)}) %collective-permute-start.61) | collective-permute-done | bytes 1048608 | tf_op jit(solution)/shard_map/ppermute | solution.py:25
  939.0 27.1 %reduce-scatter.9.cloned.1.call-done = bf16[256,2048]{1,0:T(8,128)(2,1)} async-done(((bf16[1024,2048]{1,0:T(8,128)(2,1)}), bf16[256,2048]{1,0:T(8,128)(2,1)}) %reduce-scatter.9.cloned.1.call-update) | async-done | bytes 1048592 | tf_op jit(solution)/shard_map/reduce_scatter | solution.py:634
  970.0 33.9 %attend_back.2 = (f32[2,4,128,512]{3,2,1,0:T(8,128)}, bf16[2,4,128,256]{3,2,1,0:T(8,128)(2,1)S(1)}, bf16[2,4,128,256]{3,2,1,0:T(8,128)(2,1)}, bf16[2,4,128,256]{3,2,1,0:T(8,128)(2,1)}, bf16[2,4,128,256]{3,2,1,0:T(8,128)(2,1)}) custom-call(bf16[2,4,128,512]{3,2,1,0:T(8,128)(2,1)S(1)} %copy-done.36, bf16[2,4,128,512]{3,2,1,0:T(8,128)(2,1)} %bitcast.767, ...), custom_call_target="tpu_custom_call" | custom-call | flops 21474836480 | bytes 12582912 | tf_op jit(solution)/shard_map/attend_back/pallas_call | solution.py:216
  1032.9 19.9 %collective-permute-done.65.refs_1_ = bf16[2,4,128,256]{3,2,1,0:T(8,128)(2,1)S(1)} collective-permute-done((bf16[2,4,128,256]{3,2,1,0:T(8,128)(2,1)}, bf16[2,4,128,256]{3,2,1,0:T(8,128)(2,1)S(1)}, u32[]{:S(2)}, u32[]{:S(2)}) %collective-permute-start.65) | collective-permute-done | bytes 524320 | tf_op jit(solution)/shard_map/ppermute | solution.py:692
  1052.8 66.6 %collective-permute-done.66.refs_2_ = bf16[2,4,128,256]{3,2,1,0:T(8,128)(2,1)S(1)} collective-permute-done((bf16[2,4,128,256]{3,2,1,0:T(8,128)(2,1)}, bf16[2,4,128,256]{3,2,1,0:T(8,128)(2,1)S(1)}, u32[]{:S(2)}, u32[]{:S(2)}) %collective-permute-start.66) | collective-permute-done | bytes 524320 | tf_op jit(solution)/shard_map/ppermute | solution.py:692
  1236.3 21.4 %multiply_convert_fusion.1 = (bf16[1024,2048]{1,0:T(8,128)(2,1)}, bf16[1024,2048]{1,0:T(8,128)(2,1)}) fusion(f32[1024,4096]{1,0:T(8,128)} %copy-done.53, bf16[1024,2048]{1,0:T(8,128)(2,1)} %bitcast.688, bf16[2048,6144]{1,0:T(8,128)(2,1)} %all-gather.7.cloned.1.call-done), kind=kOutput, calls=%fused_computation.16 | convolution fusion | flops 8617197568 | bytes 37748736 | tf_op jit(solution)/shard_map/dot_general | solution.py:94
  1276.8 23.0 %fusion.21 = bf16[1024,2048]{1,0:T(8,128)(2,1)S(1)} fusion(bf16[1024,4096]{1,0:T(8,128)(2,1)} %pad_maximum_fusion, bf16[2048,6144]{1,0:T(8,128)(2,1)} %all-gather.7.cloned.1.call-done), kind=kOutput, calls=%fused_computation.46 | convolution fusion | flops 17181966336 | bytes 29360128 | tf_op jit(solution)/shard_map/dot_general | solution.py:94
  1366.3 21.0 %collective-permute-done.90 = bf16[2,128,2048]{2,1,0:T(8,128)(2,1)S(1)} collective-permute-done((bf16[2,128,2048]{2,1,0:T(8,128)(2,1)S(1)}, bf16[2,128,2048]{2,1,0:T(8,128)(2,1)S(1)}, u32[]{:S(2)}, u32[]{:S(2)}) %collective-permute-start.90) | collective-permute-done | bytes 1048608 | tf_op jit(solution)/shard_map/ppermute | solution.py:25
  1422.4 34.4 %attend_back.3 = (f32[2,4,128,512]{3,2,1,0:T(8,128)}, bf16[2,4,128,256]{3,2,1,0:T(8,128)(2,1)S(1)}, bf16[2,4,128,256]{3,2,1,0:T(8,128)(2,1)S(1)}, bf16[2,4,128,2...) custom-call(bf16[2,4,128,512]{3,2,1,0:T(8,128)(2,1)S(1)} %copy-done.34, bf16[2,4,128,512]{3,2,1,0:T(8,128)(2,1)} %bitcast.766, ...), custom_call_target="tpu_custom_call" | custom-call | flops 21474836480 | bytes 12582912 | tf_op jit(solution)/shard_map/attend_back/pallas_call | solution.py:216
  1492.7 44.0 %collective-permute-done.96.refs_2_ = bf16[2,4,128,256]{3,2,1,0:T(8,128)(2,1)} collective-permute-done((bf16[2,4,128,256]{3,2,1,0:T(8,128)(2,1)S(1)}, bf16[2,4,128,256]{3,2,1,0:T(8,128)(2,1)}, u32[]{:S(2)}, u32[]{:S(2)}) %collective-permute-start.96) | collective-permute-done | bytes 524320 | tf_op jit(solution)/shard_map/ppermute | solution.py:692
  1687.4 19.1 %collective-permute-done.123 = bf16[1,128,2048]{2,1,0:T(8,128)(2,1)S(1)} collective-permute-done((bf16[1,128,2048]{2,1,0:T(8,128)(2,1)S(1)}, bf16[1,128,2048]{2,1,0:T(8,128)(2,1)S(1)}, u32[]{:S(2)}, u32[]{:S(2)}) %collective-permute-start.123) | collective-permute-done | bytes 524320 | tf_op jit(solution)/shard_map/ppermute | solution.py:25
  1840.1 16.2 assemble.7
  (1020 shorter events, 1064.4 us)
Async XLA Ops:
  7.2 88.9 %all-gather.5.cloned.1.call-start = ((), (), s32[]{:S(2)}) async-start(), calls=%async_computation.12 | async-start | bytes 5898240 | tf_op jit(solution)/shard_map/all_gather | solution.py:516
  15.1 307.3 %all-gather.7.cloned.1.call-start = ((), (), s32[]{:S(2)}) async-start(), calls=%async_computation.13 | async-start | bytes 28311552 | tf_op jit(solution)/shard_map/all_gather | solution.py:516
  35.2 383.4 %all-gather.9.cloned.1.call-start = ((), (), s32[]{:S(2)}) async-start(), calls=%async_computation.14 | async-start | bytes 5898240 | tf_op jit(solution)/shard_map/all_gather | solution.py:516
  35.9 631.5 %all-gather.11.cloned.1.call-start = ((), (), s32[]{:S(2)}) async-start(), calls=%async_computation.15 | async-start | bytes 28311552 | tf_op jit(solution)/shard_map/all_gather | solution.py:516
  100.2 111.2 %all-to-all-start = ((bf16[4,128,2048]{2,1,0:T(8,128)(2,1)}), bf16[4,128,2048]{2,1,0:T(8,128)(2,1)}, u32[]{:S(2)}, u32[]{:S(2)}) async-start(bf16[4,128,2048]{2,1,0:T(8,128)(2,1)} %all_to_all.30), calls=%async_computation | async-start | bytes 4194304 | tf_op jit(solution)/shard_map/all_to_all | solution.py:554
  115.8 64.9 %collective-permute-start.20 = (bf16[2,4,128,256]{3,2,1,0:T(8,128)(2,1)S(1)}, bf16[2,4,128,256]{3,2,1,0:T(8,128)(2,1)S(1)}, u32[]{:S(2)}, u32[]{:S(2)}) collective-permute-start(bf16[2,4,128,256]{3,2,1,0:T(8,128)(2,1)S(1)} %get-tuple-element.121.refs_0_), channel_id=1, source_target_pairs={{0,12},{1,13},{2,14},{3,15},{16,28},{17,29},{18,30},{19,31}} | collective-permute-start | bytes 1572872 | tf_op jit(solution)/shard_map/ppermute | solution.py:483
  426.2 129.1 %all-to-all-start.1 = ((bf16[4,128,2048]{2,1,0:T(8,128)(2,1)}), bf16[4,128,2048]{2,1,0:T(8,128)(2,1)}, u32[]{:S(2)}, u32[]{:S(2)}) async-start(bf16[4,128,2048]{2,1,0:T(8,128)(2,1)} %all_to_all.33), calls=%async_computation.1 | async-start | bytes 4194304 | tf_op jit(solution)/shard_map/all_to_all | solution.py:554
  430.6 535.4 %reduce-scatter.9.cloned.1.call-start = ((), (), s32[]{:S(2)}) async-start(), calls=%async_computation.16 | async-start | bytes 5242880 | tf_op jit(solution)/shard_map/reduce_scatter | solution.py:634
  640.8 71.4 %collective-permute-start.1 = (bf16[2,128,2048]{2,1,0:T(8,128)(2,1)}, bf16[2,128,2048]{2,1,0:T(8,128)(2,1)}, u32[]{:S(2)}, u32[]{:S(2)}) collective-permute-start(bf16[2,128,2048]{2,1,0:T(8,128)(2,1)} %pad_maximum_fusion.44), channel_id=1, source_target_pairs={{0,2},{1,3},{2,0},{3,1},{4,6},{5,7},{6,4},{7,5},{8,10},{9,11},{10,... | collective-permute-start | bytes 3145736 | tf_op jit(solution)/shard_map/ppermute | solution.py:25
  768.4 75.5 %collective-permute-start.64 = (bf16[1024,2048]{1,0:T(8,128)(2,1)}, bf16[1024,2048]{1,0:T(8,128)(2,1)}, u32[]{:S(2)}, u32[]{:S(2)}) collective-permute-start(bf16[1024,2048]{1,0:T(8,128)(2,1)} %convolution_convert_fusion.7), channel_id=1, source_target_pairs={{0,16},{16,0},{1,17},{17,1},{2,18},{18,2},{3,19},{19,3},{4,20},{20... | collective-permute-start | bytes 12582920 | tf_op jit(solution)/shard_map/ppermute | solution.py:626
  823.0 87.5 %collective-permute-start.63 = (bf16[1024,2048]{1,0:T(8,128)(2,1)}, bf16[1024,2048]{1,0:T(8,128)(2,1)}, u32[]{:S(2)}, u32[]{:S(2)}) collective-permute-start(bf16[1024,2048]{1,0:T(8,128)(2,1)} %convolution_convert_fusion.5), channel_id=1, source_target_pairs={{0,16},{16,0},{1,17},{17,1},{2,18},{18,2},{3,19},{19,3},{4,20},{20... | collective-permute-start | bytes 12582920 | tf_op jit(solution)/shard_map/ppermute | solution.py:626
  852.0 282.1 %reduce-scatter.11.cloned.1.call-start = ((), (), s32[]{:S(2)}) async-start(), calls=%async_computation.17 | async-start | bytes 5242880 | tf_op jit(solution)/shard_map/reduce_scatter | solution.py:634
  929.9 264.5 %reduce-scatter.13.cloned.1.call-start = ((), (), s32[]{:S(2)}) async-start(), calls=%async_computation.18 | async-start | bytes 5242880 | tf_op jit(solution)/shard_map/reduce_scatter | solution.py:634
  1008.9 118.8 %collective-permute-start.72 = (bf16[2,128,2048]{2,1,0:T(8,128)(2,1)}, bf16[2,128,2048]{2,1,0:T(8,128)(2,1)}, u32[]{:S(2)}, u32[]{:S(2)}) collective-permute-start(bf16[2,128,2048]{2,1,0:T(8,128)(2,1)} %get-tuple-element.376), channel_id=1, source_target_pairs={{0,1},{1,0},{2,3},{3,2},{4,5},{5,4},{6,7},{7,6},{8,9},{9,8},{10,11... | collective-permute-start | bytes 3145736 | tf_op jit(solution)/shard_map/ppermute | solution.py:25
  1010.5 109.0 %collective-permute-start.66 = (bf16[2,4,128,256]{3,2,1,0:T(8,128)(2,1)}, bf16[2,4,128,256]{3,2,1,0:T(8,128)(2,1)S(1)}, u32[]{:S(2)}, u32[]{:S(2)}) collective-permute-start(bf16[2,4,128,256]{3,2,1,0:T(8,128)(2,1)} %get-tuple-element.144), channel_id=1, source_target_pairs={{8,0},{12,4},{9,1},{13,5},{10,2},{14,6},{11,3},{15,7},{24,16},{28,... | collective-permute-start | bytes 1572872 | tf_op jit(solution)/shard_map/ppermute | solution.py:692
  1019.9 99.6 %collective-permute-start.67 = (bf16[2,4,128,256]{3,2,1,0:T(8,128)(2,1)}, bf16[2,4,128,256]{3,2,1,0:T(8,128)(2,1)S(1)}, u32[]{:S(2)}, u32[]{:S(2)}) collective-permute-start(bf16[2,4,128,256]{3,2,1,0:T(8,128)(2,1)} %get-tuple-element.145), channel_id=1, source_target_pairs={{12,0},{13,1},{14,2},{15,3},{28,16},{29,17},{30,18},{31,19}} | collective-permute-start | bytes 1572872 | tf_op jit(solution)/shard_map/ppermute | solution.py:692
  1023.2 108.0 %collective-permute-start.70 = (bf16[2,128,2048]{2,1,0:T(8,128)(2,1)}, bf16[2,128,2048]{2,1,0:T(8,128)(2,1)}, u32[]{:S(2)}, u32[]{:S(2)}) collective-permute-start(bf16[2,128,2048]{2,1,0:T(8,128)(2,1)} %pad_maximum_fusion.56), channel_id=1, source_target_pairs={{0,2},{1,3},{2,0},{3,1},{4,6},{5,7},{6,4},{7,5},{8,10},{9,11},{10,... | collective-permute-start | bytes 3145736 | tf_op jit(solution)/shard_map/ppermute | solution.py:25
  1028.5 105.6 %all-to-all-start.2 = ((bf16[4,64,2048]{2,1,0:T(8,128)(2,1)}), bf16[4,64,2048]{2,1,0:T(8,128)(2,1)}, u32[]{:S(2)}, u32[]{:S(2)}) async-start(bf16[4,64,2048]{2,1,0:T(8,128)(2,1)} %bitcast.716), calls=%async_computation.3 | async-start | bytes 2097152 | tf_op jit(solution)/shard_map/all_to_all | solution.py:696
  1032.9 383.2 %reduce-scatter.17.cloned.1.call-start = ((), (), s32[]{:S(2)}) async-start(), calls=%async_computation.20 | async-start | bytes 3604480 | tf_op jit(solution)/shard_map/reduce_scatter | solution.py:634
  1199.4 66.4 %collective-permute-start.94 = (bf16[1024,896]{1,0:T(8,128)(2,1)}, bf16[1024,896]{1,0:T(8,128)(2,1)}, u32[]{:S(2)}, u32[]{:S(2)}) collective-permute-start(bf16[1024,896]{1,0:T(8,128)(2,1)} %fusion.138), channel_id=1, source_target_pairs={{0,16},{16,0},{1,17},{17,1},{2,18},{18,2},{3,19},{19,3},{4,20},{20... | collective-permute-start | bytes 5505032 | tf_op jit(solution)/shard_map/ppermute | solution.py:626
  1227.6 101.0 %collective-permute-start.93 = (bf16[1024,2048]{1,0:T(8,128)(2,1)}, bf16[1024,2048]{1,0:T(8,128)(2,1)}, u32[]{:S(2)}, u32[]{:S(2)}) collective-permute-start(bf16[1024,2048]{1,0:T(8,128)(2,1)} %convolution_convert_fusion.4), channel_id=1, source_target_pairs={{0,16},{16,0},{1,17},{17,1},{2,18},{18,2},{3,19},{19,3},{4,20},{20... | collective-permute-start | bytes 12582920 | tf_op jit(solution)/shard_map/ppermute | solution.py:626
  1270.6 145.5 %reduce-scatter.15.cloned.1.call-start = ((), (), s32[]{:S(2)}) async-start(), calls=%async_computation.19 | async-start | bytes 5242880 | tf_op jit(solution)/shard_map/reduce_scatter | solution.py:634
  1309.3 81.2 %collective-permute-start.92 = (bf16[1024,2048]{1,0:T(8,128)(2,1)}, bf16[1024,2048]{1,0:T(8,128)(2,1)}, u32[]{:S(2)}, u32[]{:S(2)}) collective-permute-start(bf16[1024,2048]{1,0:T(8,128)(2,1)} %convolution_convert_fusion.2), channel_id=1, source_target_pairs={{0,16},{16,0},{1,17},{17,1},{2,18},{18,2},{3,19},{19,3},{4,20},{20... | collective-permute-start | bytes 12582920 | tf_op jit(solution)/shard_map/ppermute | solution.py:626
  1337.7 285.7 %reduce-scatter.19.cloned.1.call-start = ((), (), s32[]{:S(2)}) async-start(), calls=%async_computation.21 | async-start | bytes 5242880 | tf_op jit(solution)/shard_map/reduce_scatter | solution.py:634
  1409.8 264.9 %reduce-scatter.21.cloned.1.call-start = ((), (), s32[]{:S(2)}) async-start(), calls=%async_computation.22 | async-start | bytes 5242880 | tf_op jit(solution)/shard_map/reduce_scatter | solution.py:634
  1419.2 143.8 %collective-permute-start.103 = (bf16[2,128,4096]{2,1,0:T(8,128)(2,1)}, bf16[2,128,4096]{2,1,0:T(8,128)(2,1)}, u32[]{:S(2)}, u32[]{:S(2)}) collective-permute-start(bf16[2,128,4096]{2,1,0:T(8,128)(2,1)} %maximum_bitcast_fusion.8), channel_id=1, source_target_pairs={{0,1},{1,0},{2,3},{3,2},{4,5},{5,4},{6,7},{7,6},{8,9},{9,8},{10,11... | collective-permute-start | bytes 6291464 | tf_op jit(solution)/shard_map/ppermute | solution.py:25
  1421.8 61.0 %collective-permute-start.98 = (bf16[1,128,2048]{2,1,0:T(8,128)(2,1)}, bf16[1,128,2048]{2,1,0:T(8,128)(2,1)}, u32[]{:S(2)}, u32[]{:S(2)}) collective-permute-start(bf16[1,128,2048]{2,1,0:T(8,128)(2,1)} %get-tuple-element.366), channel_id=1, source_target_pairs={{0,1},{1,0},{2,3},{3,2},{4,5},{5,4},{6,7},{7,6},{8,9},{9,8},{10,11... | collective-permute-start | bytes 1572872 | tf_op jit(solution)/shard_map/ppermute | solution.py:25
  1462.1 74.5 %collective-permute-start.96 = (bf16[2,4,128,256]{3,2,1,0:T(8,128)(2,1)S(1)}, bf16[2,4,128,256]{3,2,1,0:T(8,128)(2,1)}, u32[]{:S(2)}, u32[]{:S(2)}) collective-permute-start(bf16[2,4,128,256]{3,2,1,0:T(8,128)(2,1)S(1)} %get-tuple-element.180), channel_id=1, source_target_pairs={{8,0},{12,4},{9,1},{13,5},{10,2},{14,6},{11,3},{15,7},{24,16},{28,... | collective-permute-start | bytes 1572872 | tf_op jit(solution)/shard_map/ppermute | solution.py:692
  1482.3 85.1 %collective-permute-start.102 = (bf16[2,128,4096]{2,1,0:T(8,128)(2,1)S(1)}, bf16[2,128,4096]{2,1,0:T(8,128)(2,1)S(1)}, u32[]{:S(2)}, u32[]{:S(2)}) collective-permute-start(bf16[2,128,4096]{2,1,0:T(8,128)(2,1)S(1)} %copy-done.68), channel_id=1, source_target_pairs={{0,2},{1,3},{2,0},{3,1},{4,6},{5,7},{6,4},{7,5},{8,10},{9,11},{10,... | collective-permute-start | bytes 6291464 | tf_op jit(solution)/shard_map/ppermute | solution.py:25
  1611.0 122.1 %reduce-scatter.23.cloned.1.call-start = ((), (), s32[]{:S(2)}) async-start(), calls=%async_computation.23 | async-start | bytes 3604480 | tf_op jit(solution)/shard_map/reduce_scatter | solution.py:634
  1613.6 61.1 %collective-permute-start.115 = (bf16[4,128,4096]{2,1,0:T(8,128)(2,1)}, bf16[4,128,4096]{2,1,0:T(8,128)(2,1)}, u32[]{:S(2)}, u32[]{:S(2)}) collective-permute-start(bf16[4,128,4096]{2,1,0:T(8,128)(2,1)} %pad_maximum_fusion.9.refs_3_), channel_id=1, source_target_pairs={{0,16},{1,17},{2,18},{3,19},{4,20},{5,21},{6,22},{7,23},{8,24},{9,... | collective-permute-start | bytes 12582920 | tf_op jit(solution)/shard_map/ppermute | solution.py:720
  1614.9 59.8 %collective-permute-start.116 = (bf16[4,128,4096]{2,1,0:T(8,128)(2,1)}, bf16[4,128,4096]{2,1,0:T(8,128)(2,1)}, u32[]{:S(2)}, u32[]{:S(2)}) collective-permute-start(bf16[4,128,4096]{2,1,0:T(8,128)(2,1)} %bitcast.634), channel_id=1, source_target_pairs={{0,16},{1,17},{2,18},{3,19},{4,20},{5,21},{6,22},{7,23},{8,24},{9,... | collective-permute-start | bytes 12582920 | tf_op jit(solution)/shard_map/ppermute | solution.py:720
  (318 other events, 6086.7 us)
Sparse Core Ops, SparseCore 0:
  15.2 58.6 all-gather.4
  76.1 246.2 all-gather.6
  324.6 71.3 all-gather.8
  398.1 246.1 all-gather.10
  852.1 113.9 reduce-scatter.8
  968.3 95.0 reduce-scatter.10
  1065.7 93.4 reduce-scatter.12
  1270.8 53.0 reduce-scatter.16
  1337.8 74.6 reduce-scatter.14
  1415.2 103.8 reduce-scatter.18
  1522.1 87.1 reduce-scatter.20
  1674.9 58.1 reduce-scatter.22

commit v5 on v4

--- a/solution.py
+++ b/solution.py
@@ -671,29 +671,40 @@
         grad_mid, gain_grad_ffn = norm_back(db, gain_ffn, unit, scale_mid)
         grad_mid = grad_mid + grad_out.astype(f32)
         go = grad_mid.astype(bf16)
+        if last:
+            go, old_rest = together(go, old_rest)
         go_all = flat(plane_gather(go))
         go_all, part_gate, part_up = together(
             go_all, finish_gate(grad_gate, sent_gate), finish_up(grad_up, sent_up)
         )
         own_gate, own_up = collect(part_gate), collect(part_up)
         grad_mixed = blocks(times_back(go_all, out_all[layer]).astype(bf16))
+        def output_part(go_all):
+            sent_o, finish_o = core_product(flat(mixed), go_all)
+            return lax.all_to_all(finish_o(go_all, sent_o), "rep", 0, 0, tiled=True)
+
         if last:
-            grad_mixed, own_down, old_rest, *ffn_state = together(
-                grad_mixed, own_down, old_rest, *ffn_state
-            )
+            grad_mixed, old_rest, *ffn_state = together(grad_mixed, old_rest, *ffn_state)
             ffn_state = gather_step(ffn_state, 1)
             rest_state = gather_step(gather_start(old_rest), 0)
+            part_o = output_part(go_all)
         else:
             grad_mixed, own_down = together(grad_mixed, own_down)
-        own_down = gather_pair(gather_start(own_down), 0)
+            own_down = gather_pair(gather_start(own_down), 0)
         grad_query, grad_kv = attend_back(query, keyvals, grad_mixed, log_total, bias)
-        grad_query, go_all, *grad_kv = together(grad_query, go_all, *grad_kv)
+        if last:
+            grad_query, part_o, own_down, *grad_kv = together(
+                grad_query, part_o, own_down, *grad_kv
+            )
+            own_down = gather_pair(gather_start(own_down), 0)
+        else:
+            grad_query, go_all, *grad_kv = together(grad_query, go_all, *grad_kv)
         grad_kv = [grad_kv[0]] + [
             lax.ppermute(grad_kv[step], "fsdp", [(i, i - step) for i in range(step, depth)])
             for step in range(1, depth)
         ]
-        sent_o, finish = core_product(flat(mixed), go_all)
-        part_o = lax.all_to_all(finish(go_all, sent_o), "rep", 0, 0, tiled=True)
+        if not last:
+            part_o = output_part(go_all)
         grad_qkv, da = project_back(grad_query, grad_kv, qkv_all[layer], cosine, sine, k_width)
         grad_qkv = flat(grad_qkv)
 

time: 1870 us -> 1880 us (level)
    ppermute x94, waiting for transfers between devices: 457 us -> 400 us  [partner(): return lax.ppermute(value, 'rep', [(i, i ^ bit) for i in range(count)])]
    ppermute x6, waiting for transfers between devices: 136 us -> 166 us  [backward(): lax.ppermute(grad_kv[step], 'fsdp', [(i, i - step) for i in range(step, d...]
    unnamed x392 -> x376, local copies, waits for them, and re-layouts: 55.4 us -> 59.2 us
  transfers between devices with their start and end apart: 157 -> 157, of which waited for: 68 -> 67; matrix products, arithmetic and copies ran while one was open for 29% -> 29% of each run, Pallas kernels for 10% -> 10%
where the time goes in v5:
time: 1880 us; the launch traced here: 1870 us
  waiting for transfers between devices  772 us (41%)
  matrix products  297 us (16%)
  starting transfers between devices  259 us (14%)
  Pallas kernels  201 us (11%)
  other arithmetic  176 us (9%)
  local copies, waits for them, and re-layouts  143 us (8%)
    ppermute x94, waiting for transfers between devices, partner(): return lax.ppermute(value, 'rep', [(i, i ^ bit) for i in range(count)])  400 us
    ppermute x6, waiting for transfers between devices, backward(): lax.ppermute(grad_kv[step], 'fsdp', [(i, i - step) for i in range(step, d...  166 us
    dot_general x20, matrix products, dot(): lax.dot_general(left, right, (((left_dim,), (right_dim,)), ((), ())), pre...  122 us
    ppermute x9, waiting for transfers between devices, back(): lax.ppermute(value, 'fsdp', [(i, i + step) for i in range(depth - step)])  113 us
    dot_general x6, matrix products, times_back(): lax.dot_general(left, weight, (((1,), (1,)), ((), ())), preferred_element...  98.5 us
    ppermute x94, starting transfers between devices, partner(): return lax.ppermute(value, 'rep', [(i, i ^ bit) for i in range(count)])  84.7 us
    dot_general x6, matrix products, times(): return jnp.dot(left, weight, preferred_element_type=f32)  76.5 us
    pallas_call x2, Pallas kernels, attend_back(): pl.pallas_call(functools.partial(attend_back_kernel, len(keyvals)), grid=...  67.3 us
  transfers between devices with their start and end apart: 157, of which 67 were waited for; matrix products, arithmetic and copies ran while one was open for 29% of the time, Pallas kernels for 10%

profile of v5, /device:TPU:1, one launch (start us, length us, event | category | flops | bytes accessed | tf_op | source)
XLA Modules:
  0.0 1866.1 jit_solution(2218341090301402333)
XLA Ops:
  75.5 16.9 collective-permute-done.11
  119.7 16.0 collective-permute-done.18.refs_1_
  135.8 22.5 %collective-permute-done.19.refs_2_ = bf16[2,4,128,256]{3,2,1,0:T(8,128)(2,1)S(1)} collective-permute-done((bf16[2,4,128,256]{3,2,1,0:T(8,128)(2,1)S(1)}, bf16[2,4,128,256]{3,2,1,0:T(8,128)(2,1)S(1)}, u32[]{:S(2)}, u32[]{:S(2)}) %collective-permute-start.19) | collective-permute-done | bytes 524320 | tf_op jit(solution)/shard_map/ppermute | solution.py:483
  158.2 22.5 %collective-permute-done.20.refs_3_ = bf16[2,4,128,256]{3,2,1,0:T(8,128)(2,1)S(1)} collective-permute-done((bf16[2,4,128,256]{3,2,1,0:T(8,128)(2,1)S(1)}, bf16[2,4,128,256]{3,2,1,0:T(8,128)(2,1)S(1)}, u32[]{:S(2)}, u32[]{:S(2)}) %collective-permute-start.20) | collective-permute-done | bytes 524320 | tf_op jit(solution)/shard_map/ppermute | solution.py:483
  180.7 28.3 %attend.2 = (bf16[2,4,128,512]{3,2,1,0:T(8,128)(2,1)S(1)}, f32[4,8,256]{2,1,0:T(8,128)S(1)}) custom-call(bf16[2,4,128,512]{3,2,1,0:T(8,128)(2,1)S(1)} %get-tuple-element.122.query_ref, bf16[4,1024,256]{2,1,0:T(8,128)(2,1)} %pad_maximum_fusion.15.bias_ref, bf16[2,4,128,256]{3,2,1,0:T(8,128)(2,1)S(1)} %get-tuple-element.123.refs_0_, ...), custom_call_target="tpu_custom_call" | custom-call | flops 8589934592 | bytes 8388608 | tf_op jit(solution)/shard_map/attend/pallas_call | solution.py:199
  218.8 18.4 collective-permute-done.21
  265.3 21.2 %collective-permute-done.28 = bf16[2,128,2048]{2,1,0:T(8,128)(2,1)S(1)} collective-permute-done((bf16[2,128,2048]{2,1,0:T(8,128)(2,1)S(1)}, bf16[2,128,2048]{2,1,0:T(8,128)(2,1)S(1)}, u32[]{:S(2)}, u32[]{:S(2)}) %collective-permute-start.28) | collective-permute-done | bytes 1048608 | tf_op jit(solution)/shard_map/ppermute | solution.py:25
  289.4 33.0 %all-gather.7.cloned.1.call-done = bf16[2048,6144]{1,0:T(8,128)(2,1)} async-done(((bf16[256,6144]{1,0:T(8,128)(2,1)}), bf16[2048,6144]{1,0:T(8,128)(2,1)}) %all-gather.7.cloned.1.call-update) | async-done | bytes 25165840 | tf_op jit(solution)/shard_map/all_gather | solution.py:516
  322.4 21.9 %fusion.6 = f32[1024,4096]{1,0:T(8,128)S(1)} fusion(bf16[1024,2048]{1,0:T(8,128)(2,1)} %bitcast.638, bf16[2048,6144]{1,0:T(8,128)(2,1)} %all-gather.7.cloned.1.call-done), kind=kOutput, calls=%fused_computation.6 | convolution fusion | flops 17179869184 | bytes 37748736 | tf_op jit(solution)/shard_map/dot_general | solution.py:90
  366.8 21.5 %collective-permute-done.30 = bf16[2,128,2048]{2,1,0:T(8,128)(2,1)S(1)} collective-permute-done((bf16[2,128,2048]{2,1,0:T(8,128)(2,1)S(1)}, bf16[2,128,2048]{2,1,0:T(8,128)(2,1)S(1)}, u32[]{:S(2)}, u32[]{:S(2)}) %collective-permute-start.30) | collective-permute-done | bytes 1048608 | tf_op jit(solution)/shard_map/ppermute | solution.py:25
  478.4 21.5 %collective-permute-done.39.refs_2_ = bf16[2,4,128,256]{3,2,1,0:T(8,128)(2,1)S(1)} collective-permute-done((bf16[2,4,128,256]{3,2,1,0:T(8,128)(2,1)S(1)}, bf16[2,4,128,256]{3,2,1,0:T(8,128)(2,1)S(1)}, u32[]{:S(2)}, u32[]{:S(2)}) %collective-permute-start.39) | collective-permute-done | bytes 524320 | tf_op jit(solution)/shard_map/ppermute | solution.py:483
  500.0 22.5 %collective-permute-done.40.refs_3_ = bf16[2,4,128,256]{3,2,1,0:T(8,128)(2,1)S(1)} collective-permute-done((bf16[2,4,128,256]{3,2,1,0:T(8,128)(2,1)S(1)}, bf16[2,4,128,256]{3,2,1,0:T(8,128)(2,1)S(1)}, u32[]{:S(2)}, u32[]{:S(2)}) %collective-permute-start.40) | collective-permute-done | bytes 524320 | tf_op jit(solution)/shard_map/ppermute | solution.py:483
  522.5 28.5 %attend.3 = (bf16[2,4,128,512]{3,2,1,0:T(8,128)(2,1)S(1)}, f32[4,8,256]{2,1,0:T(8,128)S(1)}) custom-call(bf16[2,4,128,512]{3,2,1,0:T(8,128)(2,1)S(1)} %get-tuple-element.125.query_ref, bf16[4,1024,256]{2,1,0:T(8,128)(2,1)} %pad_maximum_fusion.15.bias_ref, bf16[2,4,128,256]{3,2,1,0:T(8,128)(2,1)S(1)} %get-tuple-element.126.refs_0_, ...), custom_call_target="tpu_custom_call" | custom-call | flops 8589934592 | bytes 8388608 | tf_op jit(solution)/shard_map/attend/pallas_call | solution.py:199
  617.8 20.7 %collective-permute-done = bf16[1,128,2048]{2,1,0:T(8,128)(2,1)} collective-permute-done((bf16[1,128,2048]{2,1,0:T(8,128)(2,1)S(1)}, bf16[1,128,2048]{2,1,0:T(8,128)(2,1)}, u32[]{:S(2)}, u32[]{:S(2)}) %collective-permute-start) | collective-permute-done | bytes 524320 | tf_op jit(solution)/shard_map/ppermute | solution.py:25
  644.5 16.5 collective-permute-done.48
  667.3 21.5 %fusion.2 = f32[1024,4096]{1,0:T(8,128)S(1)} fusion(bf16[1024,2048]{1,0:T(8,128)(2,1)} %bitcast.640, bf16[2048,6144]{1,0:T(8,128)(2,1)} %all-gather.11.cloned.1.call-done), kind=kOutput, calls=%fused_computation.2 | convolution fusion | flops 17179869184 | bytes 37748736 | tf_op jit(solution)/shard_map/dot_general | solution.py:90
  735.3 19.1 %collective-permute-start.53 = (bf16[256,2048]{1,0:T(8,128)(2,1)S(1)}, bf16[256,2048]{1,0:T(8,128)(2,1)S(1)}, u32[]{:S(2)}, u32[]{:S(2)}) collective-permute-start(bf16[256,2048]{1,0:T(8,128)(2,1)S(1)} %get-tuple-element.251), channel_id=1, source_target_pairs={{0,16},{16,0},{1,17},{17,1},{2,18},{18,2},{3,19},{19,3},{4,20},{20... | collective-permute-start | bytes 3145736 | tf_op jit(solution)/shard_map/ppermute | solution.py:788
  766.0 21.1 %multiply_convert_fusion.3 = (bf16[1024,2048]{1,0:T(8,128)(2,1)}, bf16[1024,2048]{1,0:T(8,128)(2,1)}) fusion(f32[1024,4096]{1,0:T(8,128)} %copy-done.60, bf16[1024,2048]{1,0:T(8,128)(2,1)} %bitcast.679, bf16[2048,6144]{1,0:T(8,128)(2,1)} %all-gather.11.cloned.1.call-done), kind=kOutput, calls=%fused_computation.21 | convolution fusion | flops 8617197568 | bytes 37748736 | tf_op jit(solution)/shard_map/dot_general | solution.py:94
  787.2 22.8 %fusion.30 = bf16[1024,2048]{1,0:T(8,128)(2,1)S(1)} fusion(bf16[2048,6144]{1,0:T(8,128)(2,1)} %all-gather.11.cloned.1.call-done, bf16[1024,2048]{1,0:T(8,128)(2,1)} %get-tuple-element.133, bf16[1024,2048]{1,0:T(8,128)(2,1)} %get-tuple-element.132), kind=kOutput, calls=%fused_computation.57 | convolution fusion | flops 17198743552 | bytes 29360128 | tf_op jit(solution)/shard_map/dot_general | solution.py:94
  819.3 15.8 collective-permute-done.54
  880.9 21.9 %collective-permute-done.61 = bf16[2,128,2048]{2,1,0:T(8,128)(2,1)S(1)} collective-permute-done((bf16[2,128,2048]{2,1,0:T(8,128)(2,1)S(1)}, bf16[2,128,2048]{2,1,0:T(8,128)(2,1)S(1)}, u32[]{:S(2)}, u32[]{:S(2)}) %collective-permute-start.61) | collective-permute-done | bytes 1048608 | tf_op jit(solution)/shard_map/ppermute | solution.py:25
  935.2 27.0 %reduce-scatter.9.cloned.1.call-done = bf16[256,2048]{1,0:T(8,128)(2,1)} async-done(((bf16[1024,2048]{1,0:T(8,128)(2,1)}), bf16[256,2048]{1,0:T(8,128)(2,1)}) %reduce-scatter.9.cloned.1.call-update) | async-done | bytes 1048592 | tf_op jit(solution)/shard_map/reduce_scatter | solution.py:634
  966.2 33.9 %attend_back.2 = (f32[2,4,128,512]{3,2,1,0:T(8,128)}, bf16[2,4,128,256]{3,2,1,0:T(8,128)(2,1)S(1)}, bf16[2,4,128,256]{3,2,1,0:T(8,128)(2,1)}, bf16[2,4,128,256]{3,2,1,0:T(8,128)(2,1)}, bf16[2,4,128,256]{3,2,1,0:T(8,128)(2,1)}) custom-call(bf16[2,4,128,512]{3,2,1,0:T(8,128)(2,1)S(1)} %copy-done.42, bf16[2,4,128,512]{3,2,1,0:T(8,128)(2,1)} %bitcast.761, ...), custom_call_target="tpu_custom_call" | custom-call | flops 21474836480 | bytes 12582912 | tf_op jit(solution)/shard_map/attend_back/pallas_call | solution.py:216
  1029.2 19.8 %collective-permute-done.65.refs_1_ = bf16[2,4,128,256]{3,2,1,0:T(8,128)(2,1)S(1)} collective-permute-done((bf16[2,4,128,256]{3,2,1,0:T(8,128)(2,1)}, bf16[2,4,128,256]{3,2,1,0:T(8,128)(2,1)S(1)}, u32[]{:S(2)}, u32[]{:S(2)}) %collective-permute-start.65) | collective-permute-done | bytes 524320 | tf_op jit(solution)/shard_map/ppermute | solution.py:703
  1049.0 66.7 %collective-permute-done.66.refs_2_ = bf16[2,4,128,256]{3,2,1,0:T(8,128)(2,1)S(1)} collective-permute-done((bf16[2,4,128,256]{3,2,1,0:T(8,128)(2,1)}, bf16[2,4,128,256]{3,2,1,0:T(8,128)(2,1)S(1)}, u32[]{:S(2)}, u32[]{:S(2)}) %collective-permute-start.66) | collective-permute-done | bytes 524320 | tf_op jit(solution)/shard_map/ppermute | solution.py:703
  1233.2 21.4 %multiply_convert_fusion.1 = (bf16[1024,2048]{1,0:T(8,128)(2,1)}, bf16[1024,2048]{1,0:T(8,128)(2,1)}) fusion(f32[1024,4096]{1,0:T(8,128)} %copy-done.59, bf16[1024,2048]{1,0:T(8,128)(2,1)} %bitcast.682, bf16[2048,6144]{1,0:T(8,128)(2,1)} %all-gather.7.cloned.1.call-done), kind=kOutput, calls=%fused_computation.16 | convolution fusion | flops 8617197568 | bytes 37748736 | tf_op jit(solution)/shard_map/dot_general | solution.py:94
  1273.5 23.2 %fusion.21 = bf16[1024,2048]{1,0:T(8,128)(2,1)S(1)} fusion(bf16[1024,4096]{1,0:T(8,128)(2,1)} %pad_maximum_fusion, bf16[2048,6144]{1,0:T(8,128)(2,1)} %all-gather.7.cloned.1.call-done), kind=kOutput, calls=%fused_computation.46 | convolution fusion | flops 17181966336 | bytes 29360128 | tf_op jit(solution)/shard_map/dot_general | solution.py:94
  1423.7 33.5 %attend_back.3 = (f32[2,4,128,512]{3,2,1,0:T(8,128)}, bf16[2,4,128,256]{3,2,1,0:T(8,128)(2,1)S(1)}, bf16[2,4,128,256]{3,2,1,0:T(8,128)(2,1)S(1)}, bf16[2,4,128,2...) custom-call(bf16[2,4,128,512]{3,2,1,0:T(8,128)(2,1)S(1)} %copy-done.40, bf16[2,4,128,512]{3,2,1,0:T(8,128)(2,1)} %bitcast.760, ...), custom_call_target="tpu_custom_call" | custom-call | flops 21474836480 | bytes 12582912 | tf_op jit(solution)/shard_map/attend_back/pallas_call | solution.py:216
  1515.1 63.5 %collective-permute-done.97.refs_2_ = bf16[2,4,128,256]{3,2,1,0:T(8,128)(2,1)S(1)} collective-permute-done((bf16[2,4,128,256]{3,2,1,0:T(8,128)(2,1)S(1)}, bf16[2,4,128,256]{3,2,1,0:T(8,128)(2,1)S(1)}, u32[]{:S(2)}, u32[]{:S(2)}) %collective-permute-start.97) | collective-permute-done | bytes 524320 | tf_op jit(solution)/shard_map/ppermute | solution.py:703
  1636.6 18.4 collective-permute-start.112
  1691.8 18.9 %collective-permute-done.123 = bf16[1,128,2048]{2,1,0:T(8,128)(2,1)S(1)} collective-permute-done((bf16[1,128,2048]{2,1,0:T(8,128)(2,1)S(1)}, bf16[1,128,2048]{2,1,0:T(8,128)(2,1)S(1)}, u32[]{:S(2)}, u32[]{:S(2)}) %collective-permute-start.123) | collective-permute-done | bytes 524320 | tf_op jit(solution)/shard_map/ppermute | solution.py:25
  1842.6 16.2 assemble.7
  (1004 shorter events, 1051.4 us)
Async XLA Ops:
  7.2 88.9 %all-gather.5.cloned.1.call-start = ((), (), s32[]{:S(2)}) async-start(), calls=%async_computation.12 | async-start | bytes 5898240 | tf_op jit(solution)/shard_map/all_gather | solution.py:516
  15.1 307.3 %all-gather.7.cloned.1.call-start = ((), (), s32[]{:S(2)}) async-start(), calls=%async_computation.13 | async-start | bytes 28311552 | tf_op jit(solution)/shard_map/all_gather | solution.py:516
  35.2 383.4 %all-gather.9.cloned.1.call-start = ((), (), s32[]{:S(2)}) async-start(), calls=%async_computation.14 | async-start | bytes 5898240 | tf_op jit(solution)/shard_map/all_gather | solution.py:516
  35.9 631.4 %all-gather.11.cloned.1.call-start = ((), (), s32[]{:S(2)}) async-start(), calls=%async_computation.15 | async-start | bytes 28311552 | tf_op jit(solution)/shard_map/all_gather | solution.py:516
  100.2 111.2 %all-to-all-start = ((bf16[4,128,2048]{2,1,0:T(8,128)(2,1)}), bf16[4,128,2048]{2,1,0:T(8,128)(2,1)}, u32[]{:S(2)}, u32[]{:S(2)}) async-start(bf16[4,128,2048]{2,1,0:T(8,128)(2,1)} %all_to_all.32), calls=%async_computation | async-start | bytes 4194304 | tf_op jit(solution)/shard_map/all_to_all | solution.py:554
  115.8 64.9 %collective-permute-start.20 = (bf16[2,4,128,256]{3,2,1,0:T(8,128)(2,1)S(1)}, bf16[2,4,128,256]{3,2,1,0:T(8,128)(2,1)S(1)}, u32[]{:S(2)}, u32[]{:S(2)}) collective-permute-start(bf16[2,4,128,256]{3,2,1,0:T(8,128)(2,1)S(1)} %get-tuple-element.123.refs_0_), channel_id=1, source_target_pairs={{0,12},{1,13},{2,14},{3,15},{16,28},{17,29},{18,30},{19,31}} | collective-permute-start | bytes 1572872 | tf_op jit(solution)/shard_map/ppermute | solution.py:483
  426.1 129.0 %all-to-all-start.1 = ((bf16[4,128,2048]{2,1,0:T(8,128)(2,1)}), bf16[4,128,2048]{2,1,0:T(8,128)(2,1)}, u32[]{:S(2)}, u32[]{:S(2)}) async-start(bf16[4,128,2048]{2,1,0:T(8,128)(2,1)} %all_to_all.35), calls=%async_computation.1 | async-start | bytes 4194304 | tf_op jit(solution)/shard_map/all_to_all | solution.py:554
  430.6 531.7 %reduce-scatter.9.cloned.1.call-start = ((), (), s32[]{:S(2)}) async-start(), calls=%async_computation.16 | async-start | bytes 5242880 | tf_op jit(solution)/shard_map/reduce_scatter | solution.py:634
  640.7 67.6 %collective-permute-start.1 = (bf16[2,128,2048]{2,1,0:T(8,128)(2,1)}, bf16[2,128,2048]{2,1,0:T(8,128)(2,1)}, u32[]{:S(2)}, u32[]{:S(2)}) collective-permute-start(bf16[2,128,2048]{2,1,0:T(8,128)(2,1)} %pad_maximum_fusion.44), channel_id=1, source_target_pairs={{0,2},{1,3},{2,0},{3,1},{4,6},{5,7},{6,4},{7,5},{8,10},{9,11},{10,... | collective-permute-start | bytes 3145736 | tf_op jit(solution)/shard_map/ppermute | solution.py:25
  764.5 75.6 %collective-permute-start.64 = (bf16[1024,2048]{1,0:T(8,128)(2,1)}, bf16[1024,2048]{1,0:T(8,128)(2,1)}, u32[]{:S(2)}, u32[]{:S(2)}) collective-permute-start(bf16[1024,2048]{1,0:T(8,128)(2,1)} %convolution_convert_fusion.7), channel_id=1, source_target_pairs={{0,16},{16,0},{1,17},{17,1},{2,18},{18,2},{3,19},{19,3},{4,20},{20... | collective-permute-start | bytes 12582920 | tf_op jit(solution)/shard_map/ppermute | solution.py:626
  819.3 87.5 %collective-permute-start.63 = (bf16[1024,2048]{1,0:T(8,128)(2,1)}, bf16[1024,2048]{1,0:T(8,128)(2,1)}, u32[]{:S(2)}, u32[]{:S(2)}) collective-permute-start(bf16[1024,2048]{1,0:T(8,128)(2,1)} %convolution_convert_fusion.5), channel_id=1, source_target_pairs={{0,16},{16,0},{1,17},{17,1},{2,18},{18,2},{3,19},{19,3},{4,20},{20... | collective-permute-start | bytes 12582920 | tf_op jit(solution)/shard_map/ppermute | solution.py:626
  848.2 282.2 %reduce-scatter.11.cloned.1.call-start = ((), (), s32[]{:S(2)}) async-start(), calls=%async_computation.17 | async-start | bytes 5242880 | tf_op jit(solution)/shard_map/reduce_scatter | solution.py:634
  926.2 264.6 %reduce-scatter.13.cloned.1.call-start = ((), (), s32[]{:S(2)}) async-start(), calls=%async_computation.18 | async-start | bytes 5242880 | tf_op jit(solution)/shard_map/reduce_scatter | solution.py:634
  1005.1 118.8 %collective-permute-start.72 = (bf16[2,128,2048]{2,1,0:T(8,128)(2,1)}, bf16[2,128,2048]{2,1,0:T(8,128)(2,1)}, u32[]{:S(2)}, u32[]{:S(2)}) collective-permute-start(bf16[2,128,2048]{2,1,0:T(8,128)(2,1)} %get-tuple-element.380), channel_id=1, source_target_pairs={{0,1},{1,0},{2,3},{3,2},{4,5},{5,4},{6,7},{7,6},{8,9},{9,8},{10,11... | collective-permute-start | bytes 3145736 | tf_op jit(solution)/shard_map/ppermute | solution.py:25
  1006.7 109.0 %collective-permute-start.66 = (bf16[2,4,128,256]{3,2,1,0:T(8,128)(2,1)}, bf16[2,4,128,256]{3,2,1,0:T(8,128)(2,1)S(1)}, u32[]{:S(2)}, u32[]{:S(2)}) collective-permute-start(bf16[2,4,128,256]{3,2,1,0:T(8,128)(2,1)} %get-tuple-element.146), channel_id=1, source_target_pairs={{8,0},{12,4},{9,1},{13,5},{10,2},{14,6},{11,3},{15,7},{24,16},{28,... | collective-permute-start | bytes 1572872 | tf_op jit(solution)/shard_map/ppermute | solution.py:703
  1016.1 99.6 %collective-permute-start.67 = (bf16[2,4,128,256]{3,2,1,0:T(8,128)(2,1)}, bf16[2,4,128,256]{3,2,1,0:T(8,128)(2,1)S(1)}, u32[]{:S(2)}, u32[]{:S(2)}) collective-permute-start(bf16[2,4,128,256]{3,2,1,0:T(8,128)(2,1)} %get-tuple-element.147), channel_id=1, source_target_pairs={{12,0},{13,1},{14,2},{15,3},{28,16},{29,17},{30,18},{31,19}} | collective-permute-start | bytes 1572872 | tf_op jit(solution)/shard_map/ppermute | solution.py:703
  1019.4 108.0 %collective-permute-start.70 = (bf16[2,128,2048]{2,1,0:T(8,128)(2,1)}, bf16[2,128,2048]{2,1,0:T(8,128)(2,1)}, u32[]{:S(2)}, u32[]{:S(2)}) collective-permute-start(bf16[2,128,2048]{2,1,0:T(8,128)(2,1)} %pad_maximum_fusion.56), channel_id=1, source_target_pairs={{0,2},{1,3},{2,0},{3,1},{4,6},{5,7},{6,4},{7,5},{8,10},{9,11},{10,... | collective-permute-start | bytes 3145736 | tf_op jit(solution)/shard_map/ppermute | solution.py:25
  1024.7 105.6 %all-to-all-start.2 = ((bf16[4,64,2048]{2,1,0:T(8,128)(2,1)}), bf16[4,64,2048]{2,1,0:T(8,128)(2,1)}, u32[]{:S(2)}, u32[]{:S(2)}) async-start(bf16[4,64,2048]{2,1,0:T(8,128)(2,1)} %bitcast.711), calls=%async_computation.3 | async-start | bytes 2097152 | tf_op jit(solution)/shard_map/all_to_all | solution.py:684
  1029.1 318.9 %reduce-scatter.15.cloned.1.call-start = ((), (), s32[]{:S(2)}) async-start(), calls=%async_computation.19 | async-start | bytes 3604480 | tf_op jit(solution)/shard_map/reduce_scatter | solution.py:634
  1195.6 66.9 %collective-permute-start.87 = (bf16[1024,896]{1,0:T(8,128)(2,1)}, bf16[1024,896]{1,0:T(8,128)(2,1)}, u32[]{:S(2)}, u32[]{:S(2)}) collective-permute-start(bf16[1024,896]{1,0:T(8,128)(2,1)} %fusion.138), channel_id=1, source_target_pairs={{0,16},{16,0},{1,17},{17,1},{2,18},{18,2},{3,19},{19,3},{4,20},{20... | collective-permute-start | bytes 5505032 | tf_op jit(solution)/shard_map/ppermute | solution.py:626
  1227.4 78.5 %collective-permute-start.95 = (bf16[1024,2048]{1,0:T(8,128)(2,1)}, bf16[1024,2048]{1,0:T(8,128)(2,1)}, u32[]{:S(2)}, u32[]{:S(2)}) collective-permute-start(bf16[1024,2048]{1,0:T(8,128)(2,1)} %convolution_convert_fusion.4), channel_id=1, source_target_pairs={{0,16},{16,0},{1,17},{17,1},{2,18},{18,2},{3,19},{19,3},{4,20},{20... | collective-permute-start | bytes 12582920 | tf_op jit(solution)/shard_map/ppermute | solution.py:626
  1267.4 209.4 %reduce-scatter.17.cloned.1.call-start = ((), (), s32[]{:S(2)}) async-start(), calls=%async_computation.20 | async-start | bytes 5242880 | tf_op jit(solution)/shard_map/reduce_scatter | solution.py:634
  1315.3 306.3 %reduce-scatter.19.cloned.1.call-start = ((), (), s32[]{:S(2)}) async-start(), calls=%async_computation.21 | async-start | bytes 5242880 | tf_op jit(solution)/shard_map/reduce_scatter | solution.py:634
  1394.1 283.4 %reduce-scatter.21.cloned.1.call-start = ((), (), s32[]{:S(2)}) async-start(), calls=%async_computation.22 | async-start | bytes 5242880 | tf_op jit(solution)/shard_map/reduce_scatter | solution.py:634
  1412.1 68.6 %collective-permute-start.104 = (bf16[2,128,4096]{2,1,0:T(8,128)(2,1)}, bf16[2,128,4096]{2,1,0:T(8,128)(2,1)}, u32[]{:S(2)}, u32[]{:S(2)}) collective-permute-start(bf16[2,128,4096]{2,1,0:T(8,128)(2,1)} %maximum_bitcast_fusion.8), channel_id=1, source_target_pairs={{0,1},{1,0},{2,3},{3,2},{4,5},{5,4},{6,7},{7,6},{8,9},{9,8},{10,11... | collective-permute-start | bytes 6291464 | tf_op jit(solution)/shard_map/ppermute | solution.py:25
  1412.4 81.6 %collective-permute-start.103 = (bf16[2,128,4096]{2,1,0:T(8,128)(2,1)}, bf16[2,128,4096]{2,1,0:T(8,128)(2,1)}, u32[]{:S(2)}, u32[]{:S(2)}) collective-permute-start(bf16[2,128,4096]{2,1,0:T(8,128)(2,1)} %pad_maximum_fusion.28), channel_id=1, source_target_pairs={{0,2},{1,3},{2,0},{3,1},{4,6},{5,7},{6,4},{7,5},{8,10},{9,11},{10,... | collective-permute-start | bytes 6291464 | tf_op jit(solution)/shard_map/ppermute | solution.py:25
  1421.9 313.9 %reduce-scatter.23.cloned.1.call-start = ((), (), s32[]{:S(2)}) async-start(), calls=%async_computation.23 | async-start | bytes 3604480 | tf_op jit(solution)/shard_map/reduce_scatter | solution.py:634
  1486.9 91.8 %collective-permute-start.97 = (bf16[2,4,128,256]{3,2,1,0:T(8,128)(2,1)S(1)}, bf16[2,4,128,256]{3,2,1,0:T(8,128)(2,1)S(1)}, u32[]{:S(2)}, u32[]{:S(2)}) collective-permute-start(bf16[2,4,128,256]{3,2,1,0:T(8,128)(2,1)S(1)} %copy-done.31), channel_id=1, source_target_pairs={{8,0},{12,4},{9,1},{13,5},{10,2},{14,6},{11,3},{15,7},{24,16},{28,... | collective-permute-start | bytes 1572872 | tf_op jit(solution)/shard_map/ppermute | solution.py:703
  1490.6 88.1 %collective-permute-start.98 = (bf16[2,4,128,256]{3,2,1,0:T(8,128)(2,1)S(1)}, bf16[2,4,128,256]{3,2,1,0:T(8,128)(2,1)S(1)}, u32[]{:S(2)}, u32[]{:S(2)}) collective-permute-start(bf16[2,4,128,256]{3,2,1,0:T(8,128)(2,1)S(1)} %copy-done.29), channel_id=1, source_target_pairs={{12,0},{13,1},{14,2},{15,3},{28,16},{29,17},{30,18},{31,19}} | collective-permute-start | bytes 1572872 | tf_op jit(solution)/shard_map/ppermute | solution.py:703
  1492.2 94.5 %collective-permute-start.102 = (bf16[2,128,2048]{2,1,0:T(8,128)(2,1)S(1)}, bf16[2,128,2048]{2,1,0:T(8,128)(2,1)S(1)}, u32[]{:S(2)}, u32[]{:S(2)}) collective-permute-start(bf16[2,128,2048]{2,1,0:T(8,128)(2,1)S(1)} %get-tuple-element.359), channel_id=1, source_target_pairs={{0,1},{1,0},{2,3},{3,2},{4,5},{5,4},{6,7},{7,6},{8,9},{9,8},{10,11... | collective-permute-start | bytes 3145736 | tf_op jit(solution)/shard_map/ppermute | solution.py:25
  1493.9 94.7 %collective-permute-start.100 = (bf16[2,128,2048]{2,1,0:T(8,128)(2,1)S(1)}, bf16[2,128,2048]{2,1,0:T(8,128)(2,1)S(1)}, u32[]{:S(2)}, u32[]{:S(2)}) collective-permute-start(bf16[2,128,2048]{2,1,0:T(8,128)(2,1)S(1)} %pad_maximum_fusion.61), channel_id=1, source_target_pairs={{0,2},{1,3},{2,0},{3,1},{4,6},{5,7},{6,4},{7,5},{8,10},{9,11},{10,... | collective-permute-start | bytes 3145736 | tf_op jit(solution)/shard_map/ppermute | solution.py:25
  1612.3 65.3 %collective-permute-start.115 = (bf16[4,128,4096]{2,1,0:T(8,128)(2,1)}, bf16[4,128,4096]{2,1,0:T(8,128)(2,1)}, u32[]{:S(2)}, u32[]{:S(2)}) collective-permute-start(bf16[4,128,4096]{2,1,0:T(8,128)(2,1)} %pad_maximum_fusion.9.refs_3_), channel_id=1, source_target_pairs={{0,16},{1,17},{2,18},{3,19},{4,20},{5,21},{6,22},{7,23},{8,24},{9,... | collective-permute-start | bytes 12582920 | tf_op jit(solution)/shard_map/ppermute | solution.py:731
  (310 other events, 5769.4 us)
Sparse Core Ops, SparseCore 0:
  15.2 58.6 all-gather.4
  76.1 246.2 all-gather.6
  324.6 71.3 all-gather.8
  398.1 246.1 all-gather.10
  848.3 113.9 reduce-scatter.8
  964.5 95.0 reduce-scatter.10
  1061.9 93.4 reduce-scatter.12
  1267.6 52.6 reduce-scatter.14
  1322.7 76.8 reduce-scatter.16
  1402.3 77.2 reduce-scatter.18
  1482.5 113.7 reduce-scatter.20
  1677.7 58.0 reduce-scatter.22

commit v6 on v5

--- a/solution.py
+++ b/solution.py
@@ -595,9 +595,9 @@
         residual = layer_in + plane_reduce(blocks(times(flat(mixed), out_all[layer]).astype(bf16)))
         scale_mid = scale_of(residual)
         b_all = plane_gather((residual * scale_mid * gain_ffn).astype(bf16))
-        pre = times(flat(b_all), ffn_all[layer])
+        pre = times(flat(b_all), ffn_all[layer]).astype(bf16)
         gate, up = pre[:, :ff_width], pre[:, ff_width:]
-        hidden = (jax.nn.silu(gate) * up).astype(bf16)
+        hidden = (jax.nn.silu(gate.astype(f32)) * up.astype(f32)).astype(bf16)
         out = residual + plane_reduce(blocks(times(hidden, down_all[layer]).astype(bf16)))
         kept = (layer_in, scale_in, a_all, query, keyvals, mixed, log_total)
         return out.astype(bf16), kept + (residual, scale_mid, b_all, gate, up, hidden)
@@ -654,6 +654,7 @@
             sent_down, finish = core_product(hidden, gm_all)
             gm_all, sent_down, *ready = together(gm_all, sent_down, *ready)
         grad_hidden = times_back(gm_all, down_all[layer])
+        gate, up = gate.astype(f32), up.astype(f32)
         sig = jax.nn.sigmoid(gate)
         grad_gate = (grad_hidden * up * (sig * (1.0 + gate * (1.0 - sig)))).astype(bf16)
         grad_up = (grad_hidden * (gate * sig)).astype(bf16)
@@ -744,24 +745,27 @@
         da, own_gate = together(plane_reduce(da), own_gate)
         grad_in, part_rest = input_side(da)
         gate_state = gather_step(gather_start(own_gate), 0)
-        tied = together(part_rest, own_up, *gate_state, *olds_sent, *old_rest)
-        part_rest, own_up = tied[:2]
-        gate_state, olds_sent, old_rest = tied[2:4], tied[4:8], tied[8:]
+        own_rest = collect(part_rest)
+        own_up, *tied = together(own_up, *gate_state, *olds_sent, *old_rest)
+        gate_state, olds_sent, old_rest = tied[:2], tied[2:6], tied[6:]
         ffn_sent, down_sent = olds_sent[:2], olds_sent[2:]
-        own_rest = collect(part_rest)
         rest_sent = send(old_rest)
         zero_gate = gather_pair(gate_state, 1)
         up_state = gather_step(gather_start(own_up), 0)
-        own_rest, *tied = together(own_rest, *zero_gate, *up_state, *rest_sent)
+        tied = together(*zero_gate, *up_state, *rest_sent)
         zero_gate, up_state, rest_sent = tied[:2], tied[2:4], tied[4:]
-        zero_up, zero_rest = gather_pair(up_state, 1), gather_pair(gather_start(own_rest), 0)
+        zero_up = gather_pair(up_state, 1)
         places = eight(zero_gate, old_ffn, ffn_sent)
         grad_gate = assemble_columns(info, places, (0, 0), ff_piece, depth)
         grad_down = assemble_rows(info, eight(zero_down, old_down, down_sent))
-        grad_gate, grad_down, *tied = together(grad_gate, grad_down, *zero_up, *zero_rest)
-        zero_up, zero_rest = tied[:2], tied[2:]
+        grad_gate, grad_down, own_rest, *zero_up = together(
+            grad_gate, grad_down, own_rest, *zero_up
+        )
+        rest_state = gather_step(gather_start(own_rest), 0)
         places = eight(zero_up, old_ffn, ffn_sent)
         grad_up = assemble_columns(info, places, (0, depth), ff_piece, depth)
+        grad_up, *rest_state = together(grad_up, *rest_state)
+        zero_rest = gather_pair(rest_state, 1)
         height = out_rows // 2
         proj_width = own_rest.shape[1] - height * width // tall
         places = eight(zero_rest, old_rest, rest_sent)

time: 1880 us -> 1870 us (level)
    unnamed x376 -> x389, local copies, waits for them, and re-layouts: 59.2 us -> 55.3 us
  transfers between devices with their start and end apart: 157 -> 157, of which waited for: 67 -> 70; matrix products, arithmetic and copies ran while one was open for 29% -> 29% of each run, Pallas kernels for 10% -> 10%
where the time goes in v6:
time: 1870 us; the launch traced here: 1860 us
  waiting for transfers between devices  779 us (42%)
  matrix products  289 us (15%)
  starting transfers between devices  266 us (14%)
  Pallas kernels  202 us (11%)
  other arithmetic  171 us (9%)
  local copies, waits for them, and re-layouts  135 us (7%)
    ppermute x94, waiting for transfers between devices, partner(): return lax.ppermute(value, 'rep', [(i, i ^ bit) for i in range(count)])  416 us
    ppermute x6, waiting for transfers between devices, backward(): lax.ppermute(grad_kv[step], 'fsdp', [(i, i - step) for i in range(step, d...  166 us
    dot_general x20, matrix products, dot(): lax.dot_general(left, right, (((left_dim,), (right_dim,)), ((), ())), pre...  123 us
    ppermute x9, waiting for transfers between devices, back(): lax.ppermute(value, 'fsdp', [(i, i + step) for i in range(depth - step)])  113 us
    dot_general x6, matrix products, times_back(): lax.dot_general(left, weight, (((1,), (1,)), ((), ())), preferred_element...  90.7 us
    ppermute x94, starting transfers between devices, partner(): return lax.ppermute(value, 'rep', [(i, i ^ bit) for i in range(count)])  85.2 us
    dot_general x6, matrix products, times(): return jnp.dot(left, weight, preferred_element_type=f32)  76.1 us
    pallas_call x2, Pallas kernels, attend_back(): pl.pallas_call(functools.partial(attend_back_kernel, len(keyvals)), grid=...  67.4 us
  transfers between devices with their start and end apart: 157, of which 70 were waited for; matrix products, arithmetic and copies ran while one was open for 29% of the time, Pallas kernels for 10%

profile of v6, /device:TPU:1, one launch (start us, length us, event | category | flops | bytes accessed | tf_op | source)
XLA Modules:
  0.0 1860.4 jit_solution(7247556541020071771)
XLA Ops:
  75.5 16.9 collective-permute-done.11
  120.0 16.0 collective-permute-done.18.refs_1_
  136.0 22.5 %collective-permute-done.19.refs_2_ = bf16[2,4,128,256]{3,2,1,0:T(8,128)(2,1)S(1)} collective-permute-done((bf16[2,4,128,256]{3,2,1,0:T(8,128)(2,1)S(1)}, bf16[2,4,128,256]{3,2,1,0:T(8,128)(2,1)S(1)}, u32[]{:S(2)}, u32[]{:S(2)}) %collective-permute-start.19) | collective-permute-done | bytes 524320 | tf_op jit(solution)/shard_map/ppermute | solution.py:483
  158.5 22.5 %collective-permute-done.20.refs_3_ = bf16[2,4,128,256]{3,2,1,0:T(8,128)(2,1)S(1)} collective-permute-done((bf16[2,4,128,256]{3,2,1,0:T(8,128)(2,1)S(1)}, bf16[2,4,128,256]{3,2,1,0:T(8,128)(2,1)S(1)}, u32[]{:S(2)}, u32[]{:S(2)}) %collective-permute-start.20) | collective-permute-done | bytes 524320 | tf_op jit(solution)/shard_map/ppermute | solution.py:483
  181.0 28.3 %attend.2 = (bf16[2,4,128,512]{3,2,1,0:T(8,128)(2,1)S(1)}, f32[4,8,256]{2,1,0:T(8,128)S(1)}) custom-call(bf16[2,4,128,512]{3,2,1,0:T(8,128)(2,1)S(1)} %get-tuple-element.122.query_ref, bf16[4,1024,256]{2,1,0:T(8,128)(2,1)} %pad_maximum_fusion.15.bias_ref, bf16[2,4,128,256]{3,2,1,0:T(8,128)(2,1)S(1)} %get-tuple-element.123.refs_0_, ...), custom_call_target="tpu_custom_call" | custom-call | flops 8589934592 | bytes 8388608 | tf_op jit(solution)/shard_map/attend/pallas_call | solution.py:199
  219.2 18.2 collective-permute-done.21
  265.7 21.0 %collective-permute-done.28 = bf16[2,128,2048]{2,1,0:T(8,128)(2,1)S(1)} collective-permute-done((bf16[2,128,2048]{2,1,0:T(8,128)(2,1)S(1)}, bf16[2,128,2048]{2,1,0:T(8,128)(2,1)S(1)}, u32[]{:S(2)}, u32[]{:S(2)}) %collective-permute-start.28) | collective-permute-done | bytes 1048608 | tf_op jit(solution)/shard_map/ppermute | solution.py:25
  289.7 32.8 %all-gather.7.cloned.1.call-done = bf16[2048,6144]{1,0:T(8,128)(2,1)} async-done(((bf16[256,6144]{1,0:T(8,128)(2,1)}), bf16[2048,6144]{1,0:T(8,128)(2,1)}) %all-gather.7.cloned.1.call-update) | async-done | bytes 25165840 | tf_op jit(solution)/shard_map/all_gather | solution.py:516
  322.4 21.7 %fusion.27 = bf16[1024,4096]{1,0:T(8,128)(2,1)S(1)} fusion(bf16[1024,2048]{1,0:T(8,128)(2,1)} %bitcast.640, bf16[2048,6144]{1,0:T(8,128)(2,1)} %all-gather.7.cloned.1.call-done), kind=kOutput, calls=%fused_computation.46 | convolution fusion | flops 17184063488 | bytes 29360128 | tf_op jit(solution)/shard_map/dot_general | solution.py:90
  363.6 21.4 %collective-permute-done.30 = bf16[2,128,2048]{2,1,0:T(8,128)(2,1)S(1)} collective-permute-done((bf16[2,128,2048]{2,1,0:T(8,128)(2,1)S(1)}, bf16[2,128,2048]{2,1,0:T(8,128)(2,1)S(1)}, u32[]{:S(2)}, u32[]{:S(2)}) %collective-permute-start.30) | collective-permute-done | bytes 1048608 | tf_op jit(solution)/shard_map/ppermute | solution.py:25
  475.0 21.5 %collective-permute-done.39.refs_2_ = bf16[2,4,128,256]{3,2,1,0:T(8,128)(2,1)S(1)} collective-permute-done((bf16[2,4,128,256]{3,2,1,0:T(8,128)(2,1)S(1)}, bf16[2,4,128,256]{3,2,1,0:T(8,128)(2,1)S(1)}, u32[]{:S(2)}, u32[]{:S(2)}) %collective-permute-start.39) | collective-permute-done | bytes 524320 | tf_op jit(solution)/shard_map/ppermute | solution.py:483
  496.5 22.5 %collective-permute-done.40.refs_3_ = bf16[2,4,128,256]{3,2,1,0:T(8,128)(2,1)S(1)} collective-permute-done((bf16[2,4,128,256]{3,2,1,0:T(8,128)(2,1)S(1)}, bf16[2,4,128,256]{3,2,1,0:T(8,128)(2,1)S(1)}, u32[]{:S(2)}, u32[]{:S(2)}) %collective-permute-start.40) | collective-permute-done | bytes 524320 | tf_op jit(solution)/shard_map/ppermute | solution.py:483
  519.0 28.7 %attend.3 = (bf16[2,4,128,512]{3,2,1,0:T(8,128)(2,1)S(1)}, f32[4,8,256]{2,1,0:T(8,128)S(1)}) custom-call(bf16[2,4,128,512]{3,2,1,0:T(8,128)(2,1)S(1)} %get-tuple-element.125.query_ref, bf16[4,1024,256]{2,1,0:T(8,128)(2,1)} %pad_maximum_fusion.15.bias_ref, bf16[2,4,128,256]{3,2,1,0:T(8,128)(2,1)S(1)} %get-tuple-element.126.refs_0_, ...), custom_call_target="tpu_custom_call" | custom-call | flops 8589934592 | bytes 8388608 | tf_op jit(solution)/shard_map/attend/pallas_call | solution.py:199
  614.2 21.5 %collective-permute-done = bf16[1,128,2048]{2,1,0:T(8,128)(2,1)} collective-permute-done((bf16[1,128,2048]{2,1,0:T(8,128)(2,1)S(1)}, bf16[1,128,2048]{2,1,0:T(8,128)(2,1)}, u32[]{:S(2)}, u32[]{:S(2)}) %collective-permute-start) | collective-permute-done | bytes 524320 | tf_op jit(solution)/shard_map/ppermute | solution.py:25
  641.0 17.2 collective-permute-done.48
  664.4 21.5 %fusion.30 = bf16[1024,4096]{1,0:T(8,128)(2,1)S(1)} fusion(bf16[1024,2048]{1,0:T(8,128)(2,1)} %bitcast.642, bf16[2048,6144]{1,0:T(8,128)(2,1)} %all-gather.11.cloned.1.call-done), kind=kOutput, calls=%fused_computation.47 | convolution fusion | flops 17184063488 | bytes 29360128 | tf_op jit(solution)/shard_map/dot_general | solution.py:90
  730.1 20.4 %collective-permute-start.53 = (bf16[256,2048]{1,0:T(8,128)(2,1)S(1)}, bf16[256,2048]{1,0:T(8,128)(2,1)S(1)}, u32[]{:S(2)}, u32[]{:S(2)}) collective-permute-start(bf16[256,2048]{1,0:T(8,128)(2,1)S(1)} %get-tuple-element.251), channel_id=1, source_target_pairs={{0,16},{16,0},{1,17},{17,1},{2,18},{18,2},{3,19},{19,3},{4,20},{20... | collective-permute-start | bytes 3145736 | tf_op jit(solution)/shard_map/ppermute | solution.py:792
  761.8 17.5 fusion.13
  779.2 22.8 %fusion.50 = bf16[1024,2048]{1,0:T(8,128)(2,1)S(1)} fusion(bf16[2048,6144]{1,0:T(8,128)(2,1)} %all-gather.11.cloned.1.call-done, bf16[1024,2048]{1,0:T(8,128)(2,1)} %get-tuple-element.133, bf16[1024,2048]{1,0:T(8,128)(2,1)} %get-tuple-element.132), kind=kOutput, calls=%fused_computation.77 | convolution fusion | flops 17198743552 | bytes 29360128 | tf_op jit(solution)/shard_map/dot_general | solution.py:94
  811.4 15.8 collective-permute-done.54
  873.1 21.4 %collective-permute-done.61 = bf16[2,128,2048]{2,1,0:T(8,128)(2,1)S(1)} collective-permute-done((bf16[2,128,2048]{2,1,0:T(8,128)(2,1)S(1)}, bf16[2,128,2048]{2,1,0:T(8,128)(2,1)S(1)}, u32[]{:S(2)}, u32[]{:S(2)}) %collective-permute-start.61) | collective-permute-done | bytes 1048608 | tf_op jit(solution)/shard_map/ppermute | solution.py:25
  926.8 26.8 %reduce-scatter.9.cloned.1.call-done = bf16[256,2048]{1,0:T(8,128)(2,1)} async-done(((bf16[1024,2048]{1,0:T(8,128)(2,1)}), bf16[256,2048]{1,0:T(8,128)(2,1)}) %reduce-scatter.9.cloned.1.call-update) | async-done | bytes 1048592 | tf_op jit(solution)/shard_map/reduce_scatter | solution.py:634
  957.5 33.9 %attend_back.2 = (f32[2,4,128,512]{3,2,1,0:T(8,128)}, bf16[2,4,128,256]{3,2,1,0:T(8,128)(2,1)S(1)}, bf16[2,4,128,256]{3,2,1,0:T(8,128)(2,1)}, bf16[2,4,128,256]{3,2,1,0:T(8,128)(2,1)}, bf16[2,4,128,256]{3,2,1,0:T(8,128)(2,1)}) custom-call(bf16[2,4,128,512]{3,2,1,0:T(8,128)(2,1)S(1)} %copy-done.42, bf16[2,4,128,512]{3,2,1,0:T(8,128)(2,1)} %bitcast.772, ...), custom_call_target="tpu_custom_call" | custom-call | flops 21474836480 | bytes 12582912 | tf_op jit(solution)/shard_map/attend_back/pallas_call | solution.py:216
  1020.5 19.8 %collective-permute-done.65.refs_1_ = bf16[2,4,128,256]{3,2,1,0:T(8,128)(2,1)S(1)} collective-permute-done((bf16[2,4,128,256]{3,2,1,0:T(8,128)(2,1)}, bf16[2,4,128,256]{3,2,1,0:T(8,128)(2,1)S(1)}, u32[]{:S(2)}, u32[]{:S(2)}) %collective-permute-start.65) | collective-permute-done | bytes 524320 | tf_op jit(solution)/shard_map/ppermute | solution.py:704
  1040.3 66.6 %collective-permute-done.66.refs_2_ = bf16[2,4,128,256]{3,2,1,0:T(8,128)(2,1)S(1)} collective-permute-done((bf16[2,4,128,256]{3,2,1,0:T(8,128)(2,1)}, bf16[2,4,128,256]{3,2,1,0:T(8,128)(2,1)S(1)}, u32[]{:S(2)}, u32[]{:S(2)}) %collective-permute-start.66) | collective-permute-done | bytes 524320 | tf_op jit(solution)/shard_map/ppermute | solution.py:704
  1224.5 17.5 fusion.10
  1260.9 23.0 %fusion.41 = bf16[1024,2048]{1,0:T(8,128)(2,1)S(1)} fusion(bf16[1024,4096]{1,0:T(8,128)(2,1)} %pad_maximum_fusion, bf16[2048,6144]{1,0:T(8,128)(2,1)} %all-gather.7.cloned.1.call-done), kind=kOutput, calls=%fused_computation.66 | convolution fusion | flops 17181966336 | bytes 29360128 | tf_op jit(solution)/shard_map/dot_general | solution.py:94
  1410.7 33.5 %attend_back.3 = (f32[2,4,128,512]{3,2,1,0:T(8,128)}, bf16[2,4,128,256]{3,2,1,0:T(8,128)(2,1)S(1)}, bf16[2,4,128,256]{3,2,1,0:T(8,128)(2,1)S(1)}, bf16[2,4,128,2...) custom-call(bf16[2,4,128,512]{3,2,1,0:T(8,128)(2,1)S(1)} %copy-done.40, bf16[2,4,128,512]{3,2,1,0:T(8,128)(2,1)} %bitcast.771, ...), custom_call_target="tpu_custom_call" | custom-call | flops 21474836480 | bytes 12582912 | tf_op jit(solution)/shard_map/attend_back/pallas_call | solution.py:216
  1486.8 20.1 %collective-permute-done.96.refs_1_ = bf16[2,4,128,256]{3,2,1,0:T(8,128)(2,1)S(1)} collective-permute-done((bf16[2,4,128,256]{3,2,1,0:T(8,128)(2,1)S(1)}, bf16[2,4,128,256]{3,2,1,0:T(8,128)(2,1)S(1)}, u32[]{:S(2)}, u32[]{:S(2)}) %collective-permute-start.96) | collective-permute-done | bytes 524320 | tf_op jit(solution)/shard_map/ppermute | solution.py:704
  1506.9 59.7 %collective-permute-done.97.refs_2_ = bf16[2,4,128,256]{3,2,1,0:T(8,128)(2,1)S(1)} collective-permute-done((bf16[2,4,128,256]{3,2,1,0:T(8,128)(2,1)S(1)}, bf16[2,4,128,256]{3,2,1,0:T(8,128)(2,1)S(1)}, u32[]{:S(2)}, u32[]{:S(2)}) %collective-permute-start.97) | collective-permute-done | bytes 524320 | tf_op jit(solution)/shard_map/ppermute | solution.py:704
  1695.3 18.6 %collective-permute-start.128 = (bf16[4,128,2048]{2,1,0:T(8,128)(2,1)S(1)}, bf16[4,128,2048]{2,1,0:T(8,128)(2,1)S(1)}, u32[]{:S(2)}, u32[]{:S(2)}) collective-permute-start(bf16[4,128,2048]{2,1,0:T(8,128)(2,1)S(1)} %copy-done.66), channel_id=1, source_target_pairs={{16,0},{17,1},{18,2},{19,3},{20,4},{21,5},{22,6},{23,7},{24,8},{25... | collective-permute-start | bytes 6291464 | tf_op jit(solution)/shard_map/ppermute | solution.py:737
  1794.0 16.1 assemble.6
  (1018 shorter events, 1055.1 us)
Async XLA Ops:
  7.2 88.9 %all-gather.5.cloned.1.call-start = ((), (), s32[]{:S(2)}) async-start(), calls=%async_computation.12 | async-start | bytes 5898240 | tf_op jit(solution)/shard_map/all_gather | solution.py:516
  15.1 307.3 %all-gather.7.cloned.1.call-start = ((), (), s32[]{:S(2)}) async-start(), calls=%async_computation.13 | async-start | bytes 28311552 | tf_op jit(solution)/shard_map/all_gather | solution.py:516
  35.2 380.1 %all-gather.9.cloned.1.call-start = ((), (), s32[]{:S(2)}) async-start(), calls=%async_computation.14 | async-start | bytes 5898240 | tf_op jit(solution)/shard_map/all_gather | solution.py:516
  35.9 628.5 %all-gather.11.cloned.1.call-start = ((), (), s32[]{:S(2)}) async-start(), calls=%async_computation.15 | async-start | bytes 28311552 | tf_op jit(solution)/shard_map/all_gather | solution.py:516
  100.2 111.6 %all-to-all-start = ((bf16[4,128,2048]{2,1,0:T(8,128)(2,1)}), bf16[4,128,2048]{2,1,0:T(8,128)(2,1)}, u32[]{:S(2)}, u32[]{:S(2)}) async-start(bf16[4,128,2048]{2,1,0:T(8,128)(2,1)} %all_to_all.32), calls=%async_computation | async-start | bytes 4194304 | tf_op jit(solution)/shard_map/all_to_all | solution.py:554
  116.0 64.9 %collective-permute-start.20 = (bf16[2,4,128,256]{3,2,1,0:T(8,128)(2,1)S(1)}, bf16[2,4,128,256]{3,2,1,0:T(8,128)(2,1)S(1)}, u32[]{:S(2)}, u32[]{:S(2)}) collective-permute-start(bf16[2,4,128,256]{3,2,1,0:T(8,128)(2,1)S(1)} %get-tuple-element.123.refs_0_), channel_id=1, source_target_pairs={{0,12},{1,13},{2,14},{3,15},{16,28},{17,29},{18,30},{19,31}} | collective-permute-start | bytes 1572872 | tf_op jit(solution)/shard_map/ppermute | solution.py:483
  422.7 129.2 %all-to-all-start.1 = ((bf16[4,128,2048]{2,1,0:T(8,128)(2,1)}), bf16[4,128,2048]{2,1,0:T(8,128)(2,1)}, u32[]{:S(2)}, u32[]{:S(2)}) async-start(bf16[4,128,2048]{2,1,0:T(8,128)(2,1)} %all_to_all.35), calls=%async_computation.1 | async-start | bytes 4194304 | tf_op jit(solution)/shard_map/all_to_all | solution.py:554
  427.1 526.4 %reduce-scatter.9.cloned.1.call-start = ((), (), s32[]{:S(2)}) async-start(), calls=%async_computation.16 | async-start | bytes 5242880 | tf_op jit(solution)/shard_map/reduce_scatter | solution.py:634
  637.8 63.4 %collective-permute-start.1 = (bf16[2,128,2048]{2,1,0:T(8,128)(2,1)}, bf16[2,128,2048]{2,1,0:T(8,128)(2,1)}, u32[]{:S(2)}, u32[]{:S(2)}) collective-permute-start(bf16[2,128,2048]{2,1,0:T(8,128)(2,1)} %pad_maximum_fusion.43), channel_id=1, source_target_pairs={{0,2},{1,3},{2,0},{3,1},{4,6},{5,7},{6,4},{7,5},{8,10},{9,11},{10,... | collective-permute-start | bytes 3145736 | tf_op jit(solution)/shard_map/ppermute | solution.py:25
  760.3 71.5 %collective-permute-start.64 = (bf16[1024,2048]{1,0:T(8,128)(2,1)}, bf16[1024,2048]{1,0:T(8,128)(2,1)}, u32[]{:S(2)}, u32[]{:S(2)}) collective-permute-start(bf16[1024,2048]{1,0:T(8,128)(2,1)} %convolution_convert_fusion.7), channel_id=1, source_target_pairs={{0,16},{16,0},{1,17},{17,1},{2,18},{18,2},{3,19},{19,3},{4,20},{20... | collective-permute-start | bytes 12582920 | tf_op jit(solution)/shard_map/ppermute | solution.py:626
  811.4 87.2 %collective-permute-start.63 = (bf16[1024,2048]{1,0:T(8,128)(2,1)}, bf16[1024,2048]{1,0:T(8,128)(2,1)}, u32[]{:S(2)}, u32[]{:S(2)}) collective-permute-start(bf16[1024,2048]{1,0:T(8,128)(2,1)} %convolution_convert_fusion.5), channel_id=1, source_target_pairs={{0,16},{16,0},{1,17},{17,1},{2,18},{18,2},{3,19},{19,3},{4,20},{20... | collective-permute-start | bytes 12582920 | tf_op jit(solution)/shard_map/ppermute | solution.py:626
  840.0 281.7 %reduce-scatter.11.cloned.1.call-start = ((), (), s32[]{:S(2)}) async-start(), calls=%async_computation.17 | async-start | bytes 5242880 | tf_op jit(solution)/shard_map/reduce_scatter | solution.py:634
  917.8 264.3 %reduce-scatter.13.cloned.1.call-start = ((), (), s32[]{:S(2)}) async-start(), calls=%async_computation.18 | async-start | bytes 5242880 | tf_op jit(solution)/shard_map/reduce_scatter | solution.py:634
  996.5 118.8 %collective-permute-start.72 = (bf16[2,128,2048]{2,1,0:T(8,128)(2,1)}, bf16[2,128,2048]{2,1,0:T(8,128)(2,1)}, u32[]{:S(2)}, u32[]{:S(2)}) collective-permute-start(bf16[2,128,2048]{2,1,0:T(8,128)(2,1)} %get-tuple-element.380), channel_id=1, source_target_pairs={{0,1},{1,0},{2,3},{3,2},{4,5},{5,4},{6,7},{7,6},{8,9},{9,8},{10,11... | collective-permute-start | bytes 3145736 | tf_op jit(solution)/shard_map/ppermute | solution.py:25
  998.1 108.8 %collective-permute-start.66 = (bf16[2,4,128,256]{3,2,1,0:T(8,128)(2,1)}, bf16[2,4,128,256]{3,2,1,0:T(8,128)(2,1)S(1)}, u32[]{:S(2)}, u32[]{:S(2)}) collective-permute-start(bf16[2,4,128,256]{3,2,1,0:T(8,128)(2,1)} %get-tuple-element.146), channel_id=1, source_target_pairs={{8,0},{12,4},{9,1},{13,5},{10,2},{14,6},{11,3},{15,7},{24,16},{28,... | collective-permute-start | bytes 1572872 | tf_op jit(solution)/shard_map/ppermute | solution.py:704
  1007.4 99.5 %collective-permute-start.67 = (bf16[2,4,128,256]{3,2,1,0:T(8,128)(2,1)}, bf16[2,4,128,256]{3,2,1,0:T(8,128)(2,1)S(1)}, u32[]{:S(2)}, u32[]{:S(2)}) collective-permute-start(bf16[2,4,128,256]{3,2,1,0:T(8,128)(2,1)} %get-tuple-element.147), channel_id=1, source_target_pairs={{12,0},{13,1},{14,2},{15,3},{28,16},{29,17},{30,18},{31,19}} | collective-permute-start | bytes 1572872 | tf_op jit(solution)/shard_map/ppermute | solution.py:704
  1010.8 108.0 %collective-permute-start.70 = (bf16[2,128,2048]{2,1,0:T(8,128)(2,1)}, bf16[2,128,2048]{2,1,0:T(8,128)(2,1)}, u32[]{:S(2)}, u32[]{:S(2)}) collective-permute-start(bf16[2,128,2048]{2,1,0:T(8,128)(2,1)} %pad_maximum_fusion.55), channel_id=1, source_target_pairs={{0,2},{1,3},{2,0},{3,1},{4,6},{5,7},{6,4},{7,5},{8,10},{9,11},{10,... | collective-permute-start | bytes 3145736 | tf_op jit(solution)/shard_map/ppermute | solution.py:25
  1016.1 105.6 %all-to-all-start.2 = ((bf16[4,64,2048]{2,1,0:T(8,128)(2,1)}), bf16[4,64,2048]{2,1,0:T(8,128)(2,1)}, u32[]{:S(2)}, u32[]{:S(2)}) async-start(bf16[4,64,2048]{2,1,0:T(8,128)(2,1)} %bitcast.721), calls=%async_computation.3 | async-start | bytes 2097152 | tf_op jit(solution)/shard_map/all_to_all | solution.py:685
  1020.5 315.8 %reduce-scatter.15.cloned.1.call-start = ((), (), s32[]{:S(2)}) async-start(), calls=%async_computation.19 | async-start | bytes 3604480 | tf_op jit(solution)/shard_map/reduce_scatter | solution.py:634
  1187.1 62.8 %collective-permute-start.87 = (bf16[1024,896]{1,0:T(8,128)(2,1)}, bf16[1024,896]{1,0:T(8,128)(2,1)}, u32[]{:S(2)}, u32[]{:S(2)}) collective-permute-start(bf16[1024,896]{1,0:T(8,128)(2,1)} %fusion.158), channel_id=1, source_target_pairs={{0,16},{16,0},{1,17},{17,1},{2,18},{18,2},{3,19},{19,3},{4,20},{20... | collective-permute-start | bytes 5505032 | tf_op jit(solution)/shard_map/ppermute | solution.py:626
  1218.8 74.4 %collective-permute-start.95 = (bf16[1024,2048]{1,0:T(8,128)(2,1)}, bf16[1024,2048]{1,0:T(8,128)(2,1)}, u32[]{:S(2)}, u32[]{:S(2)}) collective-permute-start(bf16[1024,2048]{1,0:T(8,128)(2,1)} %convolution_convert_fusion.4), channel_id=1, source_target_pairs={{0,16},{16,0},{1,17},{17,1},{2,18},{18,2},{3,19},{19,3},{4,20},{20... | collective-permute-start | bytes 12582920 | tf_op jit(solution)/shard_map/ppermute | solution.py:626
  1254.8 209.2 %reduce-scatter.17.cloned.1.call-start = ((), (), s32[]{:S(2)}) async-start(), calls=%async_computation.20 | async-start | bytes 5242880 | tf_op jit(solution)/shard_map/reduce_scatter | solution.py:634
  1302.6 306.3 %reduce-scatter.19.cloned.1.call-start = ((), (), s32[]{:S(2)}) async-start(), calls=%async_computation.21 | async-start | bytes 5242880 | tf_op jit(solution)/shard_map/reduce_scatter | solution.py:634
  1381.8 297.8 %reduce-scatter.21.cloned.1.call-start = ((), (), s32[]{:S(2)}) async-start(), calls=%async_computation.22 | async-start | bytes 5242880 | tf_op jit(solution)/shard_map/reduce_scatter | solution.py:634
  1399.5 68.6 %collective-permute-start.104 = (bf16[2,128,4096]{2,1,0:T(8,128)(2,1)}, bf16[2,128,4096]{2,1,0:T(8,128)(2,1)}, u32[]{:S(2)}, u32[]{:S(2)}) collective-permute-start(bf16[2,128,4096]{2,1,0:T(8,128)(2,1)} %maximum_bitcast_fusion.8), channel_id=1, source_target_pairs={{0,1},{1,0},{2,3},{3,2},{4,5},{5,4},{6,7},{7,6},{8,9},{9,8},{10,11... | collective-permute-start | bytes 6291464 | tf_op jit(solution)/shard_map/ppermute | solution.py:25
  1399.6 81.5 %collective-permute-start.103 = (bf16[2,128,4096]{2,1,0:T(8,128)(2,1)}, bf16[2,128,4096]{2,1,0:T(8,128)(2,1)}, u32[]{:S(2)}, u32[]{:S(2)}) collective-permute-start(bf16[2,128,4096]{2,1,0:T(8,128)(2,1)} %pad_maximum_fusion.28), channel_id=1, source_target_pairs={{0,2},{1,3},{2,0},{3,1},{4,6},{5,7},{6,4},{7,5},{8,10},{9,11},{10,... | collective-permute-start | bytes 6291464 | tf_op jit(solution)/shard_map/ppermute | solution.py:25
  1405.0 59.1 %all-to-all-start.3 = ((bf16[4,64,2048]{2,1,0:T(8,128)(2,1)}), bf16[4,64,2048]{2,1,0:T(8,128)(2,1)}, u32[]{:S(2)}, u32[]{:S(2)}) async-start(bf16[4,64,2048]{2,1,0:T(8,128)(2,1)} %bitcast.722), calls=%async_computation.7 | async-start | bytes 2097152 | tf_op jit(solution)/shard_map/all_to_all | solution.py:685
  1409.4 365.5 %reduce-scatter.23.cloned.1.call-start = ((), (), s32[]{:S(2)}) async-start(), calls=%async_computation.23 | async-start | bytes 3604480 | tf_op jit(solution)/shard_map/reduce_scatter | solution.py:634
  1474.4 92.2 %collective-permute-start.97 = (bf16[2,4,128,256]{3,2,1,0:T(8,128)(2,1)S(1)}, bf16[2,4,128,256]{3,2,1,0:T(8,128)(2,1)S(1)}, u32[]{:S(2)}, u32[]{:S(2)}) collective-permute-start(bf16[2,4,128,256]{3,2,1,0:T(8,128)(2,1)S(1)} %copy-done.31), channel_id=1, source_target_pairs={{8,0},{12,4},{9,1},{13,5},{10,2},{14,6},{11,3},{15,7},{24,16},{28,... | collective-permute-start | bytes 1572872 | tf_op jit(solution)/shard_map/ppermute | solution.py:704
  1477.7 88.9 %collective-permute-start.98 = (bf16[2,4,128,256]{3,2,1,0:T(8,128)(2,1)S(1)}, bf16[2,4,128,256]{3,2,1,0:T(8,128)(2,1)S(1)}, u32[]{:S(2)}, u32[]{:S(2)}) collective-permute-start(bf16[2,4,128,256]{3,2,1,0:T(8,128)(2,1)S(1)} %copy-done.29), channel_id=1, source_target_pairs={{12,0},{13,1},{14,2},{15,3},{28,16},{29,17},{30,18},{31,19}} | collective-permute-start | bytes 1572872 | tf_op jit(solution)/shard_map/ppermute | solution.py:704
  1479.4 95.3 %collective-permute-start.102 = (bf16[2,128,2048]{2,1,0:T(8,128)(2,1)S(1)}, bf16[2,128,2048]{2,1,0:T(8,128)(2,1)S(1)}, u32[]{:S(2)}, u32[]{:S(2)}) collective-permute-start(bf16[2,128,2048]{2,1,0:T(8,128)(2,1)S(1)} %get-tuple-element.359), channel_id=1, source_target_pairs={{0,1},{1,0},{2,3},{3,2},{4,5},{5,4},{6,7},{7,6},{8,9},{9,8},{10,11... | collective-permute-start | bytes 3145736 | tf_op jit(solution)/shard_map/ppermute | solution.py:25
  1481.0 95.5 %collective-permute-start.100 = (bf16[2,128,2048]{2,1,0:T(8,128)(2,1)S(1)}, bf16[2,128,2048]{2,1,0:T(8,128)(2,1)S(1)}, u32[]{:S(2)}, u32[]{:S(2)}) collective-permute-start(bf16[2,128,2048]{2,1,0:T(8,128)(2,1)S(1)} %pad_maximum_fusion.60), channel_id=1, source_target_pairs={{0,2},{1,3},{2,0},{3,1},{4,6},{5,7},{6,4},{7,5},{8,10},{9,11},{10,... | collective-permute-start | bytes 3145736 | tf_op jit(solution)/shard_map/ppermute | solution.py:25
  (316 other events, 5610.4 us)
Sparse Core Ops, SparseCore 0:
  15.2 58.6 all-gather.4
  76.1 246.2 all-gather.6
  324.6 71.3 all-gather.8
  398.1 246.1 all-gather.10
  840.1 113.4 reduce-scatter.8
  955.8 95.2 reduce-scatter.10
  1053.4 93.2 reduce-scatter.12
  1255.0 52.6 reduce-scatter.14
  1310.1 76.8 reduce-scatter.16
  1389.6 77.2 reduce-scatter.18
  1469.3 114.2 reduce-scatter.20
  1649.9 60.3 reduce-scatter.22

commit v7 on v6

--- a/solution.py
+++ b/solution.py
@@ -658,12 +658,13 @@
         sig = jax.nn.sigmoid(gate)
         grad_gate = (grad_hidden * up * (sig * (1.0 + gate * (1.0 - sig)))).astype(bf16)
         grad_up = (grad_hidden * (gate * sig)).astype(bf16)
-        grad_pre = jnp.concatenate([grad_gate, grad_up], axis=1)
         part_down = finish(gm_all, sent_down)
         if last:
-            grad_pre, *ffn_state = together(grad_pre, *ffn_state)
+            grad_gate, grad_up, *ffn_state = together(grad_gate, grad_up, *ffn_state)
         own_down = collect(part_down)
-        db = blocks(times_back(grad_pre, ffn_all[layer]).astype(bf16))
+        weight_gate, weight_up = ffn_all[layer][:, :ff_width], ffn_all[layer][:, ff_width:]
+        db = times_back(grad_gate, weight_gate) + times_back(grad_up, weight_up)
+        db = blocks(db.astype(bf16))
         db, grad_gate, grad_up = together(db, grad_gate, grad_up)
         db = plane_reduce(db)
         sent_gate, finish_gate = core_product(flat(b_all), grad_gate)

time: 1870 us -> 1880 us (level)
    dot_general x6 -> x8, matrix products: 90.7 us -> 99 us  [times_back(): lax.dot_general(left, weight, (((1,), (1,)), ((), ())), preferred_element...]
    unnamed x389 -> x399, local copies, waits for them, and re-layouts: 55.3 us -> 53.5 us
where the time goes in v7:
time: 1880 us; the launch traced here: 1870 us
  waiting for transfers between devices  796 us (42%)
  matrix products  303 us (16%)
  starting transfers between devices  255 us (14%)
  Pallas kernels  201 us (11%)
  other arithmetic  164 us (9%)
  local copies, waits for them, and re-layouts  134 us (7%)
    ppermute x94, waiting for transfers between devices, partner(): return lax.ppermute(value, 'rep', [(i, i ^ bit) for i in range(count)])  427 us
    ppermute x6, waiting for transfers between devices, backward(): lax.ppermute(grad_kv[step], 'fsdp', [(i, i - step) for i in range(step, d...  173 us
    dot_general x20, matrix products, dot(): lax.dot_general(left, right, (((left_dim,), (right_dim,)), ((), ())), pre...  128 us
    ppermute x9, waiting for transfers between devices, back(): lax.ppermute(value, 'fsdp', [(i, i + step) for i in range(depth - step)])  113 us
    dot_general x8, matrix products, times_back(): lax.dot_general(left, weight, (((1,), (1,)), ((), ())), preferred_element...  99 us
    ppermute x94, starting transfers between devices, partner(): return lax.ppermute(value, 'rep', [(i, i ^ bit) for i in range(count)])  87.3 us
    dot_general x6, matrix products, times(): return jnp.dot(left, weight, preferred_element_type=f32)  76.5 us
    pallas_call x2, Pallas kernels, attend_back(): pl.pallas_call(functools.partial(attend_back_kernel, len(keyvals)), grid=...  67.4 us
  transfers between devices with their start and end apart: 157, of which 70 were waited for; matrix products, arithmetic and copies ran while one was open for 29% of the time, Pallas kernels for 10%

profile of v7, /device:TPU:1, one launch (start us, length us, event | category | flops | bytes accessed | tf_op | source)
XLA Modules:
  0.0 1871.6 jit_solution(15436552352945130390)
XLA Ops:
  75.5 16.9 collective-permute-done.11
  119.7 16.0 collective-permute-done.18.refs_1_
  135.8 22.5 %collective-permute-done.19.refs_2_ = bf16[2,4,128,256]{3,2,1,0:T(8,128)(2,1)S(1)} collective-permute-done((bf16[2,4,128,256]{3,2,1,0:T(8,128)(2,1)S(1)}, bf16[2,4,128,256]{3,2,1,0:T(8,128)(2,1)S(1)}, u32[]{:S(2)}, u32[]{:S(2)}) %collective-permute-start.19) | collective-permute-done | bytes 524320 | tf_op jit(solution)/shard_map/ppermute | solution.py:483
  158.2 22.5 %collective-permute-done.20.refs_3_ = bf16[2,4,128,256]{3,2,1,0:T(8,128)(2,1)S(1)} collective-permute-done((bf16[2,4,128,256]{3,2,1,0:T(8,128)(2,1)S(1)}, bf16[2,4,128,256]{3,2,1,0:T(8,128)(2,1)S(1)}, u32[]{:S(2)}, u32[]{:S(2)}) %collective-permute-start.20) | collective-permute-done | bytes 524320 | tf_op jit(solution)/shard_map/ppermute | solution.py:483
  180.7 28.3 %attend.2 = (bf16[2,4,128,512]{3,2,1,0:T(8,128)(2,1)S(1)}, f32[4,8,256]{2,1,0:T(8,128)S(1)}) custom-call(bf16[2,4,128,512]{3,2,1,0:T(8,128)(2,1)S(1)} %get-tuple-element.123.query_ref, bf16[4,1024,256]{2,1,0:T(8,128)(2,1)} %pad_maximum_fusion.14.bias_ref, bf16[2,4,128,256]{3,2,1,0:T(8,128)(2,1)S(1)} %get-tuple-element.124.refs_0_, ...), custom_call_target="tpu_custom_call" | custom-call | flops 8589934592 | bytes 8388608 | tf_op jit(solution)/shard_map/attend/pallas_call | solution.py:199
  218.9 18.3 collective-permute-done.21
  265.3 21.1 %collective-permute-done.28 = bf16[2,128,2048]{2,1,0:T(8,128)(2,1)S(1)} collective-permute-done((bf16[2,128,2048]{2,1,0:T(8,128)(2,1)S(1)}, bf16[2,128,2048]{2,1,0:T(8,128)(2,1)S(1)}, u32[]{:S(2)}, u32[]{:S(2)}) %collective-permute-start.28) | collective-permute-done | bytes 1048608 | tf_op jit(solution)/shard_map/ppermute | solution.py:25
  289.3 33.1 %all-gather.7.cloned.1.call-done = bf16[2048,6144]{1,0:T(8,128)(2,1)} async-done(((bf16[256,6144]{1,0:T(8,128)(2,1)}), bf16[2048,6144]{1,0:T(8,128)(2,1)}) %all-gather.7.cloned.1.call-update) | async-done | bytes 25165840 | tf_op jit(solution)/shard_map/all_gather | solution.py:516
  322.4 21.9 %fusion.28 = bf16[1024,4096]{1,0:T(8,128)(2,1)S(1)} fusion(bf16[1024,2048]{1,0:T(8,128)(2,1)} %bitcast.643, bf16[2048,6144]{1,0:T(8,128)(2,1)} %all-gather.7.cloned.1.call-done), kind=kOutput, calls=%fused_computation.48 | convolution fusion | flops 17184063488 | bytes 29360128 | tf_op jit(solution)/shard_map/dot_general | solution.py:90
  363.8 21.2 %collective-permute-done.30 = bf16[2,128,2048]{2,1,0:T(8,128)(2,1)S(1)} collective-permute-done((bf16[2,128,2048]{2,1,0:T(8,128)(2,1)S(1)}, bf16[2,128,2048]{2,1,0:T(8,128)(2,1)S(1)}, u32[]{:S(2)}, u32[]{:S(2)}) %collective-permute-start.30) | collective-permute-done | bytes 1048608 | tf_op jit(solution)/shard_map/ppermute | solution.py:25
  475.2 21.5 %collective-permute-done.39.refs_2_ = bf16[2,4,128,256]{3,2,1,0:T(8,128)(2,1)S(1)} collective-permute-done((bf16[2,4,128,256]{3,2,1,0:T(8,128)(2,1)S(1)}, bf16[2,4,128,256]{3,2,1,0:T(8,128)(2,1)S(1)}, u32[]{:S(2)}, u32[]{:S(2)}) %collective-permute-start.39) | collective-permute-done | bytes 524320 | tf_op jit(solution)/shard_map/ppermute | solution.py:483
  496.7 22.5 %collective-permute-done.40.refs_3_ = bf16[2,4,128,256]{3,2,1,0:T(8,128)(2,1)S(1)} collective-permute-done((bf16[2,4,128,256]{3,2,1,0:T(8,128)(2,1)S(1)}, bf16[2,4,128,256]{3,2,1,0:T(8,128)(2,1)S(1)}, u32[]{:S(2)}, u32[]{:S(2)}) %collective-permute-start.40) | collective-permute-done | bytes 524320 | tf_op jit(solution)/shard_map/ppermute | solution.py:483
  519.2 28.5 %attend.3 = (bf16[2,4,128,512]{3,2,1,0:T(8,128)(2,1)S(1)}, f32[4,8,256]{2,1,0:T(8,128)S(1)}) custom-call(bf16[2,4,128,512]{3,2,1,0:T(8,128)(2,1)S(1)} %get-tuple-element.126.query_ref, bf16[4,1024,256]{2,1,0:T(8,128)(2,1)} %pad_maximum_fusion.14.bias_ref, bf16[2,4,128,256]{3,2,1,0:T(8,128)(2,1)S(1)} %get-tuple-element.127.refs_0_, ...), custom_call_target="tpu_custom_call" | custom-call | flops 8589934592 | bytes 8388608 | tf_op jit(solution)/shard_map/attend/pallas_call | solution.py:199
  614.1 21.5 %collective-permute-done = bf16[1,128,2048]{2,1,0:T(8,128)(2,1)} collective-permute-done((bf16[1,128,2048]{2,1,0:T(8,128)(2,1)S(1)}, bf16[1,128,2048]{2,1,0:T(8,128)(2,1)}, u32[]{:S(2)}, u32[]{:S(2)}) %collective-permute-start) | collective-permute-done | bytes 524320 | tf_op jit(solution)/shard_map/ppermute | solution.py:25
  641.2 16.9 collective-permute-done.48
  664.4 21.5 %fusion.31 = bf16[1024,4096]{1,0:T(8,128)(2,1)S(1)} fusion(bf16[1024,2048]{1,0:T(8,128)(2,1)} %bitcast.645, bf16[2048,6144]{1,0:T(8,128)(2,1)} %all-gather.11.cloned.1.call-done), kind=kOutput, calls=%fused_computation.49 | convolution fusion | flops 17184063488 | bytes 29360128 | tf_op jit(solution)/shard_map/dot_general | solution.py:90
  730.3 20.4 %collective-permute-start.53 = (bf16[256,2048]{1,0:T(8,128)(2,1)S(1)}, bf16[256,2048]{1,0:T(8,128)(2,1)S(1)}, u32[]{:S(2)}, u32[]{:S(2)}) collective-permute-start(bf16[256,2048]{1,0:T(8,128)(2,1)S(1)} %get-tuple-element.253), channel_id=1, source_target_pairs={{0,16},{16,0},{1,17},{17,1},{2,18},{18,2},{3,19},{19,3},{4,20},{20... | collective-permute-start | bytes 3145736 | tf_op jit(solution)/shard_map/ppermute | solution.py:793
  762.0 17.4 fusion.9
  816.2 16.1 collective-permute-done.54
  878.4 21.5 %collective-permute-done.61 = bf16[2,128,2048]{2,1,0:T(8,128)(2,1)S(1)} collective-permute-done((bf16[2,128,2048]{2,1,0:T(8,128)(2,1)S(1)}, bf16[2,128,2048]{2,1,0:T(8,128)(2,1)S(1)}, u32[]{:S(2)}, u32[]{:S(2)}) %collective-permute-start.61) | collective-permute-done | bytes 1048608 | tf_op jit(solution)/shard_map/ppermute | solution.py:25
  932.6 26.1 %reduce-scatter.9.cloned.1.call-done = bf16[256,2048]{1,0:T(8,128)(2,1)} async-done(((bf16[1024,2048]{1,0:T(8,128)(2,1)}), bf16[256,2048]{1,0:T(8,128)(2,1)}) %reduce-scatter.9.cloned.1.call-update) | async-done | bytes 1048592 | tf_op jit(solution)/shard_map/reduce_scatter | solution.py:634
  962.7 33.9 %attend_back.2 = (f32[2,4,128,512]{3,2,1,0:T(8,128)}, bf16[2,4,128,256]{3,2,1,0:T(8,128)(2,1)S(1)}, bf16[2,4,128,256]{3,2,1,0:T(8,128)(2,1)}, bf16[2,4,128,256]{3,2,1,0:T(8,128)(2,1)}, bf16[2,4,128,256]{3,2,1,0:T(8,128)(2,1)}) custom-call(bf16[2,4,128,512]{3,2,1,0:T(8,128)(2,1)S(1)} %copy-done.42, bf16[2,4,128,512]{3,2,1,0:T(8,128)(2,1)} %bitcast.775, ...), custom_call_target="tpu_custom_call" | custom-call | flops 21474836480 | bytes 12582912 | tf_op jit(solution)/shard_map/attend_back/pallas_call | solution.py:216
  1025.7 19.9 %collective-permute-done.65.refs_1_ = bf16[2,4,128,256]{3,2,1,0:T(8,128)(2,1)S(1)} collective-permute-done((bf16[2,4,128,256]{3,2,1,0:T(8,128)(2,1)}, bf16[2,4,128,256]{3,2,1,0:T(8,128)(2,1)S(1)}, u32[]{:S(2)}, u32[]{:S(2)}) %collective-permute-start.65) | collective-permute-done | bytes 524320 | tf_op jit(solution)/shard_map/ppermute | solution.py:705
  1045.5 67.0 %collective-permute-done.66.refs_2_ = bf16[2,4,128,256]{3,2,1,0:T(8,128)(2,1)S(1)} collective-permute-done((bf16[2,4,128,256]{3,2,1,0:T(8,128)(2,1)}, bf16[2,4,128,256]{3,2,1,0:T(8,128)(2,1)S(1)}, u32[]{:S(2)}, u32[]{:S(2)}) %collective-permute-start.66) | collective-permute-done | bytes 524320 | tf_op jit(solution)/shard_map/ppermute | solution.py:705
  1231.8 17.4 multiply_convert_fusion
  1418.9 33.5 %attend_back.3 = (f32[2,4,128,512]{3,2,1,0:T(8,128)}, bf16[2,4,128,256]{3,2,1,0:T(8,128)(2,1)S(1)}, bf16[2,4,128,256]{3,2,1,0:T(8,128)(2,1)S(1)}, bf16[2,4,128,2...) custom-call(bf16[2,4,128,512]{3,2,1,0:T(8,128)(2,1)S(1)} %copy-done.40, bf16[2,4,128,512]{3,2,1,0:T(8,128)(2,1)} %bitcast.774, ...), custom_call_target="tpu_custom_call" | custom-call | flops 21474836480 | bytes 12582912 | tf_op jit(solution)/shard_map/attend_back/pallas_call | solution.py:216
  1493.6 21.7 %collective-permute-done.96.refs_1_ = bf16[2,4,128,256]{3,2,1,0:T(8,128)(2,1)S(1)} collective-permute-done((bf16[2,4,128,256]{3,2,1,0:T(8,128)(2,1)S(1)}, bf16[2,4,128,256]{3,2,1,0:T(8,128)(2,1)S(1)}, u32[]{:S(2)}, u32[]{:S(2)}) %collective-permute-start.96) | collective-permute-done | bytes 524320 | tf_op jit(solution)/shard_map/ppermute | solution.py:705
  1515.3 64.9 %collective-permute-done.97.refs_2_ = bf16[2,4,128,256]{3,2,1,0:T(8,128)(2,1)S(1)} collective-permute-done((bf16[2,4,128,256]{3,2,1,0:T(8,128)(2,1)S(1)}, bf16[2,4,128,256]{3,2,1,0:T(8,128)(2,1)S(1)}, u32[]{:S(2)}, u32[]{:S(2)}) %collective-permute-start.97) | collective-permute-done | bytes 524320 | tf_op jit(solution)/shard_map/ppermute | solution.py:705
  1598.3 18.0 collective-permute-done.107
  1705.4 19.2 %collective-permute-start.128 = (bf16[4,128,2048]{2,1,0:T(8,128)(2,1)S(1)}, bf16[4,128,2048]{2,1,0:T(8,128)(2,1)S(1)}, u32[]{:S(2)}, u32[]{:S(2)}) collective-permute-start(bf16[4,128,2048]{2,1,0:T(8,128)(2,1)S(1)} %copy-done.66), channel_id=1, source_target_pairs={{16,0},{17,1},{18,2},{19,3},{20,4},{21,5},{22,6},{23,7},{24,8},{25... | collective-permute-start | bytes 6291464 | tf_op jit(solution)/shard_map/ppermute | solution.py:738
  1805.2 16.1 assemble.6
  1823.5 15.5 collective-permute-done.137
  (1029 shorter events, 1070.5 us)
Async XLA Ops:
  7.2 88.9 %all-gather.5.cloned.1.call-start = ((), (), s32[]{:S(2)}) async-start(), calls=%async_computation.12 | async-start | bytes 5898240 | tf_op jit(solution)/shard_map/all_gather | solution.py:516
  15.1 307.3 %all-gather.7.cloned.1.call-start = ((), (), s32[]{:S(2)}) async-start(), calls=%async_computation.13 | async-start | bytes 28311552 | tf_op jit(solution)/shard_map/all_gather | solution.py:516
  35.2 380.2 %all-gather.9.cloned.1.call-start = ((), (), s32[]{:S(2)}) async-start(), calls=%async_computation.14 | async-start | bytes 5898240 | tf_op jit(solution)/shard_map/all_gather | solution.py:516
  35.9 628.5 %all-gather.11.cloned.1.call-start = ((), (), s32[]{:S(2)}) async-start(), calls=%async_computation.15 | async-start | bytes 28311552 | tf_op jit(solution)/shard_map/all_gather | solution.py:516
  100.2 111.2 %all-to-all-start = ((bf16[4,128,2048]{2,1,0:T(8,128)(2,1)}), bf16[4,128,2048]{2,1,0:T(8,128)(2,1)}, u32[]{:S(2)}, u32[]{:S(2)}) async-start(bf16[4,128,2048]{2,1,0:T(8,128)(2,1)} %all_to_all.32), calls=%async_computation | async-start | bytes 4194304 | tf_op jit(solution)/shard_map/all_to_all | solution.py:554
  115.8 64.9 %collective-permute-start.20 = (bf16[2,4,128,256]{3,2,1,0:T(8,128)(2,1)S(1)}, bf16[2,4,128,256]{3,2,1,0:T(8,128)(2,1)S(1)}, u32[]{:S(2)}, u32[]{:S(2)}) collective-permute-start(bf16[2,4,128,256]{3,2,1,0:T(8,128)(2,1)S(1)} %get-tuple-element.124.refs_0_), channel_id=1, source_target_pairs={{0,12},{1,13},{2,14},{3,15},{16,28},{17,29},{18,30},{19,31}} | collective-permute-start | bytes 1572872 | tf_op jit(solution)/shard_map/ppermute | solution.py:483
  422.9 129.0 %all-to-all-start.1 = ((bf16[4,128,2048]{2,1,0:T(8,128)(2,1)}), bf16[4,128,2048]{2,1,0:T(8,128)(2,1)}, u32[]{:S(2)}, u32[]{:S(2)}) async-start(bf16[4,128,2048]{2,1,0:T(8,128)(2,1)} %all_to_all.35), calls=%async_computation.1 | async-start | bytes 4194304 | tf_op jit(solution)/shard_map/all_to_all | solution.py:554
  427.3 531.5 %reduce-scatter.9.cloned.1.call-start = ((), (), s32[]{:S(2)}) async-start(), calls=%async_computation.16 | async-start | bytes 5242880 | tf_op jit(solution)/shard_map/reduce_scatter | solution.py:634
  637.8 63.8 %collective-permute-start.1 = (bf16[2,128,2048]{2,1,0:T(8,128)(2,1)}, bf16[2,128,2048]{2,1,0:T(8,128)(2,1)}, u32[]{:S(2)}, u32[]{:S(2)}) collective-permute-start(bf16[2,128,2048]{2,1,0:T(8,128)(2,1)} %pad_maximum_fusion.42), channel_id=1, source_target_pairs={{0,2},{1,3},{2,0},{3,1},{4,6},{5,7},{6,4},{7,5},{8,10},{9,11},{10,... | collective-permute-start | bytes 3145736 | tf_op jit(solution)/shard_map/ppermute | solution.py:25
  760.5 76.6 %collective-permute-start.64 = (bf16[1024,2048]{1,0:T(8,128)(2,1)}, bf16[1024,2048]{1,0:T(8,128)(2,1)}, u32[]{:S(2)}, u32[]{:S(2)}) collective-permute-start(bf16[1024,2048]{1,0:T(8,128)(2,1)} %convolution_convert_fusion.7), channel_id=1, source_target_pairs={{0,16},{16,0},{1,17},{17,1},{2,18},{18,2},{3,19},{19,3},{4,20},{20... | collective-permute-start | bytes 12582920 | tf_op jit(solution)/shard_map/ppermute | solution.py:626
  816.2 87.8 %collective-permute-start.63 = (bf16[1024,2048]{1,0:T(8,128)(2,1)}, bf16[1024,2048]{1,0:T(8,128)(2,1)}, u32[]{:S(2)}, u32[]{:S(2)}) collective-permute-start(bf16[1024,2048]{1,0:T(8,128)(2,1)} %convolution_convert_fusion.5), channel_id=1, source_target_pairs={{0,16},{16,0},{1,17},{17,1},{2,18},{18,2},{3,19},{19,3},{4,20},{20... | collective-permute-start | bytes 12582920 | tf_op jit(solution)/shard_map/ppermute | solution.py:626
  845.1 282.2 %reduce-scatter.11.cloned.1.call-start = ((), (), s32[]{:S(2)}) async-start(), calls=%async_computation.17 | async-start | bytes 5242880 | tf_op jit(solution)/shard_map/reduce_scatter | solution.py:634
  855.0 59.3 %collective-permute-start.62 = (bf16[1024,2048]{1,0:T(8,128)(2,1)}, bf16[1024,2048]{1,0:T(8,128)(2,1)}, u32[]{:S(2)}, u32[]{:S(2)}) collective-permute-start(bf16[1024,2048]{1,0:T(8,128)(2,1)} %convolution_convert_fusion.6), channel_id=1, source_target_pairs={{0,16},{16,0},{1,17},{17,1},{2,18},{18,2},{3,19},{19,3},{4,20},{20... | collective-permute-start | bytes 12582920 | tf_op jit(solution)/shard_map/ppermute | solution.py:626
  923.5 267.1 %reduce-scatter.13.cloned.1.call-start = ((), (), s32[]{:S(2)}) async-start(), calls=%async_computation.18 | async-start | bytes 5242880 | tf_op jit(solution)/shard_map/reduce_scatter | solution.py:634
  1001.7 119.2 %collective-permute-start.72 = (bf16[2,128,2048]{2,1,0:T(8,128)(2,1)}, bf16[2,128,2048]{2,1,0:T(8,128)(2,1)}, u32[]{:S(2)}, u32[]{:S(2)}) collective-permute-start(bf16[2,128,2048]{2,1,0:T(8,128)(2,1)} %get-tuple-element.382), channel_id=1, source_target_pairs={{0,1},{1,0},{2,3},{3,2},{4,5},{5,4},{6,7},{7,6},{8,9},{9,8},{10,11... | collective-permute-start | bytes 3145736 | tf_op jit(solution)/shard_map/ppermute | solution.py:25
  1003.3 109.3 %collective-permute-start.66 = (bf16[2,4,128,256]{3,2,1,0:T(8,128)(2,1)}, bf16[2,4,128,256]{3,2,1,0:T(8,128)(2,1)S(1)}, u32[]{:S(2)}, u32[]{:S(2)}) collective-permute-start(bf16[2,4,128,256]{3,2,1,0:T(8,128)(2,1)} %get-tuple-element.147), channel_id=1, source_target_pairs={{8,0},{12,4},{9,1},{13,5},{10,2},{14,6},{11,3},{15,7},{24,16},{28,... | collective-permute-start | bytes 1572872 | tf_op jit(solution)/shard_map/ppermute | solution.py:705
  1012.6 100.0 %collective-permute-start.67 = (bf16[2,4,128,256]{3,2,1,0:T(8,128)(2,1)}, bf16[2,4,128,256]{3,2,1,0:T(8,128)(2,1)S(1)}, u32[]{:S(2)}, u32[]{:S(2)}) collective-permute-start(bf16[2,4,128,256]{3,2,1,0:T(8,128)(2,1)} %get-tuple-element.148), channel_id=1, source_target_pairs={{12,0},{13,1},{14,2},{15,3},{28,16},{29,17},{30,18},{31,19}} | collective-permute-start | bytes 1572872 | tf_op jit(solution)/shard_map/ppermute | solution.py:705
  1016.0 108.4 %collective-permute-start.70 = (bf16[2,128,2048]{2,1,0:T(8,128)(2,1)}, bf16[2,128,2048]{2,1,0:T(8,128)(2,1)}, u32[]{:S(2)}, u32[]{:S(2)}) collective-permute-start(bf16[2,128,2048]{2,1,0:T(8,128)(2,1)} %pad_maximum_fusion.54), channel_id=1, source_target_pairs={{0,2},{1,3},{2,0},{3,1},{4,6},{5,7},{6,4},{7,5},{8,10},{9,11},{10,... | collective-permute-start | bytes 3145736 | tf_op jit(solution)/shard_map/ppermute | solution.py:25
  1021.2 106.1 %all-to-all-start.2 = ((bf16[4,64,2048]{2,1,0:T(8,128)(2,1)}), bf16[4,64,2048]{2,1,0:T(8,128)(2,1)}, u32[]{:S(2)}, u32[]{:S(2)}) async-start(bf16[4,64,2048]{2,1,0:T(8,128)(2,1)} %bitcast.724), calls=%async_computation.3 | async-start | bytes 2097152 | tf_op jit(solution)/shard_map/all_to_all | solution.py:686
  1025.6 317.6 %reduce-scatter.15.cloned.1.call-start = ((), (), s32[]{:S(2)}) async-start(), calls=%async_computation.19 | async-start | bytes 3604480 | tf_op jit(solution)/shard_map/reduce_scatter | solution.py:634
  1226.8 73.8 %collective-permute-start.95 = (bf16[1024,2048]{1,0:T(8,128)(2,1)}, bf16[1024,2048]{1,0:T(8,128)(2,1)}, u32[]{:S(2)}, u32[]{:S(2)}) collective-permute-start(bf16[1024,2048]{1,0:T(8,128)(2,1)} %convolution_convert_fusion.4), channel_id=1, source_target_pairs={{0,16},{16,0},{1,17},{17,1},{2,18},{18,2},{3,19},{19,3},{4,20},{20... | collective-permute-start | bytes 12582920 | tf_op jit(solution)/shard_map/ppermute | solution.py:626
  1254.1 217.9 %reduce-scatter.17.cloned.1.call-start = ((), (), s32[]{:S(2)}) async-start(), calls=%async_computation.20 | async-start | bytes 5242880 | tf_op jit(solution)/shard_map/reduce_scatter | solution.py:634
  1309.3 321.2 %reduce-scatter.19.cloned.1.call-start = ((), (), s32[]{:S(2)}) async-start(), calls=%async_computation.21 | async-start | bytes 5242880 | tf_op jit(solution)/shard_map/reduce_scatter | solution.py:634
  1389.1 301.1 %reduce-scatter.21.cloned.1.call-start = ((), (), s32[]{:S(2)}) async-start(), calls=%async_computation.22 | async-start | bytes 5242880 | tf_op jit(solution)/shard_map/reduce_scatter | solution.py:634
  1405.8 68.7 %collective-permute-start.104 = (bf16[2,128,4096]{2,1,0:T(8,128)(2,1)}, bf16[2,128,4096]{2,1,0:T(8,128)(2,1)}, u32[]{:S(2)}, u32[]{:S(2)}) collective-permute-start(bf16[2,128,4096]{2,1,0:T(8,128)(2,1)} %maximum_bitcast_fusion.8), channel_id=1, source_target_pairs={{0,1},{1,0},{2,3},{3,2},{4,5},{5,4},{6,7},{7,6},{8,9},{9,8},{10,11... | collective-permute-start | bytes 6291464 | tf_op jit(solution)/shard_map/ppermute | solution.py:25
  1406.9 82.0 %collective-permute-start.103 = (bf16[2,128,4096]{2,1,0:T(8,128)(2,1)}, bf16[2,128,4096]{2,1,0:T(8,128)(2,1)}, u32[]{:S(2)}, u32[]{:S(2)}) collective-permute-start(bf16[2,128,4096]{2,1,0:T(8,128)(2,1)} %pad_maximum_fusion.27), channel_id=1, source_target_pairs={{0,2},{1,3},{2,0},{3,1},{4,6},{5,7},{6,4},{7,5},{8,10},{9,11},{10,... | collective-permute-start | bytes 6291464 | tf_op jit(solution)/shard_map/ppermute | solution.py:25
  1413.0 58.9 %all-to-all-start.3 = ((bf16[4,64,2048]{2,1,0:T(8,128)(2,1)}), bf16[4,64,2048]{2,1,0:T(8,128)(2,1)}, u32[]{:S(2)}, u32[]{:S(2)}) async-start(bf16[4,64,2048]{2,1,0:T(8,128)(2,1)} %bitcast.725), calls=%async_computation.7 | async-start | bytes 2097152 | tf_op jit(solution)/shard_map/all_to_all | solution.py:686
  1417.4 367.5 %reduce-scatter.23.cloned.1.call-start = ((), (), s32[]{:S(2)}) async-start(), calls=%async_computation.23 | async-start | bytes 3604480 | tf_op jit(solution)/shard_map/reduce_scatter | solution.py:634
  1481.5 98.6 %collective-permute-start.97 = (bf16[2,4,128,256]{3,2,1,0:T(8,128)(2,1)S(1)}, bf16[2,4,128,256]{3,2,1,0:T(8,128)(2,1)S(1)}, u32[]{:S(2)}, u32[]{:S(2)}) collective-permute-start(bf16[2,4,128,256]{3,2,1,0:T(8,128)(2,1)S(1)} %copy-done.31), channel_id=1, source_target_pairs={{8,0},{12,4},{9,1},{13,5},{10,2},{14,6},{11,3},{15,7},{24,16},{28,... | collective-permute-start | bytes 1572872 | tf_op jit(solution)/shard_map/ppermute | solution.py:705
  1486.1 94.1 %collective-permute-start.98 = (bf16[2,4,128,256]{3,2,1,0:T(8,128)(2,1)S(1)}, bf16[2,4,128,256]{3,2,1,0:T(8,128)(2,1)S(1)}, u32[]{:S(2)}, u32[]{:S(2)}) collective-permute-start(bf16[2,4,128,256]{3,2,1,0:T(8,128)(2,1)S(1)} %copy-done.29), channel_id=1, source_target_pairs={{12,0},{13,1},{14,2},{15,3},{28,16},{29,17},{30,18},{31,19}} | collective-permute-start | bytes 1572872 | tf_op jit(solution)/shard_map/ppermute | solution.py:705
  1487.8 100.5 %collective-permute-start.102 = (bf16[2,128,2048]{2,1,0:T(8,128)(2,1)S(1)}, bf16[2,128,2048]{2,1,0:T(8,128)(2,1)S(1)}, u32[]{:S(2)}, u32[]{:S(2)}) collective-permute-start(bf16[2,128,2048]{2,1,0:T(8,128)(2,1)S(1)} %get-tuple-element.361), channel_id=1, source_target_pairs={{0,1},{1,0},{2,3},{3,2},{4,5},{5,4},{6,7},{7,6},{8,9},{9,8},{10,11... | collective-permute-start | bytes 3145736 | tf_op jit(solution)/shard_map/ppermute | solution.py:25
  1488.9 101.2 %collective-permute-start.100 = (bf16[2,128,2048]{2,1,0:T(8,128)(2,1)S(1)}, bf16[2,128,2048]{2,1,0:T(8,128)(2,1)S(1)}, u32[]{:S(2)}, u32[]{:S(2)}) collective-permute-start(bf16[2,128,2048]{2,1,0:T(8,128)(2,1)S(1)} %pad_maximum_fusion.59), channel_id=1, source_target_pairs={{0,2},{1,3},{2,0},{3,1},{4,6},{5,7},{6,4},{7,5},{8,10},{9,11},{10,... | collective-permute-start | bytes 3145736 | tf_op jit(solution)/shard_map/ppermute | solution.py:25
  (321 other events, 5630.5 us)
Sparse Core Ops, SparseCore 0:
  15.2 58.6 all-gather.4
  76.1 246.2 all-gather.6
  324.1 71.3 all-gather.8
  397.6 246.1 all-gather.10
  845.2 113.5 reduce-scatter.8
  961.0 94.6 reduce-scatter.10
  1058.6 93.2 reduce-scatter.12
  1254.2 52.8 reduce-scatter.14
  1309.5 76.8 reduce-scatter.16
  1389.2 77.0 reduce-scatter.18
  1468.7 113.0 reduce-scatter.20
  1661.0 59.8 reduce-scatter.22

commit v8 on v6

--- a/solution.py
+++ b/solution.py
@@ -588,9 +588,10 @@
         scale_in = scale_of(layer_in)
         a_all = plane_gather((layer_in * scale_in * gain_attn).astype(bf16))
         query, keyval = project(a_all, qkv_all[layer], cosine, sine, q_width, k_width)
-        keyvals = [keyval] + [
-            back(keyval, step) for step in range(1, depth)
-        ]
+        keyvals = [keyval]
+        for step in range(1, depth):
+            pairs = [(i, i + 1) for i in range(step - 1, depth - 1)]
+            keyvals.append(lax.ppermute(keyvals[-1], "fsdp", pairs))
         mixed, log_total = attend(query, keyvals, bias)
         residual = layer_in + plane_reduce(blocks(times(flat(mixed), out_all[layer]).astype(bf16)))
         scale_mid = scale_of(residual)

time: 1870 us -> 1940 us (1.037)
  waiting for transfers between devices: 779 us -> 860 us
  starting transfers between devices: 266 us -> 230 us
    reduce_scatter x8, waiting for transfers between devices: 26.8 us -> 156 us  [collect(): return lax.psum_scatter(total, 'fsdp', scatter_dimension=0, tiled=True)]
    ppermute x9 -> x3, waiting for transfers between devices: 113 us -> 0.01 us  [back(): lax.ppermute(value, 'fsdp', [(i, i + step) for i in range(depth - step)])]
    ppermute x0 -> x6, waiting for transfers between devices: none -> 42.5 us  [forward(): keyvals.append(lax.ppermute(keyvals[-1], 'fsdp', pairs))]
    ppermute x9 -> x3, starting transfers between devices: 37.2 us -> 8.39 us  [back(): lax.ppermute(value, 'fsdp', [(i, i + step) for i in range(depth - step)])]
    ppermute x94, waiting for transfers between devices: 416 us -> 444 us  [partner(): return lax.ppermute(value, 'rep', [(i, i ^ bit) for i in range(count)])]
    ppermute x0 -> x6, starting transfers between devices: none -> 19.9 us  [forward(): keyvals.append(lax.ppermute(keyvals[-1], 'fsdp', pairs))]
    ppermute x6, waiting for transfers between devices: 166 us -> 147 us  [backward(): lax.ppermute(grad_kv[step], 'fsdp', [(i, i - step) for i in range(step, d...]
    unnamed x389 -> x401, local copies, waits for them, and re-layouts: 55.3 us -> 57.7 us
  transfers between devices with their start and end apart: 157 -> 157, of which waited for: 70 -> 65; matrix products, arithmetic and copies ran while one was open for 29% -> 28% of each run, Pallas kernels for 10% -> 10%
where the time goes in v8:
time: 1940 us; the launch traced here: 1920 us
  waiting for transfers between devices  860 us (44%)
  matrix products  290 us (15%)
  starting transfers between devices  230 us (12%)
  Pallas kernels  202 us (10%)
  other arithmetic  174 us (9%)
  local copies, waits for them, and re-layouts  148 us (8%)
    ppermute x94, waiting for transfers between devices, partner(): return lax.ppermute(value, 'rep', [(i, i ^ bit) for i in range(count)])  444 us
    reduce_scatter x8, waiting for transfers between devices, collect(): return lax.psum_scatter(total, 'fsdp', scatter_dimension=0, tiled=True)  156 us
    ppermute x6, waiting for transfers between devices, backward(): lax.ppermute(grad_kv[step], 'fsdp', [(i, i - step) for i in range(step, d...  147 us
    dot_general x20, matrix products, dot(): lax.dot_general(left, right, (((left_dim,), (right_dim,)), ((), ())), pre...  123 us
    dot_general x6, matrix products, times_back(): lax.dot_general(left, weight, (((1,), (1,)), ((), ())), preferred_element...  90.9 us
    ppermute x94, starting transfers between devices, partner(): return lax.ppermute(value, 'rep', [(i, i ^ bit) for i in range(count)])  79.5 us
    dot_general x6, matrix products, times(): return jnp.dot(left, weight, preferred_element_type=f32)  76.1 us
    pallas_call x2, Pallas kernels, attend_back(): pl.pallas_call(functools.partial(attend_back_kernel, len(keyvals)), grid=...  67.5 us
  transfers between devices with their start and end apart: 157, of which 65 were waited for; matrix products, arithmetic and copies ran while one was open for 28% of the time, Pallas kernels for 10%

profile of v8, /device:TPU:1, one launch (start us, length us, event | category | flops | bytes accessed | tf_op | source)
XLA Modules:
  0.0 1923.2 jit_solution(14280840600344089691)
XLA Ops:
  75.0 16.9 collective-permute-done.11
  105.7 22.0 %collective-permute-done.18.refs_1_ = bf16[2,4,128,256]{3,2,1,0:T(8,128)(2,1)S(1)} collective-permute-done((bf16[2,4,128,256]{3,2,1,0:T(8,128)(2,1)S(1)}, bf16[2,4,128,256]{3,2,1,0:T(8,128)(2,1)S(1)}, u32[]{:S(2)}, u32[]{:S(2)}) %collective-permute-start.18) | collective-permute-done | bytes 524320 | tf_op jit(solution)/shard_map/ppermute | solution.py:594
  145.3 28.3 %attend.2 = (bf16[2,4,128,512]{3,2,1,0:T(8,128)(2,1)S(1)}, f32[4,8,256]{2,1,0:T(8,128)S(1)}) custom-call(bf16[2,4,128,512]{3,2,1,0:T(8,128)(2,1)S(1)} %copy-done.40, bf16[4,1024,256]{2,1,0:T(8,128)(2,1)} %pad_maximum_fusion.15.bias_ref, bf16[2,4,128,256]{3,2,1,0:T(8,128)(2,1)S(1)} %get-tuple-element.123.refs_0_, ...), custom_call_target="tpu_custom_call" | custom-call | flops 8589934592 | bytes 8388608 | tf_op jit(solution)/shard_map/attend/pallas_call | solution.py:199
  182.0 18.6 collective-permute-done.21
  228.7 20.9 %collective-permute-done.28 = bf16[2,128,2048]{2,1,0:T(8,128)(2,1)S(1)} collective-permute-done((bf16[2,128,2048]{2,1,0:T(8,128)(2,1)S(1)}, bf16[2,128,2048]{2,1,0:T(8,128)(2,1)S(1)}, u32[]{:S(2)}, u32[]{:S(2)}) %collective-permute-start.28) | collective-permute-done | bytes 1048608 | tf_op jit(solution)/shard_map/ppermute | solution.py:25
  252.6 47.5 %all-gather.7.cloned.1.call-done = bf16[2048,6144]{1,0:T(8,128)(2,1)} async-done(((bf16[256,6144]{1,0:T(8,128)(2,1)}), bf16[2048,6144]{1,0:T(8,128)(2,1)}) %all-gather.7.cloned.1.call-update) | async-done | bytes 25165840 | tf_op jit(solution)/shard_map/all_gather | solution.py:516
  300.1 21.7 %fusion.27 = bf16[1024,4096]{1,0:T(8,128)(2,1)S(1)} fusion(bf16[1024,2048]{1,0:T(8,128)(2,1)} %bitcast.640, bf16[2048,6144]{1,0:T(8,128)(2,1)} %all-gather.7.cloned.1.call-done), kind=kOutput, calls=%fused_computation.46 | convolution fusion | flops 17184063488 | bytes 29360128 | tf_op jit(solution)/shard_map/dot_general | solution.py:90
  341.1 21.4 %collective-permute-done.30 = bf16[2,128,2048]{2,1,0:T(8,128)(2,1)S(1)} collective-permute-done((bf16[2,128,2048]{2,1,0:T(8,128)(2,1)S(1)}, bf16[2,128,2048]{2,1,0:T(8,128)(2,1)S(1)}, u32[]{:S(2)}, u32[]{:S(2)}) %collective-permute-start.30) | collective-permute-done | bytes 1048608 | tf_op jit(solution)/shard_map/ppermute | solution.py:25
  395.5 16.3 collective-permute-done.37
  421.0 15.3 collective-permute-start.38
  437.2 20.6 %collective-permute-done.38.refs_1_ = bf16[2,4,128,256]{3,2,1,0:T(8,128)(2,1)S(1)} collective-permute-done((bf16[2,4,128,256]{3,2,1,0:T(8,128)(2,1)S(1)}, bf16[2,4,128,256]{3,2,1,0:T(8,128)(2,1)S(1)}, u32[]{:S(2)}, u32[]{:S(2)}) %collective-permute-start.38) | collective-permute-done | bytes 524320 | tf_op jit(solution)/shard_map/ppermute | solution.py:594
  476.3 28.7 %attend.3 = (bf16[2,4,128,512]{3,2,1,0:T(8,128)(2,1)S(1)}, f32[4,8,256]{2,1,0:T(8,128)S(1)}) custom-call(bf16[2,4,128,512]{3,2,1,0:T(8,128)(2,1)S(1)} %copy-done.43, bf16[4,1024,256]{2,1,0:T(8,128)(2,1)} %pad_maximum_fusion.15.bias_ref, bf16[2,4,128,256]{3,2,1,0:T(8,128)(2,1)S(1)} %copy-done.18, bf16[2,4,128,256]{3,2,1,0:T(8,128)(2,1)S(1)} %copy-done.21, ...), custom_call_target="tpu_custom_call" | custom-call | flops 8589934592 | bytes 8388608 | tf_op jit(solution)/shard_map/attend/pallas_call | solution.py:199
  516.6 15.1 collective-permute-done.41
  568.7 16.8 collective-permute-done
  590.7 17.2 collective-permute-done.48
  614.4 21.5 %fusion.30 = bf16[1024,4096]{1,0:T(8,128)(2,1)S(1)} fusion(bf16[1024,2048]{1,0:T(8,128)(2,1)} %bitcast.642, bf16[2048,6144]{1,0:T(8,128)(2,1)} %all-gather.11.cloned.1.call-done), kind=kOutput, calls=%fused_computation.47 | convolution fusion | flops 17184063488 | bytes 29360128 | tf_op jit(solution)/shard_map/dot_general | solution.py:90
  682.8 15.4 collective-permute-start.53
  709.7 17.5 fusion.13
  727.2 22.8 %fusion.50 = bf16[1024,2048]{1,0:T(8,128)(2,1)S(1)} fusion(bf16[2048,6144]{1,0:T(8,128)(2,1)} %all-gather.11.cloned.1.call-done, bf16[1024,2048]{1,0:T(8,128)(2,1)} %get-tuple-element.133, bf16[1024,2048]{1,0:T(8,128)(2,1)} %get-tuple-element.132), kind=kOutput, calls=%fused_computation.77 | convolution fusion | flops 17198743552 | bytes 29360128 | tf_op jit(solution)/shard_map/dot_general | solution.py:94
  759.6 15.6 collective-permute-done.54
  817.2 21.9 %collective-permute-done.61 = bf16[2,128,2048]{2,1,0:T(8,128)(2,1)S(1)} collective-permute-done((bf16[2,128,2048]{2,1,0:T(8,128)(2,1)S(1)}, bf16[2,128,2048]{2,1,0:T(8,128)(2,1)S(1)}, u32[]{:S(2)}, u32[]{:S(2)}) %collective-permute-start.61) | collective-permute-done | bytes 1048608 | tf_op jit(solution)/shard_map/ppermute | solution.py:25
  871.6 155.9 %reduce-scatter.9.cloned.1.call-done = bf16[256,2048]{1,0:T(8,128)(2,1)} async-done(((bf16[1024,2048]{1,0:T(8,128)(2,1)}), bf16[256,2048]{1,0:T(8,128)(2,1)}) %reduce-scatter.9.cloned.1.call-update) | async-done | bytes 1048592 | tf_op jit(solution)/shard_map/reduce_scatter | solution.py:635
  1031.5 34.0 %attend_back.2 = (f32[2,4,128,512]{3,2,1,0:T(8,128)}, bf16[2,4,128,256]{3,2,1,0:T(8,128)(2,1)S(1)}, bf16[2,4,128,256]{3,2,1,0:T(8,128)(2,1)}, bf16[2,4,128,256]{3,2,1,0:T(8,128)(2,1)}, bf16[2,4,128,256]{3,2,1,0:T(8,128)(2,1)}) custom-call(bf16[2,4,128,512]{3,2,1,0:T(8,128)(2,1)S(1)} %copy-done.44, bf16[2,4,128,512]{3,2,1,0:T(8,128)(2,1)} %bitcast.767, ...), custom_call_target="tpu_custom_call" | custom-call | flops 21474836480 | bytes 12582912 | tf_op jit(solution)/shard_map/attend_back/pallas_call | solution.py:216
  1108.5 43.1 %collective-permute-done.66.refs_2_ = bf16[2,4,128,256]{3,2,1,0:T(8,128)(2,1)S(1)} collective-permute-done((bf16[2,4,128,256]{3,2,1,0:T(8,128)(2,1)}, bf16[2,4,128,256]{3,2,1,0:T(8,128)(2,1)S(1)}, u32[]{:S(2)}, u32[]{:S(2)}) %collective-permute-start.66) | collective-permute-done | bytes 524320 | tf_op jit(solution)/shard_map/ppermute | solution.py:705
  1277.1 17.5 fusion.10
  1313.9 23.0 %fusion.41 = bf16[1024,2048]{1,0:T(8,128)(2,1)S(1)} fusion(bf16[1024,4096]{1,0:T(8,128)(2,1)} %pad_maximum_fusion, bf16[2048,6144]{1,0:T(8,128)(2,1)} %all-gather.7.cloned.1.call-done), kind=kOutput, calls=%fused_computation.66 | convolution fusion | flops 17181966336 | bytes 29360128 | tf_op jit(solution)/shard_map/dot_general | solution.py:94
  1467.7 33.5 %attend_back.3 = (f32[2,4,128,512]{3,2,1,0:T(8,128)}, bf16[2,4,128,256]{3,2,1,0:T(8,128)(2,1)S(1)}, bf16[2,4,128,256]{3,2,1,0:T(8,128)(2,1)S(1)}, bf16[2,4,128,2...) custom-call(bf16[2,4,128,512]{3,2,1,0:T(8,128)(2,1)S(1)} %copy-done.41, bf16[2,4,128,512]{3,2,1,0:T(8,128)(2,1)} %bitcast.766, ...), custom_call_target="tpu_custom_call" | custom-call | flops 21474836480 | bytes 12582912 | tf_op jit(solution)/shard_map/attend_back/pallas_call | solution.py:216
  1542.9 20.8 %collective-permute-done.96.refs_1_ = bf16[2,4,128,256]{3,2,1,0:T(8,128)(2,1)S(1)} collective-permute-done((bf16[2,4,128,256]{3,2,1,0:T(8,128)(2,1)S(1)}, bf16[2,4,128,256]{3,2,1,0:T(8,128)(2,1)S(1)}, u32[]{:S(2)}, u32[]{:S(2)}) %collective-permute-start.96) | collective-permute-done | bytes 524320 | tf_op jit(solution)/shard_map/ppermute | solution.py:705
  1563.6 68.8 %collective-permute-done.97.refs_2_ = bf16[2,4,128,256]{3,2,1,0:T(8,128)(2,1)S(1)} collective-permute-done((bf16[2,4,128,256]{3,2,1,0:T(8,128)(2,1)S(1)}, bf16[2,4,128,256]{3,2,1,0:T(8,128)(2,1)S(1)}, u32[]{:S(2)}, u32[]{:S(2)}) %collective-permute-start.97) | collective-permute-done | bytes 524320 | tf_op jit(solution)/shard_map/ppermute | solution.py:705
  1650.6 17.9 collective-permute-done.107
  1756.9 19.7 %collective-permute-start.128 = (bf16[4,128,2048]{2,1,0:T(8,128)(2,1)}, bf16[4,128,2048]{2,1,0:T(8,128)(2,1)}, u32[]{:S(2)}, u32[]{:S(2)}) collective-permute-start(bf16[4,128,2048]{2,1,0:T(8,128)(2,1)} %pad_maximum_fusion.33.refs_0_), channel_id=1, source_target_pairs={{16,0},{17,1},{18,2},{19,3},{20,4},{21,5},{22,6},{23,7},{24,8},{25... | collective-permute-start | bytes 6291464 | tf_op jit(solution)/shard_map/ppermute | solution.py:738
  1856.9 16.2 assemble.6
  (1029 shorter events, 1013.0 us)
Async XLA Ops:
  7.2 88.3 %all-gather.5.cloned.1.call-start = ((), (), s32[]{:S(2)}) async-start(), calls=%async_computation.12 | async-start | bytes 5898240 | tf_op jit(solution)/shard_map/all_gather | solution.py:516
  15.1 284.9 %all-gather.7.cloned.1.call-start = ((), (), s32[]{:S(2)}) async-start(), calls=%async_computation.13 | async-start | bytes 28311552 | tf_op jit(solution)/shard_map/all_gather | solution.py:516
  35.2 357.6 %all-gather.9.cloned.1.call-start = ((), (), s32[]{:S(2)}) async-start(), calls=%async_computation.14 | async-start | bytes 5898240 | tf_op jit(solution)/shard_map/all_gather | solution.py:516
  35.9 578.5 %all-gather.11.cloned.1.call-start = ((), (), s32[]{:S(2)}) async-start(), calls=%async_computation.15 | async-start | bytes 28311552 | tf_op jit(solution)/shard_map/all_gather | solution.py:516
  470.3 557.2 %reduce-scatter.9.cloned.1.call-start = ((), (), s32[]{:S(2)}) async-start(), calls=%async_computation.16 | async-start | bytes 5242880 | tf_op jit(solution)/shard_map/reduce_scatter | solution.py:635
  587.8 64.3 %collective-permute-start.1 = (bf16[2,128,2048]{2,1,0:T(8,128)(2,1)}, bf16[2,128,2048]{2,1,0:T(8,128)(2,1)}, u32[]{:S(2)}, u32[]{:S(2)}) collective-permute-start(bf16[2,128,2048]{2,1,0:T(8,128)(2,1)} %pad_maximum_fusion.43), channel_id=1, source_target_pairs={{0,2},{1,3},{2,0},{3,1},{4,6},{5,7},{6,4},{7,5},{8,10},{9,11},{10,... | collective-permute-start | bytes 3145736 | tf_op jit(solution)/shard_map/ppermute | solution.py:25
  708.2 70.9 %collective-permute-start.64 = (bf16[1024,2048]{1,0:T(8,128)(2,1)}, bf16[1024,2048]{1,0:T(8,128)(2,1)}, u32[]{:S(2)}, u32[]{:S(2)}) collective-permute-start(bf16[1024,2048]{1,0:T(8,128)(2,1)} %convolution_convert_fusion.7), channel_id=1, source_target_pairs={{0,16},{16,0},{1,17},{17,1},{2,18},{18,2},{3,19},{19,3},{4,20},{20... | collective-permute-start | bytes 12582920 | tf_op jit(solution)/shard_map/ppermute | solution.py:627
  759.5 82.8 %collective-permute-start.63 = (bf16[1024,2048]{1,0:T(8,128)(2,1)}, bf16[1024,2048]{1,0:T(8,128)(2,1)}, u32[]{:S(2)}, u32[]{:S(2)}) collective-permute-start(bf16[1024,2048]{1,0:T(8,128)(2,1)} %convolution_convert_fusion.5), channel_id=1, source_target_pairs={{0,16},{16,0},{1,17},{17,1},{2,18},{18,2},{3,19},{19,3},{4,20},{20... | collective-permute-start | bytes 12582920 | tf_op jit(solution)/shard_map/ppermute | solution.py:627
  788.3 379.3 %reduce-scatter.11.cloned.1.call-start = ((), (), s32[]{:S(2)}) async-start(), calls=%async_computation.17 | async-start | bytes 5242880 | tf_op jit(solution)/shard_map/reduce_scatter | solution.py:635
  797.9 54.4 %collective-permute-start.62 = (bf16[1024,2048]{1,0:T(8,128)(2,1)}, bf16[1024,2048]{1,0:T(8,128)(2,1)}, u32[]{:S(2)}, u32[]{:S(2)}) collective-permute-start(bf16[1024,2048]{1,0:T(8,128)(2,1)} %convolution_convert_fusion.6), channel_id=1, source_target_pairs={{0,16},{16,0},{1,17},{17,1},{2,18},{18,2},{3,19},{19,3},{4,20},{20... | collective-permute-start | bytes 12582920 | tf_op jit(solution)/shard_map/ppermute | solution.py:627
  862.6 372.0 %reduce-scatter.13.cloned.1.call-start = ((), (), s32[]{:S(2)}) async-start(), calls=%async_computation.18 | async-start | bytes 5242880 | tf_op jit(solution)/shard_map/reduce_scatter | solution.py:635
  1070.5 90.6 %collective-permute-start.72 = (bf16[2,128,2048]{2,1,0:T(8,128)(2,1)}, bf16[2,128,2048]{2,1,0:T(8,128)(2,1)}, u32[]{:S(2)}, u32[]{:S(2)}) collective-permute-start(bf16[2,128,2048]{2,1,0:T(8,128)(2,1)} %get-tuple-element.380), channel_id=1, source_target_pairs={{0,1},{1,0},{2,3},{3,2},{4,5},{5,4},{6,7},{7,6},{8,9},{9,8},{10,11... | collective-permute-start | bytes 3145736 | tf_op jit(solution)/shard_map/ppermute | solution.py:25
  1072.2 79.5 %collective-permute-start.66 = (bf16[2,4,128,256]{3,2,1,0:T(8,128)(2,1)}, bf16[2,4,128,256]{3,2,1,0:T(8,128)(2,1)S(1)}, u32[]{:S(2)}, u32[]{:S(2)}) collective-permute-start(bf16[2,4,128,256]{3,2,1,0:T(8,128)(2,1)} %get-tuple-element.146), channel_id=1, source_target_pairs={{8,0},{12,4},{9,1},{13,5},{10,2},{14,6},{11,3},{15,7},{24,16},{28,... | collective-permute-start | bytes 1572872 | tf_op jit(solution)/shard_map/ppermute | solution.py:705
  1081.6 70.1 %collective-permute-start.67 = (bf16[2,4,128,256]{3,2,1,0:T(8,128)(2,1)}, bf16[2,4,128,256]{3,2,1,0:T(8,128)(2,1)}, u32[]{:S(2)}, u32[]{:S(2)}) collective-permute-start(bf16[2,4,128,256]{3,2,1,0:T(8,128)(2,1)} %get-tuple-element.147), channel_id=1, source_target_pairs={{12,0},{13,1},{14,2},{15,3},{28,16},{29,17},{30,18},{31,19}} | collective-permute-start | bytes 1572872 | tf_op jit(solution)/shard_map/ppermute | solution.py:705
  1084.9 79.8 %collective-permute-start.70 = (bf16[2,128,2048]{2,1,0:T(8,128)(2,1)}, bf16[2,128,2048]{2,1,0:T(8,128)(2,1)}, u32[]{:S(2)}, u32[]{:S(2)}) collective-permute-start(bf16[2,128,2048]{2,1,0:T(8,128)(2,1)} %pad_maximum_fusion.55), channel_id=1, source_target_pairs={{0,2},{1,3},{2,0},{3,1},{4,6},{5,7},{6,4},{7,5},{8,10},{9,11},{10,... | collective-permute-start | bytes 3145736 | tf_op jit(solution)/shard_map/ppermute | solution.py:25
  1090.2 77.3 %all-to-all-start.2 = ((bf16[4,64,2048]{2,1,0:T(8,128)(2,1)}), bf16[4,64,2048]{2,1,0:T(8,128)(2,1)}, u32[]{:S(2)}, u32[]{:S(2)}) async-start(bf16[4,64,2048]{2,1,0:T(8,128)(2,1)} %bitcast.717), calls=%async_computation.3 | async-start | bytes 2097152 | tf_op jit(solution)/shard_map/all_to_all | solution.py:686
  1094.5 296.2 %reduce-scatter.15.cloned.1.call-start = ((), (), s32[]{:S(2)}) async-start(), calls=%async_computation.19 | async-start | bytes 3604480 | tf_op jit(solution)/shard_map/reduce_scatter | solution.py:635
  1239.3 63.3 %collective-permute-start.87 = (bf16[1024,896]{1,0:T(8,128)(2,1)}, bf16[1024,896]{1,0:T(8,128)(2,1)}, u32[]{:S(2)}, u32[]{:S(2)}) collective-permute-start(bf16[1024,896]{1,0:T(8,128)(2,1)} %fusion.158), channel_id=1, source_target_pairs={{0,16},{16,0},{1,17},{17,1},{2,18},{18,2},{3,19},{19,3},{4,20},{20... | collective-permute-start | bytes 5505032 | tf_op jit(solution)/shard_map/ppermute | solution.py:627
  1272.4 75.0 %collective-permute-start.95 = (bf16[1024,2048]{1,0:T(8,128)(2,1)}, bf16[1024,2048]{1,0:T(8,128)(2,1)}, u32[]{:S(2)}, u32[]{:S(2)}) collective-permute-start(bf16[1024,2048]{1,0:T(8,128)(2,1)} %convolution_convert_fusion.4), channel_id=1, source_target_pairs={{0,16},{16,0},{1,17},{17,1},{2,18},{18,2},{3,19},{19,3},{4,20},{20... | collective-permute-start | bytes 12582920 | tf_op jit(solution)/shard_map/ppermute | solution.py:627
  1307.4 213.3 %reduce-scatter.17.cloned.1.call-start = ((), (), s32[]{:S(2)}) async-start(), calls=%async_computation.20 | async-start | bytes 5242880 | tf_op jit(solution)/shard_map/reduce_scatter | solution.py:635
  1343.4 51.5 %collective-permute-start.93 = (bf16[1024,2048]{1,0:T(8,128)(2,1)}, bf16[1024,2048]{1,0:T(8,128)(2,1)}, u32[]{:S(2)}, u32[]{:S(2)}) collective-permute-start(bf16[1024,2048]{1,0:T(8,128)(2,1)} %convolution_convert_fusion.2), channel_id=1, source_target_pairs={{0,16},{16,0},{1,17},{17,1},{2,18},{18,2},{3,19},{19,3},{4,20},{20... | collective-permute-start | bytes 12582920 | tf_op jit(solution)/shard_map/ppermute | solution.py:627
  1355.7 325.9 %reduce-scatter.19.cloned.1.call-start = ((), (), s32[]{:S(2)}) async-start(), calls=%async_computation.21 | async-start | bytes 5242880 | tf_op jit(solution)/shard_map/reduce_scatter | solution.py:635
  1437.7 304.0 %reduce-scatter.21.cloned.1.call-start = ((), (), s32[]{:S(2)}) async-start(), calls=%async_computation.22 | async-start | bytes 5242880 | tf_op jit(solution)/shard_map/reduce_scatter | solution.py:635
  1454.6 51.7 %collective-permute-start.105 = (bf16[1,128,1408]{2,1,0:T(8,128)(2,1)S(1)}, bf16[1,128,1408]{2,1,0:T(8,128)(2,1)}, u32[]{:S(2)}, u32[]{:S(2)}) collective-permute-start(bf16[1,128,1408]{2,1,0:T(8,128)(2,1)S(1)} %get-tuple-element.426), channel_id=1, source_target_pairs={{0,1},{1,0},{2,3},{3,2},{4,5},{5,4},{6,7},{7,6},{8,9},{9,8},{10,11... | collective-permute-start | bytes 1081352 | tf_op jit(solution)/shard_map/ppermute | solution.py:25
  1455.4 68.6 %collective-permute-start.104 = (bf16[2,128,4096]{2,1,0:T(8,128)(2,1)}, bf16[2,128,4096]{2,1,0:T(8,128)(2,1)}, u32[]{:S(2)}, u32[]{:S(2)}) collective-permute-start(bf16[2,128,4096]{2,1,0:T(8,128)(2,1)} %maximum_bitcast_fusion.8), channel_id=1, source_target_pairs={{0,1},{1,0},{2,3},{3,2},{4,5},{5,4},{6,7},{7,6},{8,9},{9,8},{10,11... | collective-permute-start | bytes 6291464 | tf_op jit(solution)/shard_map/ppermute | solution.py:25
  1456.2 82.0 %collective-permute-start.103 = (bf16[2,128,4096]{2,1,0:T(8,128)(2,1)}, bf16[2,128,4096]{2,1,0:T(8,128)(2,1)}, u32[]{:S(2)}, u32[]{:S(2)}) collective-permute-start(bf16[2,128,4096]{2,1,0:T(8,128)(2,1)} %pad_maximum_fusion.28), channel_id=1, source_target_pairs={{0,2},{1,3},{2,0},{3,1},{4,6},{5,7},{6,4},{7,5},{8,10},{9,11},{10,... | collective-permute-start | bytes 6291464 | tf_op jit(solution)/shard_map/ppermute | solution.py:25
  1462.1 58.6 %all-to-all-start.3 = ((bf16[4,64,2048]{2,1,0:T(8,128)(2,1)}), bf16[4,64,2048]{2,1,0:T(8,128)(2,1)}, u32[]{:S(2)}, u32[]{:S(2)}) async-start(bf16[4,64,2048]{2,1,0:T(8,128)(2,1)} %bitcast.718), calls=%async_computation.7 | async-start | bytes 2097152 | tf_op jit(solution)/shard_map/all_to_all | solution.py:686
  1466.4 370.5 %reduce-scatter.23.cloned.1.call-start = ((), (), s32[]{:S(2)}) async-start(), calls=%async_computation.23 | async-start | bytes 3604480 | tf_op jit(solution)/shard_map/reduce_scatter | solution.py:635
  1530.3 102.2 %collective-permute-start.97 = (bf16[2,4,128,256]{3,2,1,0:T(8,128)(2,1)S(1)}, bf16[2,4,128,256]{3,2,1,0:T(8,128)(2,1)S(1)}, u32[]{:S(2)}, u32[]{:S(2)}) collective-permute-start(bf16[2,4,128,256]{3,2,1,0:T(8,128)(2,1)S(1)} %copy-done.31), channel_id=1, source_target_pairs={{8,0},{12,4},{9,1},{13,5},{10,2},{14,6},{11,3},{15,7},{24,16},{28,... | collective-permute-start | bytes 1572872 | tf_op jit(solution)/shard_map/ppermute | solution.py:705
  1534.5 98.0 %collective-permute-start.98 = (bf16[2,4,128,256]{3,2,1,0:T(8,128)(2,1)S(1)}, bf16[2,4,128,256]{3,2,1,0:T(8,128)(2,1)S(1)}, u32[]{:S(2)}, u32[]{:S(2)}) collective-permute-start(bf16[2,4,128,256]{3,2,1,0:T(8,128)(2,1)S(1)} %copy-done.29), channel_id=1, source_target_pairs={{12,0},{13,1},{14,2},{15,3},{28,16},{29,17},{30,18},{31,19}} | collective-permute-start | bytes 1572872 | tf_op jit(solution)/shard_map/ppermute | solution.py:705
  1536.1 104.4 %collective-permute-start.102 = (bf16[2,128,2048]{2,1,0:T(8,128)(2,1)S(1)}, bf16[2,128,2048]{2,1,0:T(8,128)(2,1)S(1)}, u32[]{:S(2)}, u32[]{:S(2)}) collective-permute-start(bf16[2,128,2048]{2,1,0:T(8,128)(2,1)S(1)} %get-tuple-element.359), channel_id=1, source_target_pairs={{0,1},{1,0},{2,3},{3,2},{4,5},{5,4},{6,7},{7,6},{8,9},{9,8},{10,11... | collective-permute-start | bytes 3145736 | tf_op jit(solution)/shard_map/ppermute | solution.py:25
  1538.2 104.2 %collective-permute-start.100 = (bf16[2,128,2048]{2,1,0:T(8,128)(2,1)S(1)}, bf16[2,128,2048]{2,1,0:T(8,128)(2,1)S(1)}, u32[]{:S(2)}, u32[]{:S(2)}) collective-permute-start(bf16[2,128,2048]{2,1,0:T(8,128)(2,1)S(1)} %pad_maximum_fusion.60), channel_id=1, source_target_pairs={{0,2},{1,3},{2,0},{3,1},{4,6},{5,7},{6,4},{7,5},{8,10},{9,11},{10,... | collective-permute-start | bytes 3145736 | tf_op jit(solution)/shard_map/ppermute | solution.py:25
  (321 other events, 4871.9 us)
Sparse Core Ops, SparseCore 0:
  15.2 58.6 all-gather.4
  76.1 223.8 all-gather.6
  301.7 82.7 all-gather.8
  386.6 223.7 all-gather.10
  788.4 239.0 reduce-scatter.8
  1029.8 96.5 reduce-scatter.10
  1128.7 91.7 reduce-scatter.12
  1307.5 52.8 reduce-scatter.14
  1362.8 76.8 reduce-scatter.16
  1442.4 77.2 reduce-scatter.18
  1522.1 115.7 reduce-scatter.20
  1711.6 60.4 reduce-scatter.22
